TPU v7x, 512 devices: a whole 4x8x8 slice. The times are simulated.
512 devices in a mesh: layer: 8 (over z_hi, core), row: 64 (over x, y, z_lo).
Axes of the slice: x: 4, y: 8, z: 8 (z_hi: 4, z_lo: 2; z = z_hi * 2 + z_lo), core: 2. Of those that a mesh axis runs over, the one named last changes fastest.
Arguments:
- state: float32 [8, 2048, 2048], P('layer', 'row'), may hold values from -6 to 6
- start_state: float32 [8, 2048, 2048], P('layer', 'row'), may hold values from -6 to 6
- to_modes: float32 [8, 8], replicated, may hold values from -2 to 2
- from_modes: float32 [8, 8], replicated, may hold values from -2 to 2
- deform: float32 [8], replicated, may hold values from 4 to 900
Outputs:
- tendency: float32 [8, 2048, 2048], P('layer', 'row')
- new_state: float32 [8, 2048, 2048], P('layer', 'row')
All inputs are finite; a program needn't handle non-finite values.
Results may differ from a plain program's by a relative error of at most 0.0005.
Values sent between devices are 32-bit elements; how exact they have to be, the bound alone decides.
No kernel may reach another device: no remote copies, remote signals or barrier semaphores. Data moves between devices by JAX's collectives and lax.ppermute only.
A program may use at most 64 MiB of HBM per device.

v0:
```python
import math

import jax
import jax.numpy as jnp
from jax import lax
from jax.sharding import PartitionSpec as P

GRID = 2048
FA = 16
FB = 128
KCUT = 672
JSPAN = 84
KEEP = 1344


TRANSFORM_PRECISION = lax.Precision.HIGH
HIGHEST = lax.Precision.HIGHEST
FULL_TURN = 2.0 * math.pi
HYPER_RATE = 0.2
STEP_SIZE = 0.5


def product(pattern, operand, table_part):
    return jnp.einsum(pattern, operand, table_part, precision=TRANSFORM_PRECISION)


def mixing(pattern, operand, table_part):
    return jnp.einsum(pattern, operand, table_part, precision=HIGHEST)


def contract(pattern, real_part, imag_part, table):
    cos_part, sin_part = table
    if imag_part is None:
        return (product(pattern, real_part, cos_part), product(pattern, real_part, sin_part))
    return (
        product(pattern, real_part, cos_part) - product(pattern, imag_part, sin_part),
        product(pattern, real_part, sin_part) + product(pattern, imag_part, cos_part),
    )


def rotate(real_part, imag_part, table):
    cos_part, sin_part = table
    return (
        real_part * cos_part - imag_part * sin_part,
        real_part * sin_part + imag_part * cos_part,
    )


def phase_table(left_index, right_index, modulus, direction, factor):
    residue = left_index[:, None] * right_index[None, :] % modulus
    angles = residue.astype(jnp.float32) * (FULL_TURN / modulus)
    return (factor * jnp.cos(angles), factor * direction * jnp.sin(angles))


def kept_second(values):
    return jnp.where(values < JSPAN // 2, values, values + (FB - JSPAN))


def make_tables(direction, factor, kept_count):
    small_index = jnp.arange(FA, dtype=jnp.int32)
    large_index = jnp.arange(FB, dtype=jnp.int32)
    kept_index = kept_second(jnp.arange(kept_count, dtype=jnp.int32))
    first_table = phase_table(small_index, small_index, FA, direction, factor)
    twiddle = phase_table(small_index, large_index, GRID, direction, 1.0)
    second_table = phase_table(large_index, kept_index, FB, direction, 1.0)
    return (first_table, twiddle, second_table)


def wavenumber(index):
    leading = index // JSPAN
    trailing = kept_second(index % JSPAN)
    combined = leading + FA * trailing
    return jnp.where(combined < GRID // 2, combined, combined - GRID).astype(jnp.float32)


def rows_forward(field, tables):
    layer_count, row_count, width = field.shape
    blocked = field.reshape(layer_count, row_count, FA, FB)
    real_part, imag_part = contract("lrab,ak->lrkb", blocked, None, tables[0])
    real_part, imag_part = rotate(real_part, imag_part, tables[1])
    real_part, imag_part = contract("lrkb,bj->lkjr", real_part, imag_part, tables[2])
    real_part = real_part.reshape(layer_count, -1, row_count)
    imag_part = imag_part.reshape(layer_count, -1, row_count)
    return (real_part, imag_part)


def columns_forward(halves, tables):
    real_part, imag_part = halves
    layer_count, columns, length = real_part.shape
    real_part = real_part.reshape(layer_count, columns, FA, FB)
    imag_part = imag_part.reshape(layer_count, columns, FA, FB)
    real_part, imag_part = contract("lcab,ak->lckb", real_part, imag_part, tables[0])
    real_part, imag_part = rotate(real_part, imag_part, tables[1])
    real_part, imag_part = contract("lckb,bj->lckj", real_part, imag_part, tables[2])
    return (
        real_part.reshape(layer_count, columns, KEEP),
        imag_part.reshape(layer_count, columns, KEEP),
    )


def columns_inverse(halves, tables):
    real_part, imag_part = halves
    layer_count, columns, length = real_part.shape
    real_part = real_part.reshape(layer_count, columns, FA, JSPAN)
    imag_part = imag_part.reshape(layer_count, columns, FA, JSPAN)
    real_part, imag_part = contract("lckj,bj->lckb", real_part, imag_part, tables[2])
    real_part, imag_part = rotate(real_part, imag_part, tables[1])
    real_part, imag_part = contract("lckb,ak->lcab", real_part, imag_part, tables[0])
    return (
        real_part.reshape(layer_count, columns, GRID),
        imag_part.reshape(layer_count, columns, GRID),
    )


def rows_partial(halves, tables):
    real_part, imag_part = halves
    layer_count, length, row_count = real_part.shape
    real_part = real_part.reshape(layer_count, FA, length // FA, row_count)
    imag_part = imag_part.reshape(layer_count, FA, length // FA, row_count)
    real_part, imag_part = contract("lkjr,bj->lrkb", real_part, imag_part, tables[2])
    return rotate(real_part, imag_part, tables[1])


def rows_inverse_real(halves, tables):
    real_part, imag_part = rows_partial(halves, tables)
    cos_part, sin_part = tables[0]
    result = product("lrkb,ak->lrab", real_part, cos_part) - product(
        "lrkb,ak->lrab", imag_part, sin_part
    )
    return result.reshape(result.shape[0], result.shape[1], GRID)


def per_device(state, start_state, to_modes, from_modes, deform):
    layer_count = state.shape[0]
    devices_row = lax.axis_size("row")
    forward_tables = make_tables(-1.0, 1.0, JSPAN)
    inverse_tables = make_tables(1.0, 1.0 / GRID, JSPAN)
    columns = KEEP // devices_row
    column_index = lax.axis_index("row") * columns + jnp.arange(columns, dtype=jnp.int32)
    wave_x = wavenumber(column_index)[None, :, None]
    wave_y = wavenumber(jnp.arange(KEEP, dtype=jnp.int32))[None, None, :]
    retained = ((jnp.abs(wave_x) < KCUT) & (jnp.abs(wave_y) < KCUT)).astype(jnp.float32)
    square = wave_x * wave_x + wave_y * wave_y

    def spectrum(field):
        outgoing = rows_forward(field, forward_tables)
        real_part, imag_part = columns_forward(
            (
                lax.all_to_all(outgoing[0], "row", split_axis=1, concat_axis=2, tiled=True),
                lax.all_to_all(outgoing[1], "row", split_axis=1, concat_axis=2, tiled=True),
            ),
            forward_tables,
        )
        return (real_part * retained, imag_part * retained)

    def physical(real_part, imag_part):
        outgoing = columns_inverse((real_part, imag_part), inverse_tables)
        return rows_inverse_real(
            (
                lax.all_to_all(outgoing[0], "row", split_axis=2, concat_axis=1, tiled=True),
                lax.all_to_all(outgoing[1], "row", split_axis=2, concat_axis=1, tiled=True),
            ),
            inverse_tables,
        )

    vort_real, vort_imag = spectrum(state)
    scaling = -1.0 / (square + deform[:, None, None])
    own_rows = lax.dynamic_slice_in_dim(
        from_modes, lax.axis_index("layer") * layer_count, layer_count, 0
    )
    modal_real = (
        mixing("mn,nck->mck", to_modes, lax.all_gather(vort_real, "layer", axis=0, tiled=True))
        * scaling
    )
    modal_imag = (
        mixing("mn,nck->mck", to_modes, lax.all_gather(vort_imag, "layer", axis=0, tiled=True))
        * scaling
    )
    stream_real = mixing("lm,mck->lck", own_rows, modal_real)
    stream_imag = mixing("lm,mck->lck", own_rows, modal_imag)
    east_real = wave_y * stream_imag
    east_imag = -wave_y * stream_real
    north_real = -wave_x * stream_imag
    north_imag = wave_x * stream_real
    slope_x_real = -wave_x * vort_imag
    slope_x_imag = wave_x * vort_real
    slope_y_real = -wave_y * vort_imag
    slope_y_imag = wave_y * vort_real
    eastward = physical(east_real, east_imag)
    northward = physical(north_real, north_imag)
    slope_x = physical(slope_x_real, slope_x_imag)
    slope_y = physical(slope_y_real, slope_y_imag)
    jacobian = eastward * slope_x + northward * slope_y
    flux_real, flux_imag = spectrum(jacobian)
    ratio = square / (KCUT * KCUT)
    ratio_sq = ratio * ratio
    damping = HYPER_RATE * ratio_sq * ratio_sq
    tendency = physical(-flux_real - damping * vort_real, -flux_imag - damping * vort_imag)
    new_state = 0.75 * start_state + 0.25 * (state + STEP_SIZE * tendency)
    return (tendency, new_state)


def solution(mesh):
    in_specs = (P("layer", "row", None), P("layer", "row", None), P(), P(), P())
    out_specs = (P("layer", "row", None), P("layer", "row", None))
    return jax.shard_map(
        per_device, mesh=mesh, in_specs=in_specs, out_specs=out_specs, check_vma=False
    )
```

profile of v0, /device:TPU:8, one launch (start us, length us, event | category | flops | bytes accessed | tf_op | source)
XLA Modules:
  0.0 500.8 jit_solution(7801726906742165417)
XLA Ops:
  5.3 6.4 %reduce = f32[1344,32]{1,0:T(8,128)S(1)} reduce(f32[1344,1,32]{2,1,0:T(1,128)S(1)} %bitcast.743, f32[]{:T(128)} %broadcast.1692), dimensions={1}, to_apply=%bitcast.637.reduce_sub_computation | reduce | bytes 344068
  12.9 12.4 %all-to-all-start = ((f32[64,1,672]{2,1,0:T(1,128)}), f32[64,1,672]{2,1,0:T(1,128)S(1)}, u32[]{:S(2)}, u32[]{:S(2)}) async-start(f32[64,1,672]{2,1,0:T(1,128)} %reshape.1274), calls=%async_computation | async-start | bytes 393216 | tf_op jit(solution)/shard_map/all_to_all | solution.py:149
  27.9 6.4 %reduce.2 = f32[1344,32]{1,0:T(8,128)S(1)} reduce(f32[1344,1,32]{2,1,0:T(1,128)S(1)} %bitcast.744, f32[]{:T(128)} %broadcast.1692), dimensions={1}, to_apply=%bitcast.639.reduce_sub_computation | reduce | bytes 344068
  36.3 10.5 %all-to-all-start.1 = ((f32[64,1,672]{2,1,0:T(1,128)}), f32[64,1,672]{2,1,0:T(1,128)S(1)}, u32[]{:S(2)}, u32[]{:S(2)}) async-start(f32[64,1,672]{2,1,0:T(1,128)} %reshape.1276), calls=%async_computation.1 | async-start | bytes 393216 | tf_op jit(solution)/shard_map/all_to_all | solution.py:150
  52.4 4.8 all-to-all-done.1
  65.2 23.1 %all_gather.6 = f32[8,21,1344]{2,1,0:T(8,128)S(1)} all-gather(f32[1,21,1344]{2,1,0:T(8,128)S(1)} %get-tuple-element.27), channel_id=1, replica_groups=mesh['layer'=8,'row'=64] {'layer'}, dimensions={0}, use_global_device_ids=true | all-gather | bytes 1016064 | tf_op jit(solution)/shard_map/all_gather | solution.py:176
  92.1 17.5 %all_gather.7 = f32[8,21,1344]{2,1,0:T(8,128)S(1)} all-gather(f32[1,21,1344]{2,1,0:T(8,128)S(1)} %get-tuple-element.26), channel_id=1, replica_groups=mesh['layer'=8,'row'=64] {'layer'}, dimensions={0}, use_global_device_ids=true | all-gather | bytes 1016064 | tf_op jit(solution)/shard_map/all_gather | solution.py:172
  125.3 9.4 %reduce.18 = f32[2048,21]{1,0:T(8,128)S(1)} reduce(f32[2048,1,21]{2,1,0:T(1,128)S(1)} %bitcast.719, f32[]{:T(128)} %broadcast.1692), dimensions={1}, to_apply=%bitcast.651.reduce_sub_computation | reduce | bytes 344068
  136.5 6.5 %all-to-all-start.7 = ((f32[64,1,672]{2,1,0:T(1,128)}), f32[64,1,672]{2,1,0:T(1,128)S(1)}, u32[]{:S(2)}, u32[]{:S(2)}) async-start(f32[64,1,672]{2,1,0:T(1,128)} %reshape.1288), calls=%async_computation.7 | async-start | bytes 393216 | tf_op jit(solution)/shard_map/all_to_all | solution.py:161
  148.2 9.4 %reduce.16 = f32[2048,21]{1,0:T(8,128)S(1)} reduce(f32[2048,1,21]{2,1,0:T(1,128)S(1)} %bitcast.720, f32[]{:T(128)} %broadcast.1692), dimensions={1}, to_apply=%bitcast.649.reduce_sub_computation | reduce | bytes 344068
  161.4 9.8 %reduce.14 = f32[2048,21]{1,0:T(8,128)S(1)} reduce(f32[2048,1,21]{2,1,0:T(1,128)S(1)} %bitcast.721, f32[]{:T(128)} %broadcast.1692), dimensions={1}, to_apply=%bitcast.647.reduce_sub_computation | reduce | bytes 344068
  173.6 9.4 %reduce.12 = f32[2048,21]{1,0:T(8,128)S(1)} reduce(f32[2048,1,21]{2,1,0:T(1,128)S(1)} %bitcast.722, f32[]{:T(128)} %broadcast.1692), dimensions={1}, to_apply=%bitcast.645.reduce_sub_computation | reduce | bytes 344068
  185.4 9.4 %reduce.10 = f32[2048,21]{1,0:T(8,128)S(1)} reduce(f32[2048,1,21]{2,1,0:T(1,128)S(1)} %bitcast.723, f32[]{:T(128)} %broadcast.1692), dimensions={1}, to_apply=%bitcast.643.reduce_sub_computation | reduce | bytes 344068
  197.1 9.5 %reduce.8 = f32[2048,21]{1,0:T(8,128)S(1)} reduce(f32[2048,1,21]{2,1,0:T(1,128)S(1)} %bitcast.724, f32[]{:T(128)} %broadcast.1692), dimensions={1}, to_apply=%bitcast.641.reduce_sub_computation | reduce | bytes 344068
  209.1 9.4 %reduce.6 = f32[2048,21]{1,0:T(8,128)S(1)} reduce(f32[2048,1,21]{2,1,0:T(1,128)S(1)} %bitcast.725, f32[]{:T(128)} %broadcast.1692), dimensions={1}, to_apply=%bitcast.655.reduce_sub_computation | reduce | bytes 344068
  221.2 9.6 %reduce.4 = f32[2048,21]{1,0:T(8,128)S(1)} reduce(f32[2048,1,21]{2,1,0:T(1,128)S(1)} %bitcast.726, f32[]{:T(128)} %broadcast.1692), dimensions={1}, to_apply=%bitcast.653.reduce_sub_computation | reduce | bytes 344068
  232.5 11.2 %all-to-all-start.6 = ((f32[64,1,672]{2,1,0:T(1,128)}), f32[64,1,672]{2,1,0:T(1,128)S(1)}, u32[]{:S(2)}, u32[]{:S(2)}) async-start(f32[64,1,672]{2,1,0:T(1,128)} %reshape.1286), calls=%async_computation.6 | async-start | bytes 393216 | tf_op jit(solution)/shard_map/all_to_all | solution.py:160
  249.9 4.9 all-to-all-done.6
  254.8 6.9 %all-to-all-start.5 = ((f32[64,1,672]{2,1,0:T(1,128)}), f32[64,1,672]{2,1,0:T(1,128)S(1)}, u32[]{:S(2)}, u32[]{:S(2)}) async-start(f32[64,1,672]{2,1,0:T(1,128)} %reshape.1284), calls=%async_computation.5 | async-start | bytes 393216 | tf_op jit(solution)/shard_map/all_to_all | solution.py:161
  272.1 7.0 %all-to-all-start.4 = ((f32[64,1,672]{2,1,0:T(1,128)}), f32[64,1,672]{2,1,0:T(1,128)S(1)}, u32[]{:S(2)}, u32[]{:S(2)}) async-start(f32[64,1,672]{2,1,0:T(1,128)} %reshape.1282), calls=%async_computation.4 | async-start | bytes 393216 | tf_op jit(solution)/shard_map/all_to_all | solution.py:160
  289.5 8.0 %all-to-all-start.3 = ((f32[64,1,672]{2,1,0:T(1,128)}), f32[64,1,672]{2,1,0:T(1,128)S(1)}, u32[]{:S(2)}, u32[]{:S(2)}) async-start(f32[64,1,672]{2,1,0:T(1,128)} %reshape.1280), calls=%async_computation.3 | async-start | bytes 393216 | tf_op jit(solution)/shard_map/all_to_all | solution.py:161
  307.7 8.7 %all-to-all-start.2 = ((f32[64,1,672]{2,1,0:T(1,128)}), f32[64,1,672]{2,1,0:T(1,128)}, u32[]{:S(2)}, u32[]{:S(2)}) async-start(f32[64,1,672]{2,1,0:T(1,128)} %reshape.1278), calls=%async_computation.2 | async-start | bytes 393216 | tf_op jit(solution)/shard_map/all_to_all | solution.py:160
  326.6 8.7 %all-to-all-start.9 = ((f32[64,1,672]{2,1,0:T(1,128)}), f32[64,1,672]{2,1,0:T(1,128)}, u32[]{:S(2)}, u32[]{:S(2)}) async-start(f32[64,1,672]{2,1,0:T(1,128)} %reshape.1292), calls=%async_computation.9 | async-start | bytes 393216 | tf_op jit(solution)/shard_map/all_to_all | solution.py:161
  345.6 9.3 %all-to-all-start.8 = ((f32[64,1,672]{2,1,0:T(1,128)}), f32[64,1,672]{2,1,0:T(1,128)}, u32[]{:S(2)}, u32[]{:S(2)}) async-start(f32[64,1,672]{2,1,0:T(1,128)} %reshape.1290), calls=%async_computation.8 | async-start | bytes 393216 | tf_op jit(solution)/shard_map/all_to_all | solution.py:160
  380.6 6.4 %reduce.20 = f32[1344,32]{1,0:T(8,128)S(1)} reduce(f32[1344,1,32]{2,1,0:T(1,128)S(1)} %bitcast.755, f32[]{:T(128)} %broadcast.1692), dimensions={1}, to_apply=%bitcast.657.reduce_sub_computation | reduce | bytes 344068
  388.2 9.8 %all-to-all-start.10 = ((f32[64,1,672]{2,1,0:T(1,128)}), f32[64,1,672]{2,1,0:T(1,128)S(1)}, u32[]{:S(2)}, u32[]{:S(2)}) async-start(f32[64,1,672]{2,1,0:T(1,128)} %reshape.1294), calls=%async_computation.10 | async-start | bytes 393216 | tf_op jit(solution)/shard_map/all_to_all | solution.py:149
  400.2 6.4 %reduce.22 = f32[1344,32]{1,0:T(8,128)S(1)} reduce(f32[1344,1,32]{2,1,0:T(1,128)S(1)} %bitcast.756, f32[]{:T(128)} %broadcast.1692), dimensions={1}, to_apply=%bitcast.659.reduce_sub_computation | reduce | bytes 344068
  408.3 11.0 %all-to-all-start.11 = ((f32[64,1,672]{2,1,0:T(1,128)}), f32[64,1,672]{2,1,0:T(1,128)S(1)}, u32[]{:S(2)}, u32[]{:S(2)}) async-start(f32[64,1,672]{2,1,0:T(1,128)} %reshape.1296), calls=%async_computation.11 | async-start | bytes 393216 | tf_op jit(solution)/shard_map/all_to_all | solution.py:150
  440.1 9.8 %reduce.26 = f32[2048,21]{1,0:T(8,128)S(1)} reduce(f32[2048,1,21]{2,1,0:T(1,128)S(1)} %bitcast.727, f32[]{:T(128)} %broadcast.1692), dimensions={1}, to_apply=%bitcast.663.reduce_sub_computation | reduce | bytes 344068
  451.7 6.7 %all-to-all-start.13 = ((f32[64,1,672]{2,1,0:T(1,128)}), f32[64,1,672]{2,1,0:T(1,128)S(1)}, u32[]{:S(2)}, u32[]{:S(2)}) async-start(f32[64,1,672]{2,1,0:T(1,128)} %reshape.1300), calls=%async_computation.13 | async-start | bytes 393216 | tf_op jit(solution)/shard_map/all_to_all | solution.py:161
  459.6 9.4 %reduce.24 = f32[2048,21]{1,0:T(8,128)S(1)} reduce(f32[2048,1,21]{2,1,0:T(1,128)S(1)} %bitcast.728, f32[]{:T(128)} %broadcast.1692), dimensions={1}, to_apply=%bitcast.661.reduce_sub_computation | reduce | bytes 344068
  470.8 11.4 %all-to-all-start.12 = ((f32[64,1,672]{2,1,0:T(1,128)}), f32[64,1,672]{2,1,0:T(1,128)S(1)}, u32[]{:S(2)}, u32[]{:S(2)}) async-start(f32[64,1,672]{2,1,0:T(1,128)} %reshape.1298), calls=%async_computation.12 | async-start | bytes 393216 | tf_op jit(solution)/shard_map/all_to_all | solution.py:160
  (315 shorter events, 199.3 us)
Async XLA Ops:
  0.6 87.7 %copy-start = (f32[8,8]{1,0:T(8,128)S(1)}, f32[8,8]{1,0:T(8,128)}, u32[]{:S(2)}) copy-start(f32[8,8]{1,0:T(8,128)} %param.7) | copy-start | bytes 772
  12.9 23.4 %all-to-all-start = ((f32[64,1,672]{2,1,0:T(1,128)}), f32[64,1,672]{2,1,0:T(1,128)S(1)}, u32[]{:S(2)}, u32[]{:S(2)}) async-start(f32[64,1,672]{2,1,0:T(1,128)} %reshape.1274), calls=%async_computation | async-start | bytes 393216 | tf_op jit(solution)/shard_map/all_to_all | solution.py:149
  25.9 9.6 %copy-start.22 = (f32[21]{0:T(128)}, f32[21]{0:T(128)S(1)}, u32[]{:S(2)}) copy-start(f32[21]{0:T(128)S(1)} %fusion.840) | copy-start | bytes 256
  36.3 21.0 %all-to-all-start.1 = ((f32[64,1,672]{2,1,0:T(1,128)}), f32[64,1,672]{2,1,0:T(1,128)S(1)}, u32[]{:S(2)}, u32[]{:S(2)}) async-start(f32[64,1,672]{2,1,0:T(1,128)} %reshape.1276), calls=%async_computation.1 | async-start | bytes 393216 | tf_op jit(solution)/shard_map/all_to_all | solution.py:150
  64.9 58.1 %copy-start.12 = (f32[21,16,84]{2,1,0:T(8,128)}, f32[21,16,84]{2,1,0:T(8,128)S(1)}, u32[]{:S(2)}) copy-start(f32[21,16,84]{2,1,0:T(8,128)S(1)} %convolution_add_fusion.15) | copy-start | bytes 338692
  65.0 23.3 %copy-start.24 = (f32[8]{0:T(128)S(1)}, f32[8]{0:T(128)}, u32[]{:S(2)}) copy-start(f32[8]{0:T(128)} %param.9) | copy-start | bytes 100
  134.7 8.6 %copy-start.16 = (f32[16,21,128]{2,0,1:T(8,128)S(1)}, f32[16,21,128]{2,0,1:T(8,128)}, u32[]{:S(2)}) copy-start(f32[16,21,128]{2,0,1:T(8,128)} %fusion.128) | copy-start | bytes 516100
  136.5 7.8 %copy-start.14 = (f32[16,21,128]{2,0,1:T(8,128)S(1)}, f32[16,21,128]{2,0,1:T(8,128)}, u32[]{:S(2)}) copy-start(f32[16,21,128]{2,0,1:T(8,128)} %fusion.129) | copy-start | bytes 516100
  136.5 96.1 %all-to-all-start.7 = ((f32[64,1,672]{2,1,0:T(1,128)}), f32[64,1,672]{2,1,0:T(1,128)S(1)}, u32[]{:S(2)}, u32[]{:S(2)}) async-start(f32[64,1,672]{2,1,0:T(1,128)} %reshape.1288), calls=%async_computation.7 | async-start | bytes 393216 | tf_op jit(solution)/shard_map/all_to_all | solution.py:161
  143.0 1.6 copy-start.18
  218.5 1.8 copy-start.15
  232.5 22.2 %all-to-all-start.6 = ((f32[64,1,672]{2,1,0:T(1,128)}), f32[64,1,672]{2,1,0:T(1,128)S(1)}, u32[]{:S(2)}, u32[]{:S(2)}) async-start(f32[64,1,672]{2,1,0:T(1,128)} %reshape.1286), calls=%async_computation.6 | async-start | bytes 393216 | tf_op jit(solution)/shard_map/all_to_all | solution.py:160
  254.8 17.3 %all-to-all-start.5 = ((f32[64,1,672]{2,1,0:T(1,128)}), f32[64,1,672]{2,1,0:T(1,128)S(1)}, u32[]{:S(2)}, u32[]{:S(2)}) async-start(f32[64,1,672]{2,1,0:T(1,128)} %reshape.1284), calls=%async_computation.5 | async-start | bytes 393216 | tf_op jit(solution)/shard_map/all_to_all | solution.py:161
  272.1 17.4 %all-to-all-start.4 = ((f32[64,1,672]{2,1,0:T(1,128)}), f32[64,1,672]{2,1,0:T(1,128)S(1)}, u32[]{:S(2)}, u32[]{:S(2)}) async-start(f32[64,1,672]{2,1,0:T(1,128)} %reshape.1282), calls=%async_computation.4 | async-start | bytes 393216 | tf_op jit(solution)/shard_map/all_to_all | solution.py:160
  289.5 18.2 %all-to-all-start.3 = ((f32[64,1,672]{2,1,0:T(1,128)}), f32[64,1,672]{2,1,0:T(1,128)S(1)}, u32[]{:S(2)}, u32[]{:S(2)}) async-start(f32[64,1,672]{2,1,0:T(1,128)} %reshape.1280), calls=%async_computation.3 | async-start | bytes 393216 | tf_op jit(solution)/shard_map/all_to_all | solution.py:161
  307.7 19.0 %all-to-all-start.2 = ((f32[64,1,672]{2,1,0:T(1,128)}), f32[64,1,672]{2,1,0:T(1,128)}, u32[]{:S(2)}, u32[]{:S(2)}) async-start(f32[64,1,672]{2,1,0:T(1,128)} %reshape.1278), calls=%async_computation.2 | async-start | bytes 393216 | tf_op jit(solution)/shard_map/all_to_all | solution.py:160
  326.6 18.9 %all-to-all-start.9 = ((f32[64,1,672]{2,1,0:T(1,128)}), f32[64,1,672]{2,1,0:T(1,128)}, u32[]{:S(2)}, u32[]{:S(2)}) async-start(f32[64,1,672]{2,1,0:T(1,128)} %reshape.1292), calls=%async_computation.9 | async-start | bytes 393216 | tf_op jit(solution)/shard_map/all_to_all | solution.py:161
  345.6 19.2 %all-to-all-start.8 = ((f32[64,1,672]{2,1,0:T(1,128)}), f32[64,1,672]{2,1,0:T(1,128)}, u32[]{:S(2)}, u32[]{:S(2)}) async-start(f32[64,1,672]{2,1,0:T(1,128)} %reshape.1290), calls=%async_computation.8 | async-start | bytes 393216 | tf_op jit(solution)/shard_map/all_to_all | solution.py:160
  370.4 3.2 copy-start.8
  370.4 3.2 copy-start.9
  371.4 2.2 copy-start.2
  371.4 2.2 copy-start.3
  371.4 2.2 copy-start.4
  371.4 2.3 copy-start.5
  371.4 2.3 copy-start.6
  371.4 2.3 copy-start.7
  388.2 20.1 %all-to-all-start.10 = ((f32[64,1,672]{2,1,0:T(1,128)}), f32[64,1,672]{2,1,0:T(1,128)S(1)}, u32[]{:S(2)}, u32[]{:S(2)}) async-start(f32[64,1,672]{2,1,0:T(1,128)} %reshape.1294), calls=%async_computation.10 | async-start | bytes 393216 | tf_op jit(solution)/shard_map/all_to_all | solution.py:149
  408.3 21.2 %all-to-all-start.11 = ((f32[64,1,672]{2,1,0:T(1,128)}), f32[64,1,672]{2,1,0:T(1,128)S(1)}, u32[]{:S(2)}, u32[]{:S(2)}) async-start(f32[64,1,672]{2,1,0:T(1,128)} %reshape.1296), calls=%async_computation.11 | async-start | bytes 393216 | tf_op jit(solution)/shard_map/all_to_all | solution.py:150
  434.5 1.6 copy-start.23
  435.7 1.9 copy-start.13
  451.7 19.1 %all-to-all-start.13 = ((f32[64,1,672]{2,1,0:T(1,128)}), f32[64,1,672]{2,1,0:T(1,128)S(1)}, u32[]{:S(2)}, u32[]{:S(2)}) async-start(f32[64,1,672]{2,1,0:T(1,128)} %reshape.1300), calls=%async_computation.13 | async-start | bytes 393216 | tf_op jit(solution)/shard_map/all_to_all | solution.py:161
  470.8 21.7 %all-to-all-start.12 = ((f32[64,1,672]{2,1,0:T(1,128)}), f32[64,1,672]{2,1,0:T(1,128)S(1)}, u32[]{:S(2)}, u32[]{:S(2)}) async-start(f32[64,1,672]{2,1,0:T(1,128)} %reshape.1298), calls=%async_computation.12 | async-start | bytes 393216 | tf_op jit(solution)/shard_map/all_to_all | solution.py:160
  (7 other events, 7.7 us)
where the time goes:
time: 510 us; the launch traced here: 501 us
  other arithmetic  141 us (28%)
  starting transfers between devices  128 us (25%)
  local copies, waits for them, and re-layouts  94.1 us (18%)
  matrix products  57.1 us (11%)
  blocking collectives  40.6 us (8%)
  waiting for transfers between devices  36.9 us (7%)
    unnamed x14, other arithmetic  120 us
    all_to_all x5, starting transfers between devices, physical(): lax.all_to_all(outgoing[0], 'row', split_axis=2, concat_axis=1, tiled=True)  47.7 us
    unnamed x80, local copies, waits for them, and re-layouts  46 us
    all_to_all x5, starting transfers between devices, physical(): lax.all_to_all(outgoing[1], 'row', split_axis=2, concat_axis=1, tiled=True)  36.8 us
    dot_general x78, matrix products, product(): jnp.einsum(pattern, operand, table_part, precision=TRANSFORM_PRECISION)  36.1 us
    all_gather x1, blocking collectives, per_device(): lax.all_gather(vort_imag, 'layer', axis=0, tiled=True)  23.1 us
    all_to_all x2, starting transfers between devices, spectrum(): lax.all_to_all(outgoing[0], 'row', split_axis=1, concat_axis=2, tiled=True)  22.2 us
    all_to_all x2, starting transfers between devices, spectrum(): lax.all_to_all(outgoing[1], 'row', split_axis=1, concat_axis=2, tiled=True)  21.5 us
  transfers between devices with their start and end apart: 14, of which 12 were waited for; matrix products, arithmetic and copies ran while one was open for 37% of the time, Pallas kernels for 0%

commit v1 on v0

v1 whole, which is shorter than its diff:
```python
import functools
import math

import jax
import jax.numpy as jnp
import ml_dtypes
import numpy as np
from jax import lax
from jax.experimental import pallas as pl
from jax.experimental.pallas import tpu as pltpu
from jax.sharding import PartitionSpec as P

GRID = 2048
KCUT = 672
ROWS = 32
HALF = 14
CHUNK = 6
KAP = 64
JP = 21
PIECE = 8 * JP
SPAN = 512
HYPER_RATE = 0.2
STEP_SIZE = 0.5
BF16 = jnp.bfloat16
F32 = jnp.float32


def halves(table):
    high = table.astype(ml_dtypes.bfloat16)
    low = (table - high.astype(np.float64)).astype(ml_dtypes.bfloat16)
    return np.stack([high, low])


def turn(numerator, denominator):
    angle = 2.0 * math.pi * (np.mod(numerator, denominator) / denominator)
    return np.cos(angle), np.sin(angle)


def x_forward_table():
    b = np.arange(128)
    table = np.zeros((2, 16, 8, 2, 128))
    for half in range(2):
        for tau in range(HALF):
            for j3 in range(3):
                c, s = turn((3 * tau + j3 - 42 * half) * b, 128)
                table[half, tau, j3, 0] = c
                table[half, tau, j3, 1] = s
                table[half, tau, 3 + j3, 0] = -s
                table[half, tau, 3 + j3, 1] = c
    return halves(table.reshape(2, 128, 256))


def x_inverse_table(times_i):
    b = np.arange(128)
    table = np.zeros((2, 2, 3, 16, 2, 128))
    for half in range(2):
        for tau in range(HALF):
            for j3 in range(3):
                c, s = turn((3 * tau + j3 - 42 * half) * b, 128)
                if times_i:
                    c, s = -s, c
                table[half, 0, j3, tau, 0] = c
                table[half, 0, j3, tau, 1] = s
                table[half, 1, j3, tau, 0] = -s
                table[half, 1, j3, tau, 1] = c
    return halves(table.reshape(192, 256) * (2.0 / (GRID * GRID)))


def x_twiddle():
    table = np.zeros((32, 128))
    c, s = turn(np.arange(9)[:, None] * np.arange(128)[None, :], GRID)
    table[0:9] = c
    table[16:25] = s
    return table.astype(np.float32)


def y_radix_table():
    c, s = turn(np.arange(KAP)[:, None] * np.arange(64)[None, :] + 32 * np.arange(64)[None, :], 64)
    return halves(np.block([[c, s], [-s, c]]))


def y_radix_inverse_table():
    c, s = turn(np.arange(64)[:, None] * np.arange(KAP)[None, :] + 32 * np.arange(64)[:, None], 64)
    return halves(np.block([[c, -s], [s, c]]))


def y_twiddle():
    c, s = turn((np.arange(KAP)[:, None] - KCUT) * np.arange(ROWS)[None, :], GRID)
    return np.stack([np.tile(c, (1, 4)), np.tile(s, (1, 4))]).astype(np.float32)


def y_lane_table():
    c, s = turn(np.arange(ROWS)[:, None] * np.arange(JP)[None, :], ROWS)
    table = np.zeros((3, 2, 4, ROWS, 256))
    for j3 in range(3):
        for slot in range(4):
            re = 40 * j3 + slot * JP
            im = re + 4 * JP
            table[j3, 0, slot, :, re : re + JP] = c
            table[j3, 1, slot, :, re : re + JP] = s
            table[j3, 0, slot, :, im : im + JP] = -s
            table[j3, 1, slot, :, im : im + JP] = c
    return halves(table.reshape(3, 256, 256))


def y_lane_inverse_table():
    high, low = y_lane_table()
    return np.stack([np.swapaxes(high, 1, 2), np.swapaxes(low, 1, 2)])


def lane_facts():
    lane = np.arange(SPAN)
    j3 = lane // PIECE
    slot = (lane % (4 * JP)) // JP
    facts = np.zeros((8, SPAN))
    facts[0] = 16 * j3
    facts[1] = slot
    facts[2] = 64 * (lane % JP) - KCUT
    facts[3] = slot == 0
    return facts.astype(np.float32)


def split(value):
    high = value.astype(BF16)
    low = (value - high.astype(F32)).astype(BF16)
    return high, low


def matmul(left, right, dims):
    def one(a, b):
        return lax.dot_general(a, b, (dims, ((), ())), preferred_element_type=F32)

    return one(left[0], right[0]) + (one(left[0], right[1]) + one(left[1], right[0]))


NN = ((1,), (0,))
NT = ((1,), (1,))
TN = ((0,), (0,))

C1 = math.cos(math.pi / 8)
C2 = math.cos(math.pi / 4)
C3 = math.cos(3 * math.pi / 8)


def real_analysis(x):
    s = [x[a] + x[a + 8] for a in range(8)]
    d = [x[a] - x[a + 8] for a in range(8)]
    e = [None] + [d[a] - d[8 - a] for a in range(1, 4)]
    f = [None] + [d[a] + d[8 - a] for a in range(1, 4)]
    e2, f2 = e[2] * C2, f[2] * C2
    plus, minus = d[0] + e2, d[0] - e2
    first, second = e[1] * C1 + e[3] * C3, e[1] * C3 - e[3] * C1
    third, fourth = f[1] * C3 + f[3] * C1, f[1] * C1 - f[3] * C3
    u, v = d[4] + f2, f2 - d[4]
    p = [s[a] + s[a + 4] for a in range(4)]
    q = [s[a] - s[a + 4] for a in range(4)]
    even, odd = p[0] + p[2], p[1] + p[3]
    hd, hs = (q[1] - q[3]) * C2, (q[1] + q[3]) * C2
    real = [
        even + odd,
        plus + first,
        q[0] + hd,
        minus + second,
        p[0] - p[2],
        minus - second,
        q[0] - hd,
        plus - first,
        even - odd,
    ]
    imag = [
        None,
        -(third + u),
        -(q[2] + hs),
        -(fourth + v),
        p[3] - p[1],
        v - fourth,
        q[2] - hs,
        u - third,
        None,
    ]
    return real, imag


def real_synthesis(real, imag):
    plus, first = real[1] + real[7], real[1] - real[7]
    minus, second = real[3] + real[5], real[3] - real[5]
    third, u = -(imag[1] + imag[7]), imag[7] - imag[1]
    fourth, v = -(imag[3] + imag[5]), imag[5] - imag[3]
    d = [None] * 8
    d[0], d[4] = plus + minus, u - v
    e = [None, first * C1 + second * C3, (plus - minus) * C2, first * C3 - second * C1]
    f = [None, third * C3 + fourth * C1, (u + v) * C2, third * C1 - fourth * C3]
    for a in range(1, 4):
        d[a], d[8 - a] = f[a] + e[a], f[a] - e[a]
    even, odd = real[0] + real[8], real[0] - real[8]
    p = [even + real[4], odd - imag[4], even - real[4], odd + imag[4]]
    hr, hi = (real[2] - real[6]) * C2, (imag[2] + imag[6]) * C2
    q = [real[2] + real[6], hr - hi, imag[6] - imag[2], -(hr + hi)]
    s = [p[a] + q[a] for a in range(4)] + [p[a] - q[a] for a in range(4)]
    return [s[a] + d[a] for a in range(8)] + [s[a] - d[a] for a in range(8)]


def x_forward(real, imag, twiddle, table):
    pieces = []
    for k in range(9):
        if k == 0:
            pieces.append(jnp.concatenate([real[0], jnp.zeros_like(real[0])], axis=1))
            continue
        c, s = twiddle[k : k + 1], twiddle[16 + k : 17 + k]
        if k == 8:
            re, im = real[8] * c, -(real[8] * s)
        else:
            re, im = real[k] * c + imag[k] * s, imag[k] * c - real[k] * s
        pieces.append(jnp.concatenate([re, im], axis=1))
    shared = split(jnp.concatenate(pieces[1:8], axis=0))
    results = []
    for half, own in enumerate((pieces[0], pieces[8])):
        own = split(own)
        right = [jnp.concatenate([own[i], shared[i]], axis=0) for i in range(2)]
        results.append(matmul([table[0, half], table[1, half]], right, NT))
    return results


def x_inverse(left, right, fields, table):
    left = split(left)
    right = split(right)
    upper = [table[i][:96] for i in range(2)]
    lower = [table[i][96:] for i in range(2)]
    first = matmul([part[:96] for part in left], upper, TN)
    second = matmul([part[96:] for part in left], lower, TN)
    rest = matmul(right, [table[i] for i in range(2)], TN)
    return first, second, rest


def modes_of(first, second, rest, field, rows, twiddle):
    real, imag = [], []
    for k in range(9):
        c, s = twiddle[k : k + 1], twiddle[16 + k : 17 + k]
        base = field * 128 + rows.start
        size = rows.stop - rows.start
        if k in (0, 8):
            source = first if k == 0 else second
            z = source[base : base + size]
        elif k < 4:
            start = base + 32 * k
            z = first[start : start + size] + second[start : start + size]
        else:
            start = base + 32 * (k - 4)
            z = rest[start : start + size]
        re, im = z[:, :128], z[:, 128:]
        if k == 0:
            real.append(re)
            imag.append(None)
        else:
            real.append(re * c - im * s)
            imag.append(None if k == 8 else re * s + im * c)
    return real, imag


def y_forward(pieces, radix, twiddle, lanes, facts):
    stacked = jnp.concatenate(
        [jnp.concatenate(pieces[0], axis=1), jnp.concatenate(pieces[1], axis=1)], axis=0
    )
    mixed = matmul([radix[0], radix[1]], split(stacked), NN)
    c, s = twiddle[0], twiddle[1]
    windows = []
    for j3 in range(3):
        re, im = mixed[:KAP, 128 * j3 : 128 * j3 + 128], mixed[KAP:, 128 * j3 : 128 * j3 + 128]
        turned = jnp.concatenate([re * c + im * s, im * c - re * s], axis=1)
        windows.append(matmul(split(turned), [lanes[0, j3], lanes[1, j3]], NN))
    first, second, third = windows
    spectrum = jnp.concatenate(
        [
            first[:, :128],
            first[:, 128:] + second[:, :128],
            second[:, 128:] + third[:, :128],
            third[:, 128:],
        ],
        axis=1,
    )
    wave_y = y_waves(facts)
    return jnp.where(wave_y > -KCUT, spectrum, 0.0)


def y_waves(facts):
    kap = lax.broadcasted_iota(jnp.int32, (KAP, 1), 0).astype(F32)
    return kap + facts[2:3]


def x_waves(facts, owner):
    group = owner // 32
    half = (owner % 32) // 16
    tau = owner % 16
    base = (4 * group + 16 * (3 * tau - 42 * half)).astype(F32)
    shift = (8 * half * (1 - group)).astype(F32)
    return facts[0:1] + facts[1:2] + base + shift * facts[3:4]


def y_inverse(spectra, radix, twiddle, lanes):
    count = len(spectra)
    stacked = split(jnp.concatenate(spectra, axis=0) if count > 1 else spectra[0])
    c, s = twiddle[0], twiddle[1]
    real, imag = [], []
    for j3 in range(3):
        window = [part[:, 128 * j3 : 128 * j3 + 256] for part in stacked]
        out = matmul(window, [lanes[0, j3], lanes[1, j3]], NN)
        for field in range(count):
            own = out[KAP * field : KAP * field + KAP]
            re, im = own[:, :128], own[:, 128:]
            real.append(re * c - im * s)
            imag.append(re * s + im * c)
    right = split(
        jnp.concatenate([jnp.concatenate(real, axis=1), jnp.concatenate(imag, axis=1)], axis=0)
    )
    out = matmul([radix[0], radix[1]], right, NN)
    fields = []
    for field in range(count):
        columns = [slice(128 * (count * j3 + field), 128 * (count * j3 + field) + 128) for j3 in range(3)]
        fields.append([[out[:64, own] for own in columns], [out[64:, own] for own in columns]])
    return fields


def stream_function(gathered, to_modes, from_modes, deform, layer, square):
    weights = [from_modes(layer, m) * (-1.0 / (square + deform(m))) for m in range(8)]
    total = None
    for n in range(8):
        factor = None
        for m in range(8):
            term = weights[m] * to_modes(m, n)
            factor = term if factor is None else factor + term
        term = factor * gathered(n)
        total = term if total is None else total + term
    return total


def store_x(out_ref, results):
    for half in range(2):
        for group in range(2):
            block = results[half][:, 128 * group : 128 * group + 128]
            for tau in range(16):
                start = (32 * group + 16 * half + tau) * CHUNK
                out_ref[start : start + CHUNK, :] = block[8 * tau : 8 * tau + CHUNK]


def load_pieces(ref):
    return [
        [ref[pl.ds(3 * part + j3, 64, stride=CHUNK), :] for j3 in range(3)] for part in range(2)
    ]


def store_pieces(ref, fields):
    stride = CHUNK * len(fields)
    for field, pieces in enumerate(fields):
        for part in range(2):
            for j3 in range(3):
                ref[pl.ds(CHUNK * field + 3 * part + j3, 64, stride=stride), :] = pieces[part][j3]


def load_x(ref, fields):
    stride = CHUNK * fields
    groups = []
    for group in range(2):
        columns = []
        for field in range(fields):
            rows = []
            for half in range(2):
                for part in range(CHUNK):
                    start = (32 * group + 16 * half) * stride + CHUNK * field + part
                    rows.append(ref[pl.ds(start, 16, stride=stride), :])
            columns.append(jnp.concatenate(rows, axis=0))
        groups.append(columns)
    return groups


def state_kernel(state_ref, twiddle_ref, table_ref, out_ref):
    x = [state_ref[0, :, 128 * a : 128 * a + 128] for a in range(16)]
    real, imag = real_analysis(x)
    store_x(out_ref, x_forward(real, imag, twiddle_ref[...], table_ref))


def spectrum_kernel(in_ref, radix_ref, unradix_ref, turn_ref, lanes_ref, unlanes_ref, facts_ref, spec_ref, out_ref):
    facts = facts_ref[...]
    spectrum = y_forward(load_pieces(in_ref), radix_ref, turn_ref, lanes_ref, facts)
    spec_ref[...] = spectrum
    wave_x = x_waves(facts, lax.axis_index("row"))
    wave_y = y_waves(facts)
    weight = jnp.where(wave_x == 0.0, 0.5, 1.0)
    fields = [wave_x * spectrum, (wave_y * weight) * spectrum]
    store_pieces(out_ref, y_inverse(fields, unradix_ref, turn_ref, unlanes_ref))


def stream_kernel(
    to_ref, from_ref, deform_ref, all_ref, unradix_ref, turn_ref, unlanes_ref, facts_ref, out_ref
):
    facts = facts_ref[...]
    wave_x = x_waves(facts, lax.axis_index("row"))
    wave_y = y_waves(facts)
    square = wave_x * wave_x + wave_y * wave_y
    stream = stream_function(
        lambda n: all_ref[n],
        lambda m, n: to_ref[m, n],
        lambda l, m: from_ref[l, m],
        lambda m: deform_ref[m],
        lax.axis_index("layer"),
        square,
    )
    weight = jnp.where(wave_x == 0.0, 0.5, 1.0)
    fields = [-(wave_y * weight) * stream, wave_x * stream]
    store_pieces(out_ref, y_inverse(fields, unradix_ref, turn_ref, unlanes_ref))


def jacobian_kernel(flow_ref, slope_ref, twiddle_ref, untable_ref, table_ref, out_ref, z0, z1, z2, jac):
    flow = load_x(flow_ref, 2)
    slope = load_x(slope_ref, 2)
    left = jnp.concatenate(flow[0] + slope[0], axis=1)
    right = jnp.concatenate(flow[1] + slope[1], axis=1)
    z0[...], z1[...], z2[...] = x_inverse(left, right, 4, untable_ref)
    twiddle = twiddle_ref[...]
    for block in range(4):
        rows = slice(8 * block, 8 * block + 8)

        def physical(field):
            return real_synthesis(*modes_of(z0, z1, z2, field, rows, twiddle))

        east, slope_x = physical(0), physical(2)
        product = [a * b for a, b in zip(east, slope_x)]
        north, slope_y = physical(1), physical(3)
        product = [p + a * b for p, a, b in zip(product, north, slope_y)]
        real, imag = real_analysis(product)
        for k in range(9):
            jac[0, k, rows, :] = real[k]
            if imag[k] is not None:
                jac[1, k, rows, :] = imag[k]
    real = [jac[0, k] for k in range(9)]
    imag = [None] + [jac[1, k] for k in range(1, 8)] + [None]
    store_x(out_ref, x_forward(real, imag, twiddle, table_ref))


def tendency_kernel(
    in_ref, spec_ref, radix_ref, unradix_ref, turn_ref, lanes_ref, unlanes_ref, facts_ref, out_ref
):
    facts = facts_ref[...]
    flux = y_forward(load_pieces(in_ref), radix_ref, turn_ref, lanes_ref, facts)
    wave_x = x_waves(facts, lax.axis_index("row"))
    wave_y = y_waves(facts)
    ratio = (wave_x * wave_x + wave_y * wave_y) * (1.0 / (KCUT * KCUT))
    ratio = ratio * ratio
    damping = HYPER_RATE * (ratio * ratio)
    weight = jnp.where(wave_x == 0.0, 0.5, 1.0)
    total = -(flux + damping * spec_ref[...]) * weight
    store_pieces(out_ref, y_inverse([total], unradix_ref, turn_ref, unlanes_ref))


def state_update_kernel(
    in_ref, state_ref, start_ref, twiddle_ref, untable_ref, tendency_ref, new_ref, z0, z1, z2
):
    groups = load_x(in_ref, 1)
    z0[...], z1[...], z2[...] = x_inverse(groups[0][0], groups[1][0], 1, untable_ref)
    twiddle = twiddle_ref[...]
    for block in range(4):
        rows = slice(8 * block, 8 * block + 8)
        tendency = real_synthesis(*modes_of(z0, z1, z2, 0, rows, twiddle))
        for a in range(16):
            columns = slice(128 * a, 128 * a + 128)
            tendency_ref[0, rows, columns] = tendency[a]
            new_ref[0, rows, columns] = 0.75 * start_ref[0, rows, columns] + 0.25 * (
                state_ref[0, rows, columns] + STEP_SIZE * tendency[a]
            )


VMEM = pl.BlockSpec(memory_space=pltpu.VMEM)
SMEM = pl.BlockSpec(memory_space=pltpu.SMEM)


def call(kernel, outs, operands, scalars=0, scratch=()):
    return pl.pallas_call(
        kernel,
        out_shape=[jax.ShapeDtypeStruct(shape, F32) for shape in outs],
        in_specs=[SMEM] * scalars + [VMEM] * (len(operands) - scalars),
        out_specs=[VMEM] * len(outs),
        scratch_shapes=[pltpu.VMEM(shape, F32) for shape in scratch],
        compiler_params=pltpu.CompilerParams(vmem_limit_bytes=40 * 1024 * 1024),
    )(*operands)


def exchange(chunks, devices):
    length = chunks.shape[0]
    sent = chunks.reshape(devices, 1, length * 128 // devices)
    return lax.all_to_all(sent, "row", split_axis=0, concat_axis=0, tiled=True).reshape(length, 128)


def per_device(state, start_state, to_modes, from_modes, deform):
    devices = lax.axis_size("row")
    turn_x = jnp.asarray(x_twiddle())
    forward_x = jnp.asarray(x_forward_table())
    inverse_x = jnp.asarray(x_inverse_table(False))
    inverse_ix = jnp.asarray(x_inverse_table(True))
    radix = jnp.asarray(y_radix_table())
    unradix = jnp.asarray(y_radix_inverse_table())
    turn_y = jnp.asarray(y_twiddle())
    lanes = jnp.asarray(y_lane_table())
    unlanes = jnp.asarray(y_lane_inverse_table())
    facts = jnp.asarray(lane_facts())

    one, two = (64 * CHUNK, 128), (128 * CHUNK, 128)
    (columns,) = call(state_kernel, [one], [state, turn_x, forward_x])
    columns = exchange(columns, devices)
    spectrum, slopes = call(
        spectrum_kernel,
        [(KAP, SPAN), two],
        [columns, radix, unradix, turn_y, lanes, unlanes, facts],
    )
    slopes = exchange(slopes, devices)
    gathered = lax.all_gather(spectrum, "layer", axis=0, tiled=False)
    (flow,) = call(
        stream_kernel,
        [two],
        [to_modes, from_modes, deform, gathered, unradix, turn_y, unlanes, facts],
        scalars=3,
    )
    flow = exchange(flow, devices)
    (flux,) = call(
        jacobian_kernel,
        [one],
        [flow, slopes, turn_x, inverse_ix, forward_x],
        scratch=[(512, 256)] * 3 + [(2, 9, ROWS, 128)],
    )
    flux = exchange(flux, devices)
    (total,) = call(
        tendency_kernel, [one], [flux, spectrum, radix, unradix, turn_y, lanes, unlanes, facts]
    )
    total = exchange(total, devices)
    return tuple(
        call(
            state_update_kernel,
            [(1, ROWS, GRID)] * 2,
            [total, state, start_state, turn_x, inverse_x],
            scratch=[(128, 256)] * 3,
        )
    )


def solution(mesh):
    in_specs = (P("layer", "row", None), P("layer", "row", None), P(), P(), P())
    out_specs = (P("layer", "row", None), P("layer", "row", None))
    return jax.shard_map(
        per_device, mesh=mesh, in_specs=in_specs, out_specs=out_specs, check_vma=False
    )
```

time: 510 us -> 144 us (0.28); the launches traced: 501 us -> 143 us
  other arithmetic: 141 us -> 0 us
  starting transfers between devices: 128 us -> 5.69 us
  local copies, waits for them, and re-layouts: 94.1 us -> 5.12 us
  matrix products: 57.1 us -> 0 us
  blocking collectives: 40.6 us -> 81.8 us
  between operations: 2.7 us -> 14.2 us
  waiting for transfers between devices: 36.9 us -> 27.2 us
  Pallas kernels: 0 us -> 9.34 us
    all_to_all x14 -> x1, starting transfers between devices: 128 us -> 5.65 us  [exchange(): lax.all_to_all(sent, 'row', split_axis=0, concat_axis=0, tiled=True)]
    unnamed x14 -> x0, other arithmetic: 120 us -> none
    all_to_all x0 -> x4, blocking collectives: none -> 81.8 us  [exchange(): lax.all_to_all(sent, 'row', split_axis=0, concat_axis=0, tiled=True)]
    dot_general x82 -> x0, matrix products: 41.3 us -> none  [the longest x78 36.1 us: product(): jnp.einsum(pattern, operand, table_part, precision=TRANSFORM_PRECISION)]
    unnamed x80 -> x40, local copies, waits for them, and re-layouts: 46 us -> 5.12 us
    all_gather x2 -> x0, blocking collectives: 40.6 us -> none  [the longest x1 23.1 us: per_device(): lax.all_gather(vort_imag, 'layer', axis=0, tiled=True)]
    all_to_all x14 -> x1, waiting for transfers between devices: 36.9 us -> 0.01 us  [exchange(): lax.all_to_all(sent, 'row', split_axis=0, concat_axis=0, tiled=True)]
    all_to_all x32 -> x0, local copies, waits for them, and re-layouts: 28.2 us -> none  [the longest x10 8.33 us: physical(): lax.all_to_all(outgoing[0], 'row', split_axis=2, concat_axis=1, tiled=True)]
  transfers between devices with their start and end apart: 14 -> 2, of which waited for: 12 -> 1; matrix products, arithmetic and copies ran while one was open for 37% -> 0% of each run, Pallas kernels for 0% -> 1%
where the time goes in v1:
time: 144 us; the launch traced here: 143 us
  blocking collectives  81.8 us (57%)
  waiting for transfers between devices  27.2 us (19%)
  between operations  14.2 us (10%)
  Pallas kernels  9.34 us (6%)
  starting transfers between devices  5.69 us (4%)
  local copies, waits for them, and re-layouts  5.12 us (4%)
    all_to_all x4, blocking collectives, exchange(): lax.all_to_all(sent, 'row', split_axis=0, concat_axis=0, tiled=True)  81.8 us
    all_gather x1, waiting for transfers between devices, per_device(): gathered = lax.all_gather(spectrum, 'layer', axis=0, tiled=False)  27.1 us
    pallas_call x6, Pallas kernels, call(): pl.pallas_call(kernel, out_shape=[jax.ShapeDtypeStruct(shape, F32) for sh...  9.34 us
    all_to_all x1, starting transfers between devices, exchange(): lax.all_to_all(sent, 'row', split_axis=0, concat_axis=0, tiled=True)  5.65 us
    unnamed x40, local copies, waits for them, and re-layouts  5.12 us
  transfers between devices with their start and end apart: 2, of which 1 were waited for; matrix products, arithmetic and copies ran while one was open for 0% of the time, Pallas kernels for 1%

profile of v1, /device:TPU:8, one launch (start us, length us, event | category | flops | bytes accessed | tf_op | source)
XLA Modules:
  0.0 143.4 jit_solution(15113730665032968054)
XLA Ops:
  7.2 0.0 copy-start
  7.2 0.0 all-gather.3.cloned.1.call-start
  7.2 0.0 copy-start.3
  7.2 1.0 copy-done.3
  8.2 0.9 copy-done.5
  9.2 0.7 copy-done.15
  9.9 0.4 shard_map.158
  10.3 0.0 copy-start.8
  10.3 0.0 copy-start.9
  10.4 0.0 copy-start.11
  10.4 0.0 copy-start.14
  10.4 23.3 %all_to_all.25 = f32[64,1,768]{2,1,0:T(1,128)S(1)} all-to-all(f32[64,1,768]{2,1,0:T(1,128)S(1)} %bitcast.18), channel_id=1, replica_groups=mesh['layer'=8,'row'=64] {'row'}, dimensions={0} | all-to-all | bytes 393216 | tf_op jit(solution)/shard_map/all_to_all | solution.py:489
  33.7 0.0 copy-start.1
  33.8 1.1 copy-done.1
  34.9 1.9 %shard_map.159 = (f32[64,512]{1,0:T(8,128)}, f32[768,128]{1,0:T(8,128)}) custom-call(f32[384,128]{1,0:T(8,128)S(1)} %bitcast.20, bf16[2,128,128]{2,1,0:T(8,128)(2,1)S(1)} %copy-done.11, bf16[2,128,128]{2,1,0:T(8,128)(2,1)S(1)} %copy-done.9, f32[2,64,128]{2,1,0:T(8,128)S(1)} %copy-done.8, bf16[2,3,256,256]{3,2,1,0:T(8,128)(2,1)S(1)} %copy-done.1, ...), custom_call_target="tpu_custom_call" | custom-call | tf_op jit(solution)/shard_map/pallas_call | solution.py:476
  36.8 0.0 all-gather.3.cloned.1.call-update
  36.8 0.0 copy-start.17
  36.8 0.0 copy-start.18
  36.8 5.6 %all-to-all-start.2 = ((f32[64,1,1536]{2,1,0:T(1,128)}), f32[64,1,1536]{2,1,0:T(1,128)S(1)}, u32[]{:S(2)}, u32[]{:S(2)}) async-start(f32[64,1,1536]{2,1,0:T(1,128)} %bitcast.5), calls=%async_computation.2 | async-start | bytes 786432 | tf_op jit(solution)/shard_map/all_to_all | solution.py:489
  42.5 27.1 %all-gather.3.cloned.1.call-done = f32[512,512]{1,0:T(8,128)} async-done(((f32[64,512]{1,0:T(8,128)}), f32[512,512]{1,0:T(8,128)}) %all-gather.3.cloned.1.call-update) | async-done | bytes 1048592 | tf_op jit(solution)/shard_map/all_gather | solution.py:514
  69.6 1.2 copy-done.7
  70.9 2.1 %shard_map.160 = f32[768,128]{1,0:T(8,128)S(1)} custom-call(f32[8,8]{1,0:T(8,128)S(1)} %copy-done.17, f32[8,8]{1,0:T(8,128)S(1)} %copy-done.18, f32[8]{0:T(128)S(1)} %copy-done.19, f32[8,64,512]{2,1,0:T(8,128)S(1)} %bitcast.14, bf16[2,128,128]{2,1,0:T(8,128)(2,1)S(1)} %copy-done.9, f32[2,64,128]{2,1,0:T(8,128)S(1)} %copy-done.8, ...), custom_call_target="tpu_custom_call" | custom-call | tf_op jit(solution)/shard_map/pallas_call | solution.py:476
  73.0 0.0 copy-start.6
  73.0 0.0 copy-start.13
  73.0 0.0 copy-start.16
  73.0 25.3 %all_to_all.26 = f32[64,1,1536]{2,1,0:T(1,128)S(1)} all-to-all(f32[64,1,1536]{2,1,0:T(1,128)S(1)} %bitcast.13), channel_id=1, replica_groups=mesh['layer'=8,'row'=64] {'row'}, dimensions={0} | all-to-all | bytes 786432 | tf_op jit(solution)/shard_map/all_to_all | solution.py:489
  98.4 0.0 copy-start.2
  98.4 1.7 %shard_map.161 = f32[384,128]{1,0:T(8,128)S(1)} custom-call(f32[768,128]{1,0:T(8,128)S(1)} %bitcast.12, f32[768,128]{1,0:T(8,128)S(1)} %bitcast.11, f32[32,128]{1,0:T(8,128)S(1)} %copy-done.16, bf16[2,192,256]{2,1,0:T(8,128)(2,1)S(1)} %copy-done.13, bf16[2,2,128,256]{3,2,1,0:T(8,128)(2,1)S(1)} %copy-done.6), custom_call_target="tpu_custom_call" | custom-call | tf_op jit(solution)/shard_map/pallas_call | solution.py:476
  100.1 17.3 %all_to_all.27 = f32[64,1,768]{2,1,0:T(1,128)S(1)} all-to-all(f32[64,1,768]{2,1,0:T(1,128)S(1)} %bitcast.19), channel_id=1, replica_groups=mesh['layer'=8,'row'=64] {'row'}, dimensions={0} | all-to-all | bytes 393216 | tf_op jit(solution)/shard_map/all_to_all | solution.py:489
  117.4 2.0 %shard_map.162 = f32[384,128]{1,0:T(8,128)S(1)} custom-call(f32[384,128]{1,0:T(8,128)S(1)} %bitcast.15, f32[64,512]{1,0:T(8,128)} %get-tuple-element.4.spec_ref, bf16[2,128,128]{2,1,0:T(8,128)(2,1)S(1)} %copy-done.11, bf16[2,128,128]{2,1,0:T(8,128)(2,1)S(1)} %copy-done.9, f32[2,64,128]{2,1,0:T(8,128)S(1)} %copy-done.8, ...), custom_call_target="tpu_custom_call" | custom-call | tf_op jit(solution)/shard_map/pallas_call | solution.py:476
  119.4 15.9 %all_to_all.28 = f32[64,1,768]{2,1,0:T(1,128)S(1)} all-to-all(f32[64,1,768]{2,1,0:T(1,128)S(1)} %bitcast.16), channel_id=1, replica_groups=mesh['layer'=8,'row'=64] {'row'}, dimensions={0} | all-to-all | bytes 393216 | tf_op jit(solution)/shard_map/all_to_all | solution.py:489
  135.3 1.2 shard_map.163
  (23 shorter events, 0.1 us)
Async XLA Ops:
  7.2 26.6 %copy-start = (bf16[2,3,256,256]{3,2,1,0:T(8,128)(2,1)S(1)}, bf16[2,3,256,256]{3,2,1,0:T(8,128)(2,1)}, u32[]{:S(2)}) copy-start(bf16[2,3,256,256]{3,2,1,0:T(8,128)(2,1)} %constant.28.clone.unlanes_ref) | copy-start | bytes 2359300
  7.2 62.5 %all-gather.3.cloned.1.call-start = ((), (), s32[]{:S(2)}) async-start(), calls=%async_computation.5 | async-start | bytes 1179648 | tf_op jit(solution)/shard_map/all_gather | solution.py:514
  7.2 1.0 copy-start.3
  8.2 0.9 copy-start.5
  9.2 0.7 copy-start.15
  10.3 23.4 %copy-start.8 = (f32[2,64,128]{2,1,0:T(8,128)S(1)}, f32[2,64,128]{2,1,0:T(8,128)}, u32[]{:S(2)}) copy-start(f32[2,64,128]{2,1,0:T(8,128)} %constant.26.clone.turn_ref) | copy-start | bytes 196612
  10.3 23.4 %copy-start.9 = (bf16[2,128,128]{2,1,0:T(8,128)(2,1)S(1)}, bf16[2,128,128]{2,1,0:T(8,128)(2,1)}, u32[]{:S(2)}) copy-start(bf16[2,128,128]{2,1,0:T(8,128)(2,1)} %constant.25.clone.unradix_ref) | copy-start | bytes 196612
  10.4 23.4 %copy-start.11 = (bf16[2,128,128]{2,1,0:T(8,128)(2,1)S(1)}, bf16[2,128,128]{2,1,0:T(8,128)(2,1)}, u32[]{:S(2)}) copy-start(bf16[2,128,128]{2,1,0:T(8,128)(2,1)} %constant.24.clone.radix_ref) | copy-start | bytes 196612
  10.4 23.4 %copy-start.14 = (f32[8,512]{1,0:T(8,128)S(1)}, f32[8,512]{1,0:T(8,128)}, u32[]{:S(2)}) copy-start(f32[8,512]{1,0:T(8,128)} %constant.29.clone.facts_ref) | copy-start | bytes 49156
  33.7 1.1 copy-start.1
  36.8 32.8 %copy-start.17 = (f32[8,8]{1,0:T(8,128)S(1)}, f32[8,8]{1,0:T(8,128)}, u32[]{:S(2)}) copy-start(f32[8,8]{1,0:T(8,128)} %to_ref.1) | copy-start | bytes 772
  36.8 32.8 %copy-start.18 = (f32[8,8]{1,0:T(8,128)S(1)}, f32[8,8]{1,0:T(8,128)}, u32[]{:S(2)}) copy-start(f32[8,8]{1,0:T(8,128)} %from_ref.1) | copy-start | bytes 772
  36.8 36.2 %all-to-all-start.2 = ((f32[64,1,1536]{2,1,0:T(1,128)}), f32[64,1,1536]{2,1,0:T(1,128)S(1)}, u32[]{:S(2)}, u32[]{:S(2)}) async-start(f32[64,1,1536]{2,1,0:T(1,128)} %bitcast.5), calls=%async_computation.2 | async-start | bytes 786432 | tf_op jit(solution)/shard_map/all_to_all | solution.py:489
  42.5 27.2 %copy-start.19 = (f32[8]{0:T(128)S(1)}, f32[8]{0:T(128)}, u32[]{:S(2)}) copy-start(f32[8]{0:T(128)} %deform_ref.1) | copy-start | bytes 100
  69.6 1.2 copy-start.7
  73.0 25.4 %copy-start.6 = (bf16[2,2,128,256]{3,2,1,0:T(8,128)(2,1)S(1)}, bf16[2,2,128,256]{3,2,1,0:T(8,128)(2,1)}, u32[]{:S(2)}) copy-start(bf16[2,2,128,256]{3,2,1,0:T(8,128)(2,1)} %constant.21.clone.table_ref) | copy-start | bytes 786436
  73.0 25.4 %copy-start.13 = (bf16[2,192,256]{2,1,0:T(8,128)(2,1)S(1)}, bf16[2,192,256]{2,1,0:T(8,128)(2,1)}, u32[]{:S(2)}) copy-start(bf16[2,192,256]{2,1,0:T(8,128)(2,1)} %constant.23.clone.untable_ref) | copy-start | bytes 589828
  73.0 25.3 %copy-start.16 = (f32[32,128]{1,0:T(8,128)S(1)}, f32[32,128]{1,0:T(8,128)}, u32[]{:S(2)}) copy-start(f32[32,128]{1,0:T(8,128)} %constant.20.clone.twiddle_ref) | copy-start | bytes 49156
  98.4 19.0 %copy-start.2 = (bf16[2,3,256,256]{3,2,1,0:T(8,128)(2,1)S(1)}, bf16[2,3,256,256]{3,2,1,0:T(8,128)(2,1)}, u32[]{:S(2)}) copy-start(bf16[2,3,256,256]{3,2,1,0:T(8,128)(2,1)} %constant.27.clone.lanes_ref) | copy-start | bytes 2359300
  117.4 17.9 %copy-start.10 = (f32[1,32,2048]{2,1,0:T(8,128)S(1)}, f32[1,32,2048]{2,1,0:T(8,128)}, u32[]{:S(2)}) copy-start(f32[1,32,2048]{2,1,0:T(8,128)} %start_ref.1) | copy-start | bytes 786436
  117.4 17.9 %copy-start.12 = (bf16[2,192,256]{2,1,0:T(8,128)(2,1)S(1)}, bf16[2,192,256]{2,1,0:T(8,128)(2,1)}, u32[]{:S(2)}) copy-start(bf16[2,192,256]{2,1,0:T(8,128)(2,1)} %constant.22.clone.untable_ref) | copy-start | bytes 589828
  119.4 15.9 %copy-start.4 = (f32[1,32,2048]{2,1,0:T(8,128)S(1)}, f32[1,32,2048]{2,1,0:T(8,128)}, u32[]{:S(2)}) copy-start(f32[1,32,2048]{2,1,0:T(8,128)} %state_ref.3) | copy-start | bytes 786436
Sparse Core Ops, SparseCore 0:
  36.9 32.6 all-gather.2

commit v2 on v1

--- a/solution.py
+++ b/solution.py
@@ -19,6 +19,7 @@
 JP = 21
 PIECE = 8 * JP
 SPAN = 512
+USED = 504
 HYPER_RATE = 0.2
 STEP_SIZE = 0.5
 BF16 = jnp.bfloat16
@@ -372,30 +373,42 @@
     return groups
 
 
-def state_kernel(state_ref, twiddle_ref, table_ref, out_ref):
+def state_kernel(state_hbm, twiddle_hbm, table_hbm, out_ref, state_ref, twiddle_ref, table_ref, sems):
+    pairs = ((state_hbm, state_ref), (twiddle_hbm, twiddle_ref), (table_hbm, table_ref))
+    copies = [pltpu.make_async_copy(a, b, sems.at[i]) for i, (a, b) in enumerate(pairs)]
+    for copy in copies:
+        copy.start()
+    for copy in copies:
+        copy.wait()
     x = [state_ref[0, :, 128 * a : 128 * a + 128] for a in range(16)]
     real, imag = real_analysis(x)
     store_x(out_ref, x_forward(real, imag, twiddle_ref[...], table_ref))
 
 
-def spectrum_kernel(in_ref, radix_ref, unradix_ref, turn_ref, lanes_ref, unlanes_ref, facts_ref, spec_ref, out_ref):
+def spectrum_kernel(in_ref, radix_ref, turn_ref, lanes_ref, facts_ref, spec_ref, used_ref):
     facts = facts_ref[...]
     spectrum = y_forward(load_pieces(in_ref), radix_ref, turn_ref, lanes_ref, facts)
     spec_ref[...] = spectrum
-    wave_x = x_waves(facts, lax.axis_index("row"))
-    wave_y = y_waves(facts)
-    weight = jnp.where(wave_x == 0.0, 0.5, 1.0)
-    fields = [wave_x * spectrum, (wave_y * weight) * spectrum]
-    store_pieces(out_ref, y_inverse(fields, unradix_ref, turn_ref, unlanes_ref))
+    used_ref[...] = spectrum[:, :USED]
 
 
 def stream_kernel(
-    to_ref, from_ref, deform_ref, all_ref, unradix_ref, turn_ref, unlanes_ref, facts_ref, out_ref
+    to_ref,
+    from_ref,
+    deform_ref,
+    all_ref,
+    spec_ref,
+    unradix_ref,
+    turn_ref,
+    unlanes_ref,
+    facts_ref,
+    out_ref,
+    stream_ref,
 ):
     facts = facts_ref[...]
     wave_x = x_waves(facts, lax.axis_index("row"))
     wave_y = y_waves(facts)
-    square = wave_x * wave_x + wave_y * wave_y
+    square = (wave_x * wave_x + wave_y * wave_y)[:, :USED]
     stream = stream_function(
         lambda n: all_ref[n],
         lambda m, n: to_ref[m, n],
@@ -404,16 +417,19 @@
         lax.axis_index("layer"),
         square,
     )
-    weight = jnp.where(wave_x == 0.0, 0.5, 1.0)
-    fields = [-(wave_y * weight) * stream, wave_x * stream]
+    stream_ref[:, SPAN - 128 :] = jnp.zeros((KAP, 128), F32)
+    stream_ref[:, :USED] = stream
+    stream = stream_ref[...]
+    spectrum = spec_ref[...]
+    along_y = wave_y * jnp.where(wave_x == 0.0, 0.5, 1.0)
+    fields = [-along_y * stream, wave_x * stream, wave_x * spectrum, along_y * spectrum]
     store_pieces(out_ref, y_inverse(fields, unradix_ref, turn_ref, unlanes_ref))
 
 
-def jacobian_kernel(flow_ref, slope_ref, twiddle_ref, untable_ref, table_ref, out_ref, z0, z1, z2, jac):
-    flow = load_x(flow_ref, 2)
-    slope = load_x(slope_ref, 2)
-    left = jnp.concatenate(flow[0] + slope[0], axis=1)
-    right = jnp.concatenate(flow[1] + slope[1], axis=1)
+def jacobian_kernel(in_ref, twiddle_ref, untable_ref, table_ref, out_ref, z0, z1, z2, jac):
+    groups = load_x(in_ref, 4)
+    left = jnp.concatenate(groups[0], axis=1)
+    right = jnp.concatenate(groups[1], axis=1)
     z0[...], z1[...], z2[...] = x_inverse(left, right, 4, untable_ref)
     twiddle = twiddle_ref[...]
     for block in range(4):
@@ -470,15 +486,23 @@
 
 VMEM = pl.BlockSpec(memory_space=pltpu.VMEM)
 SMEM = pl.BlockSpec(memory_space=pltpu.SMEM)
-
-
-def call(kernel, outs, operands, scalars=0, scratch=()):
+ANY = pl.BlockSpec(memory_space=pl.ANY)
+
+
+def call(kernel, outs, operands, scalars=0, scratch=(), fetched=False):
+    if fetched:
+        in_specs = [ANY] * len(operands)
+        scratch_shapes = [pltpu.VMEM(operand.shape, operand.dtype) for operand in operands]
+        scratch_shapes.append(pltpu.SemaphoreType.DMA((len(operands),)))
+    else:
+        in_specs = [SMEM] * scalars + [VMEM] * (len(operands) - scalars)
+        scratch_shapes = [pltpu.VMEM(shape, F32) for shape in scratch]
     return pl.pallas_call(
         kernel,
         out_shape=[jax.ShapeDtypeStruct(shape, F32) for shape in outs],
-        in_specs=[SMEM] * scalars + [VMEM] * (len(operands) - scalars),
+        in_specs=in_specs,
         out_specs=[VMEM] * len(outs),
-        scratch_shapes=[pltpu.VMEM(shape, F32) for shape in scratch],
+        scratch_shapes=scratch_shapes,
         compiler_params=pltpu.CompilerParams(vmem_limit_bytes=40 * 1024 * 1024),
     )(*operands)
 
@@ -502,27 +526,25 @@
     unlanes = jnp.asarray(y_lane_inverse_table())
     facts = jnp.asarray(lane_facts())
 
-    one, two = (64 * CHUNK, 128), (128 * CHUNK, 128)
-    (columns,) = call(state_kernel, [one], [state, turn_x, forward_x])
+    one, four = (64 * CHUNK, 128), (256 * CHUNK, 128)
+    (columns,) = call(state_kernel, [one], [state, turn_x, forward_x], fetched=True)
     columns = exchange(columns, devices)
-    spectrum, slopes = call(
-        spectrum_kernel,
-        [(KAP, SPAN), two],
-        [columns, radix, unradix, turn_y, lanes, unlanes, facts],
-    )
-    slopes = exchange(slopes, devices)
-    gathered = lax.all_gather(spectrum, "layer", axis=0, tiled=False)
-    (flow,) = call(
+    spectrum, used = call(
+        spectrum_kernel, [(KAP, SPAN), (KAP, USED)], [columns, radix, turn_y, lanes, facts]
+    )
+    gathered = lax.all_gather(used, "layer", axis=0, tiled=False)
+    (fields,) = call(
         stream_kernel,
-        [two],
-        [to_modes, from_modes, deform, gathered, unradix, turn_y, unlanes, facts],
+        [four],
+        [to_modes, from_modes, deform, gathered, spectrum, unradix, turn_y, unlanes, facts],
         scalars=3,
-    )
-    flow = exchange(flow, devices)
+        scratch=[(KAP, SPAN)],
+    )
+    fields = exchange(fields, devices)
     (flux,) = call(
         jacobian_kernel,
         [one],
-        [flow, slopes, turn_x, inverse_ix, forward_x],
+        [fields, turn_x, inverse_ix, forward_x],
         scratch=[(512, 256)] * 3 + [(2, 9, ROWS, 128)],
     )
     flux = exchange(flux, devices)

time: 144 us -> 121 us (0.84)
  waiting for transfers between devices: 27.2 us -> 0 us
  blocking collectives: 81.8 us -> 108 us
  between operations: 14.2 us -> 0.81 us
  starting transfers between devices: 5.69 us -> 0 us
  local copies, waits for them, and re-layouts: 5.12 us -> 3.41 us
  Pallas kernels: 9.34 us -> 7.67 us
    all_gather x1 -> x0, waiting for transfers between devices: 27.1 us -> none  [per_device(): gathered = lax.all_gather(spectrum, 'layer', axis=0, tiled=False)]
    all_gather x0 -> x1, blocking collectives: none -> 22.9 us  [per_device(): gathered = lax.all_gather(used, 'layer', axis=0, tiled=False)]
    all_to_all x1 -> x0, starting transfers between devices: 5.65 us -> none  [exchange(): lax.all_to_all(sent, 'row', split_axis=0, concat_axis=0, tiled=True)]
    all_to_all x4, blocking collectives: 81.8 us -> 85.4 us  [exchange(): lax.all_to_all(sent, 'row', split_axis=0, concat_axis=0, tiled=True)]
    unnamed x40 -> x36, local copies, waits for them, and re-layouts: 5.12 us -> 3.41 us
    pallas_call x6, Pallas kernels: 9.34 us -> 7.67 us  [call(): pl.pallas_call(kernel, out_shape=[jax.ShapeDtypeStruct(shape, F32) for sh...]
  transfers between devices with their start and end apart: 2 -> 0, of which waited for: 1 -> 0; matrix products, arithmetic and copies ran while one was open for 0% -> 0% of each run, Pallas kernels for 1% -> 0%
where the time goes in v2:
time: 121 us; the launch traced here: 120 us
  blocking collectives  108 us (89%)
  Pallas kernels  7.67 us (6%)
  local copies, waits for them, and re-layouts  3.41 us (3%)
    all_to_all x4, blocking collectives, exchange(): lax.all_to_all(sent, 'row', split_axis=0, concat_axis=0, tiled=True)  85.4 us
    all_gather x1, blocking collectives, per_device(): gathered = lax.all_gather(used, 'layer', axis=0, tiled=False)  22.9 us
    pallas_call x6, Pallas kernels, call(): pl.pallas_call(kernel, out_shape=[jax.ShapeDtypeStruct(shape, F32) for sh...  7.67 us
    unnamed x36, local copies, waits for them, and re-layouts  3.41 us

profile of v2, /device:TPU:8, one launch (start us, length us, event | category | flops | bytes accessed | tf_op | source)
XLA Modules:
  0.0 120.2 jit_solution(11180840214041707814)
XLA Ops:
  0.6 0.0 copy-start
  0.6 0.0 copy-start.2
  0.7 1.0 copy-done.2
  1.7 0.9 copy-done.4
  2.6 0.7 copy-done.13
  3.3 0.5 shard_map.158
  3.9 0.0 copy-start.6
  3.9 0.0 copy-start.8
  3.9 0.0 copy-start.12
  3.9 23.3 %all_to_all.20 = f32[64,1,768]{2,1,0:T(1,128)S(1)} all-to-all(f32[64,1,768]{2,1,0:T(1,128)S(1)} %bitcast.15), channel_id=1, replica_groups=mesh['layer'=8,'row'=64] {'row'}, dimensions={0} | all-to-all | bytes 393216 | tf_op jit(solution)/shard_map/all_to_all | solution.py:513
  27.2 0.0 copy-done
  27.2 0.0 copy-done.6
  27.2 0.6 shard_map.159
  27.8 0.0 copy-start.1
  27.8 0.0 copy-start.9
  27.8 0.0 copy-start.15
  27.8 0.0 copy-start.16
  27.9 22.9 %all-gather = f32[512,504]{1,0:T(8,128)S(1)} all-gather(f32[64,504]{1,0:T(8,128)S(1)} %get-tuple-element.4), channel_id=2, replica_groups=mesh['layer'=8,'row'=64] {'layer'}, dimensions={0}, use_global_device_ids=true | all-gather | bytes 1161216 | tf_op jit(solution)/shard_map/all_gather | solution.py:535
  50.8 0.0 copy-done.16
  50.8 0.6 copy-done.17
  51.4 2.6 %shard_map.160 = f32[1536,128]{1,0:T(8,128)S(1)} custom-call(f32[8,8]{1,0:T(8,128)S(1)} %copy-done.15, f32[8,8]{1,0:T(8,128)S(1)} %copy-done.16, f32[8]{0:T(128)S(1)} %copy-done.17, f32[8,64,504]{2,1,0:T(8,128)S(1)} %bitcast.9, f32[64,512]{1,0:T(8,128)S(1)} %get-tuple-element.5.spec_ref, bf16[2,128,128]{2,1,0:T(8,128)(2,1)S(1)} %copy-done.9, ...), custom_call_target="tpu_custom_call" | custom-call | tf_op jit(solution)/shard_map/pallas_call | solution.py:500
  54.0 0.0 copy-start.5
  54.1 0.0 copy-start.11
  54.1 0.0 copy-start.14
  54.1 28.4 %all_to_all.21 = f32[64,1,3072]{2,1,0:T(1,128)S(1)} all-to-all(f32[64,1,3072]{2,1,0:T(1,128)S(1)} %bitcast.11), channel_id=1, replica_groups=mesh['layer'=8,'row'=64] {'row'}, dimensions={0} | all-to-all | bytes 1572864 | tf_op jit(solution)/shard_map/all_to_all | solution.py:513
  82.5 1.7 %shard_map.161 = f32[384,128]{1,0:T(8,128)S(1)} custom-call(f32[1536,128]{1,0:T(8,128)S(1)} %bitcast.10, f32[32,128]{1,0:T(8,128)S(1)} %copy-done.14, bf16[2,192,256]{2,1,0:T(8,128)(2,1)S(1)} %copy-done.11, bf16[2,2,128,256]{3,2,1,0:T(8,128)(2,1)S(1)} %copy-done.5), custom_call_target="tpu_custom_call" | custom-call | tf_op jit(solution)/shard_map/pallas_call | solution.py:500
  84.2 17.8 %all_to_all.22 = f32[64,1,768]{2,1,0:T(1,128)S(1)} all-to-all(f32[64,1,768]{2,1,0:T(1,128)S(1)} %bitcast.17), channel_id=1, replica_groups=mesh['layer'=8,'row'=64] {'row'}, dimensions={0} | all-to-all | bytes 393216 | tf_op jit(solution)/shard_map/all_to_all | solution.py:513
  102.0 1.0 shard_map.162
  103.1 0.0 copy-start.3
  103.1 15.9 %all_to_all.23 = f32[64,1,768]{2,1,0:T(1,128)S(1)} all-to-all(f32[64,1,768]{2,1,0:T(1,128)S(1)} %bitcast.13), channel_id=1, replica_groups=mesh['layer'=8,'row'=64] {'row'}, dimensions={0} | all-to-all | bytes 393216 | tf_op jit(solution)/shard_map/all_to_all | solution.py:513
  119.0 0.0 copy-done.7
  119.0 1.2 %shard_map.163 = (f32[1,32,2048]{2,1,0:T(8,128)}, f32[1,32,2048]{2,1,0:T(8,128)}) custom-call(f32[384,128]{1,0:T(8,128)S(1)} %bitcast.14, f32[1,32,2048]{2,1,0:T(8,128)S(1)} %copy-done.3, f32[1,32,2048]{2,1,0:T(8,128)S(1)} %copy-done.7, f32[32,128]{1,0:T(8,128)S(1)} %copy-done.14, bf16[2,192,256]{2,1,0:T(8,128)(2,1)S(1)} %copy-done.10), custom_call_target="tpu_custom_call" | custom-call | tf_op jit(solution)/shard_map/pallas_call | solution.py:500
  (15 shorter events, 0.0 us)
Async XLA Ops:
  0.6 26.6 %copy-start = (bf16[2,3,256,256]{3,2,1,0:T(8,128)(2,1)S(1)}, bf16[2,3,256,256]{3,2,1,0:T(8,128)(2,1)}, u32[]{:S(2)}) copy-start(bf16[2,3,256,256]{3,2,1,0:T(8,128)(2,1)} %constant.27.clone.lanes_ref) | copy-start | bytes 2359300
  0.6 1.0 copy-start.2
  1.7 0.9 copy-start.4
  2.6 0.7 copy-start.13
  3.9 23.4 %copy-start.6 = (f32[2,64,128]{2,1,0:T(8,128)S(1)}, f32[2,64,128]{2,1,0:T(8,128)}, u32[]{:S(2)}) copy-start(f32[2,64,128]{2,1,0:T(8,128)} %constant.26.clone.turn_ref) | copy-start | bytes 196612
  3.9 23.4 %copy-start.8 = (bf16[2,128,128]{2,1,0:T(8,128)(2,1)S(1)}, bf16[2,128,128]{2,1,0:T(8,128)(2,1)}, u32[]{:S(2)}) copy-start(bf16[2,128,128]{2,1,0:T(8,128)(2,1)} %constant.24.clone.radix_ref) | copy-start | bytes 196612
  3.9 23.4 %copy-start.12 = (f32[8,512]{1,0:T(8,128)S(1)}, f32[8,512]{1,0:T(8,128)}, u32[]{:S(2)}) copy-start(f32[8,512]{1,0:T(8,128)} %constant.29.clone.facts_ref) | copy-start | bytes 49156
  27.8 23.0 %copy-start.1 = (bf16[2,3,256,256]{3,2,1,0:T(8,128)(2,1)S(1)}, bf16[2,3,256,256]{3,2,1,0:T(8,128)(2,1)}, u32[]{:S(2)}) copy-start(bf16[2,3,256,256]{3,2,1,0:T(8,128)(2,1)} %constant.28.clone.unlanes_ref) | copy-start | bytes 2359300
  27.8 23.0 %copy-start.9 = (bf16[2,128,128]{2,1,0:T(8,128)(2,1)S(1)}, bf16[2,128,128]{2,1,0:T(8,128)(2,1)}, u32[]{:S(2)}) copy-start(bf16[2,128,128]{2,1,0:T(8,128)(2,1)} %constant.25.clone.unradix_ref) | copy-start | bytes 196612
  27.8 22.9 %copy-start.15 = (f32[8,8]{1,0:T(8,128)S(1)}, f32[8,8]{1,0:T(8,128)}, u32[]{:S(2)}) copy-start(f32[8,8]{1,0:T(8,128)} %to_ref.1) | copy-start | bytes 772
  27.8 22.9 %copy-start.16 = (f32[8,8]{1,0:T(8,128)S(1)}, f32[8,8]{1,0:T(8,128)}, u32[]{:S(2)}) copy-start(f32[8,8]{1,0:T(8,128)} %from_ref.1) | copy-start | bytes 772
  50.8 0.7 copy-start.17
  54.0 28.4 %copy-start.5 = (bf16[2,2,128,256]{3,2,1,0:T(8,128)(2,1)S(1)}, bf16[2,2,128,256]{3,2,1,0:T(8,128)(2,1)}, u32[]{:S(2)}) copy-start(bf16[2,2,128,256]{3,2,1,0:T(8,128)(2,1)} %constant.21.clone.table_hbm.table_ref) | copy-start | bytes 786436
  54.1 28.4 %copy-start.11 = (bf16[2,192,256]{2,1,0:T(8,128)(2,1)S(1)}, bf16[2,192,256]{2,1,0:T(8,128)(2,1)}, u32[]{:S(2)}) copy-start(bf16[2,192,256]{2,1,0:T(8,128)(2,1)} %constant.23.clone.untable_ref) | copy-start | bytes 589828
  54.1 28.4 %copy-start.14 = (f32[32,128]{1,0:T(8,128)S(1)}, f32[32,128]{1,0:T(8,128)}, u32[]{:S(2)}) copy-start(f32[32,128]{1,0:T(8,128)} %constant.20.clone.twiddle_hbm.twiddle_ref) | copy-start | bytes 49156
  102.0 17.0 %copy-start.7 = (f32[1,32,2048]{2,1,0:T(8,128)S(1)}, f32[1,32,2048]{2,1,0:T(8,128)}, u32[]{:S(2)}) copy-start(f32[1,32,2048]{2,1,0:T(8,128)} %start_ref.1) | copy-start | bytes 786436
  102.0 17.0 %copy-start.10 = (bf16[2,192,256]{2,1,0:T(8,128)(2,1)S(1)}, bf16[2,192,256]{2,1,0:T(8,128)(2,1)}, u32[]{:S(2)}) copy-start(bf16[2,192,256]{2,1,0:T(8,128)(2,1)} %constant.22.clone.untable_ref) | copy-start | bytes 589828
  103.1 15.9 %copy-start.3 = (f32[1,32,2048]{2,1,0:T(8,128)S(1)}, f32[1,32,2048]{2,1,0:T(8,128)}, u32[]{:S(2)}) copy-start(f32[1,32,2048]{2,1,0:T(8,128)} %state_ref.1) | copy-start | bytes 786436

commit v3 on v2

v3 whole, which is shorter than its diff:
```python
import functools
import math

import jax
import jax.numpy as jnp
import ml_dtypes
import numpy as np
from jax import lax
from jax.experimental import pallas as pl
from jax.experimental.pallas import tpu as pltpu
from jax.sharding import PartitionSpec as P

GRID = 2048
KCUT = 672
ROWS = 32
HALF = 14
CHUNK = 6
KAP = 64
JP = 21
USED = 6 * JP
WIDE = 256
FIELDS = 4
HYPER_RATE = 0.2
STEP_SIZE = 0.5
BF16 = jnp.bfloat16
F32 = jnp.float32


def halves(table):
    high = table.astype(ml_dtypes.bfloat16)
    low = (table - high.astype(np.float64)).astype(ml_dtypes.bfloat16)
    return np.stack([high, low])


def turn(numerator, denominator):
    angle = 2.0 * math.pi * (np.mod(numerator, denominator) / denominator)
    return np.cos(angle), np.sin(angle)


def x_forward_table(apart):
    b = np.arange(128)
    table = np.zeros((2, 3, 16, 2, 2, 128))
    for half in range(2):
        for tau in range(HALF):
            for j3 in range(3):
                c, s = turn((3 * tau + j3 - 42 * half) * b, 128)
                table[half, j3, tau, 0, 0] = c
                table[half, j3, tau, 0, 1] = s
                table[half, j3, tau, 1, 0] = -s
                table[half, j3, tau, 1, 1] = c
    if apart:
        table = np.swapaxes(table, 2, 3)
    return halves(table.reshape(2, 96, 256))


def x_inverse_table(times_i):
    b = np.arange(128)
    table = np.zeros((2, 2, 3, 16, 2, 128))
    for half in range(2):
        for tau in range(HALF):
            for j3 in range(3):
                c, s = turn((3 * tau + j3 - 42 * half) * b, 128)
                if times_i:
                    c, s = -s, c
                table[half, 0, j3, tau, 0] = c
                table[half, 0, j3, tau, 1] = s
                table[half, 1, j3, tau, 0] = -s
                table[half, 1, j3, tau, 1] = c
    return halves(table.reshape(192, 256) * (2.0 / (GRID * GRID)))


def x_twiddle():
    table = np.zeros((32, 128))
    c, s = turn(np.arange(9)[:, None] * np.arange(128)[None, :], GRID)
    table[0:9] = c
    table[16:25] = s
    return table.astype(np.float32)


def paired(table):
    high, low = halves(table)
    return np.concatenate([high, high, low], axis=1)


def y_radix_table():
    c, s = turn(np.arange(KAP)[:, None] * np.arange(64)[None, :] + 32 * np.arange(64)[None, :], 64)
    return paired(np.block([[c, s], [-s, c]]))


def y_radix_inverse_table():
    c, s = turn(np.arange(64)[:, None] * np.arange(KAP)[None, :] + 32 * np.arange(64)[:, None], 64)
    return paired(np.block([[c, -s], [s, c]]))


def y_twiddle():
    c, s = turn((np.arange(KAP)[:, None] - KCUT) * np.arange(ROWS)[None, :], GRID)
    return np.stack([np.tile(c, (1, 4)), np.tile(s, (1, 4))]).astype(np.float32)


def lanes_of(block, j3):
    c, s = turn(np.arange(ROWS)[:, None] * np.arange(JP)[None, :], ROWS)
    table = np.zeros((2, 4, ROWS, 128))
    re = 2 * JP * j3
    im = re + JP
    table[0, block, :, re : re + JP] = c
    table[1, block, :, re : re + JP] = s
    table[0, block, :, im : im + JP] = -s
    table[1, block, :, im : im + JP] = c
    return table.reshape(256, 128)


def y_lane_table():
    return halves(sum(lanes_of(j3, j3) for j3 in range(3)))


def y_lane_inverse_table():
    own = sum(lanes_of(j3, j3) for j3 in range(3)).T
    return halves(np.stack([np.concatenate([own, lanes_of(3, f).T], axis=0) for f in range(3)]))


def y_projection_table():
    difference = np.arange(ROWS)[None, :] - np.arange(ROWS)[:, None]
    c, s = turn(difference[:, :, None] * np.arange(JP)[None, None, :], ROWS)
    c, s = np.kron(np.eye(4), c.sum(-1)), np.kron(np.eye(4), s.sum(-1))
    return halves(np.block([[c, s], [-s, c]]))


def y_mean_table():
    return np.kron(np.eye(8), np.ones((ROWS, ROWS))).astype(ml_dtypes.bfloat16)


def lane_facts():
    lane = np.arange(128)
    facts = np.zeros((8, 128))
    facts[0] = 16 * (lane // (2 * JP))
    facts[1] = 64 * (lane % JP) - KCUT
    return facts.astype(np.float32)


def split(value):
    high = value.astype(BF16)
    low = (value - high.astype(F32)).astype(BF16)
    return high, low


def matmul(left, right, dims):
    def one(a, b):
        return lax.dot_general(a, b, (dims, ((), ())), preferred_element_type=F32)

    return one(left[0], right[0]) + (one(left[0], right[1]) + one(left[1], right[0]))


def matmul_deep(table, right):
    depth = right[0].shape[0]

    def one(a, b):
        return lax.dot_general(a, b, (NN, ((), ())), preferred_element_type=F32)

    both = jnp.concatenate(right, axis=0)
    return one(table[:, : 2 * depth], both) + one(table[:, 2 * depth :], right[0])


NN = ((1,), (0,))
NT = ((1,), (1,))
TN = ((0,), (0,))

C1 = math.cos(math.pi / 8)
C2 = math.cos(math.pi / 4)
C3 = math.cos(3 * math.pi / 8)


def real_analysis(x):
    s = [x[a] + x[a + 8] for a in range(8)]
    d = [x[a] - x[a + 8] for a in range(8)]
    e = [None] + [d[a] - d[8 - a] for a in range(1, 4)]
    f = [None] + [d[a] + d[8 - a] for a in range(1, 4)]
    e2, f2 = e[2] * C2, f[2] * C2
    plus, minus = d[0] + e2, d[0] - e2
    first, second = e[1] * C1 + e[3] * C3, e[1] * C3 - e[3] * C1
    third, fourth = f[1] * C3 + f[3] * C1, f[1] * C1 - f[3] * C3
    u, v = d[4] + f2, f2 - d[4]
    p = [s[a] + s[a + 4] for a in range(4)]
    q = [s[a] - s[a + 4] for a in range(4)]
    even, odd = p[0] + p[2], p[1] + p[3]
    hd, hs = (q[1] - q[3]) * C2, (q[1] + q[3]) * C2
    real = [
        even + odd,
        plus + first,
        q[0] + hd,
        minus + second,
        p[0] - p[2],
        minus - second,
        q[0] - hd,
        plus - first,
        even - odd,
    ]
    imag = [
        None,
        -(third + u),
        -(q[2] + hs),
        -(fourth + v),
        p[3] - p[1],
        v - fourth,
        q[2] - hs,
        u - third,
        None,
    ]
    return real, imag


def real_synthesis(real, imag):
    plus, first = real[1] + real[7], real[1] - real[7]
    minus, second = real[3] + real[5], real[3] - real[5]
    third, u = -(imag[1] + imag[7]), imag[7] - imag[1]
    fourth, v = -(imag[3] + imag[5]), imag[5] - imag[3]
    d = [None] * 8
    d[0], d[4] = plus + minus, u - v
    e = [None, first * C1 + second * C3, (plus - minus) * C2, first * C3 - second * C1]
    f = [None, third * C3 + fourth * C1, (u + v) * C2, third * C1 - fourth * C3]
    for a in range(1, 4):
        d[a], d[8 - a] = f[a] + e[a], f[a] - e[a]
    even, odd = real[0] + real[8], real[0] - real[8]
    p = [even + real[4], odd - imag[4], even - real[4], odd + imag[4]]
    hr, hi = (real[2] - real[6]) * C2, (imag[2] + imag[6]) * C2
    q = [real[2] + real[6], hr - hi, imag[6] - imag[2], -(hr + hi)]
    s = [p[a] + q[a] for a in range(4)] + [p[a] - q[a] for a in range(4)]
    return [s[a] + d[a] for a in range(8)] + [s[a] - d[a] for a in range(8)]


def regroup(blocks, wanted):
    block = lax.broadcasted_iota(jnp.int32, (1, 128), 1) // 32
    turned = [
        b if b is None or i == 0 else pltpu.roll(b, 32 * i, 1) for i, b in enumerate(blocks)
    ]
    results = []
    for p in wanted:
        total = None
        for i in range(4):
            part = jnp.zeros_like(turned[0]) if turned[i] is None else turned[i]
            total = part if total is None else jnp.where(block == (p + i) % 4, part, total)
        results.append(total if p == 0 else pltpu.roll(total, 128 - 32 * p, 1))
    return results


def x_forward(real, imag, twiddle, table):
    pieces = []
    for k in range(9):
        if k == 0:
            pieces.append(jnp.concatenate([real[0], jnp.zeros_like(real[0])], axis=1))
            continue
        c, s = twiddle[k : k + 1], twiddle[16 + k : 17 + k]
        if k == 8:
            re, im = real[8] * c, -(real[8] * s)
        else:
            re, im = real[k] * c + imag[k] * s, imag[k] * c - real[k] * s
        pieces.append(jnp.concatenate([re, im], axis=1))
    shared = split(jnp.concatenate(pieces[1:8], axis=0))
    results = []
    for half, own in enumerate((pieces[0], pieces[8])):
        own = split(own)
        right = [jnp.concatenate([own[i], shared[i]], axis=0) for i in range(2)]
        results.append(matmul([table[0, half], table[1, half]], right, NT))
    return results


def x_inverse(left, right, fields, table):
    left = split(left)
    right = split(right)
    upper = [table[i][:96] for i in range(2)]
    lower = [table[i][96:] for i in range(2)]
    first = matmul([part[:96] for part in left], upper, TN)
    second = matmul([part[96:] for part in left], lower, TN)
    rest = matmul(right, [table[i] for i in range(2)], TN)
    return first, second, rest


def modes_of(first, second, rest, field, rows, twiddle):
    real, imag = [], []
    for k in range(9):
        c, s = twiddle[k : k + 1], twiddle[16 + k : 17 + k]
        base = field * 128 + rows.start
        size = rows.stop - rows.start
        if k in (0, 8):
            source = first if k == 0 else second
            z = source[base : base + size]
        elif k < 4:
            start = base + 32 * k
            z = first[start : start + size] + second[start : start + size]
        else:
            start = base + 32 * (k - 4)
            z = rest[start : start + size]
        re, im = z[:, :128], z[:, 128:]
        if k == 0:
            real.append(re)
            imag.append(None)
        else:
            real.append(re * c - im * s)
            imag.append(None if k == 8 else re * s + im * c)
    return real, imag


def turn_by(re, im, c, s):
    return re * c + im * s, im * c - re * s


def retained_y(facts):
    kap = lax.broadcasted_iota(jnp.int32, (KAP, 1), 0).astype(F32)
    return kap + facts[1:2]


def place():
    layer = lax.axis_index("layer")
    return layer // 2, layer % 2, lax.axis_index("row")


def x_waves(facts, z, place_index):
    group = place_index // 32
    half = (place_index % 32) // 16
    tau = place_index % 16
    eight = jnp.where((group == 0) & (z == 0), 8 * half, 0)
    return facts[0:1] + (4 * group + z + eight + 16 * (3 * tau - 42 * half)).astype(F32)


def store_wide(out_ref, results):
    for half in range(2):
        for group in range(2):
            lanes = slice(128 * group, 128 * group + 128)
            blocks = [results[half][32 * j3 : 32 * j3 + 32, lanes] for j3 in range(3)] + [None]
            for z, block in enumerate(regroup(blocks, range(4))):
                start = 2 * (64 * z + 32 * group + 16 * half)
                out_ref[start : start + 32, :] = block


def state_kernel(
    state_hbm,
    twiddle_hbm,
    table_hbm,
    to_hbm,
    from_hbm,
    deform_hbm,
    out_ref,
    scalars_ref,
    state_ref,
    twiddle_ref,
    table_ref,
    to_ref,
    from_ref,
    deform_ref,
    sems,
):
    pairs = (
        (state_hbm, state_ref),
        (twiddle_hbm, twiddle_ref),
        (table_hbm, table_ref),
        (to_hbm, to_ref),
        (from_hbm, from_ref),
        (deform_hbm, deform_ref),
    )
    copies = [pltpu.make_async_copy(a, b, sems.at[i]) for i, (a, b) in enumerate(pairs)]
    for copy in copies:
        copy.start()
    for copy in copies:
        copy.wait()
    x = [state_ref[0, :, 128 * a : 128 * a + 128] for a in range(16)]
    real, imag = real_analysis(x)
    store_wide(out_ref, x_forward(real, imag, twiddle_ref[...], table_ref))
    for n in range(8):
        scalars_ref[8 * n : 8 * n + 8, :] = jnp.broadcast_to(to_ref[:, n : n + 1], (8, 128))
        start = 64 + 8 * n
        scalars_ref[start : start + 8, :] = jnp.broadcast_to(from_ref[:, n : n + 1], (8, 128))
    equal = lax.broadcasted_iota(jnp.int32, (8, 8), 0) == lax.broadcasted_iota(jnp.int32, (8, 8), 1)
    column = jnp.sum(jnp.where(equal, deform_ref[...], 0.0), axis=1, keepdims=True)
    scalars_ref[128:136, :] = jnp.broadcast_to(column, (8, 128))


def spectrum_kernel(in_ref, radix_ref, turn_ref, lanes_ref, facts_ref, spec_ref):
    def rows(part):
        return jnp.concatenate(
            [in_ref[pl.ds(128 * z + part, 64, stride=2), :] for z in range(4)], axis=1
        )

    mixed = matmul_deep(radix_ref, split(jnp.concatenate([rows(0), rows(1)], axis=0)))
    c, s = turn_ref[0], turn_ref[1]
    turned = []
    for z in range(4):
        lanes = slice(128 * z, 128 * z + 128)
        turned.append(jnp.concatenate(turn_by(mixed[:KAP, lanes], mixed[KAP:, lanes], c, s), axis=1))
    spectrum = matmul(split(jnp.concatenate(turned, axis=0)), lanes_ref, NN)
    wave_y = retained_y(facts_ref[...])
    for z in range(4):
        own = jnp.where(wave_y > -KCUT, spectrum[64 * z : 64 * z + 64], 0.0)
        spec_ref[64 * z : 64 * z + 64, :] = own[:, :USED]


def stream_kernel(
    scalars_ref, all_ref, unradix_ref, turn_ref, unlanes_ref, facts_ref, out_ref, full_ref
):
    z_own, core, row = place()
    for i in range(2):
        rows = slice(256 * i, 256 * i + 256)
        full_ref[rows, :] = jnp.zeros((256, 128), F32)
        full_ref[rows, :USED] = all_ref[i]

    def scalar(index):
        return scalars_ref[pl.ds(index, 1), :]

    facts = facts_ref[...]
    wave_x = x_waves(facts, z_own, row)
    wave_y = retained_y(facts)
    square = wave_x * wave_x + wave_y * wave_y
    modal = []
    for m in range(8):
        total = None
        for n in range(8):
            start = 256 * (n % 2) + 64 * (n // 2)
            term = scalar(8 * n + m) * full_ref[start : start + 64, :]
            total = term if total is None else total + term
        modal.append(total * (-1.0 / (square + scalar(128 + m))))
    ratio = square * (1.0 / (KCUT * KCUT))
    ratio = ratio * ratio
    weight = jnp.where(wave_x == 0.0, 0.5, 1.0)
    damping = (-HYPER_RATE * weight) * (ratio * ratio)
    along_y = wave_y * weight
    fields = [[] for _ in range(5)]
    for z in range(4):
        stream = None
        for m in range(8):
            term = scalar(64 + 8 * m + 2 * z + core) * modal[m]
            stream = term if stream is None else stream + term
        own = full_ref[pl.ds(256 * core + 64 * z, 64), :]
        fields[0].append(-along_y * stream)
        fields[1].append(wave_x * stream)
        fields[2].append(wave_x * own)
        fields[3].append(along_y * own)
        fields[4].append(damping * own)
    fields = [split(jnp.concatenate(field, axis=0)) for field in fields]
    c, s = turn_ref[0], turn_ref[1]
    for f in range(FIELDS):
        if f < 3:
            left = [jnp.concatenate([fields[f][i], fields[4][i]], axis=1) for i in range(2)]
            out = matmul(left, [unlanes_ref[i, f] for i in range(2)], NN)
        else:
            out = matmul(fields[f], [unlanes_ref[i, 0, :128] for i in range(2)], NN)
        real, imag = [], []
        for z in range(4):
            own = out[64 * z : 64 * z + 64]
            re, im = turn_by(own[:, :128], own[:, 128:], c, -s)
            real.append(re)
            imag.append(im)
        right = jnp.concatenate(
            [jnp.concatenate(real, axis=1), jnp.concatenate(imag, axis=1)], axis=0
        )
        out = matmul_deep(unradix_ref, split(right))
        for z in range(4):
            for part in range(2):
                out_ref[pl.ds(512 * z + 2 * f + part, 64, stride=8), :] = out[
                    64 * part : 64 * part + 64, 128 * z : 128 * z + 128
                ]


def jacobian_kernel(
    in_ref, twiddle_ref, untable_ref, table_ref, out_ref, damp_ref, z0, z1, z2, jac
):
    sides = []
    for group in range(2):
        columns = []
        for f in range(FIELDS):
            parts = []
            for part in range(2):
                blocks = [
                    in_ref[pl.ds((64 * z + 32 * group) * 8 + 2 * f + part, 32, stride=8), :]
                    for z in range(4)
                ]
                found = regroup(blocks, range(4 if f < 3 else 3))
                if f < 3:
                    for half in range(2):
                        start = 192 * group + 96 * half + 48 * part + 16 * f
                        damp_ref[start : start + 16, :] = found[3][16 * half : 16 * half + 16]
                parts.append(found)
            rows = [
                parts[part][j3][16 * half : 16 * half + 16]
                for half in range(2)
                for part in range(2)
                for j3 in range(3)
            ]
            columns.append(jnp.concatenate(rows, axis=0))
        sides.append(jnp.concatenate(columns, axis=1))
    z0[...], z1[...], z2[...] = x_inverse(sides[0], sides[1], 4, untable_ref)
    twiddle = twiddle_ref[...]
    for block in range(4):
        rows = slice(8 * block, 8 * block + 8)

        def physical(field):
            return real_synthesis(*modes_of(z0, z1, z2, field, rows, twiddle))

        east, slope_x = physical(0), physical(2)
        product = [a * b for a, b in zip(east, slope_x)]
        north, slope_y = physical(1), physical(3)
        product = [p + a * b for p, a, b in zip(product, north, slope_y)]
        real, imag = real_analysis(product)
        for k in range(9):
            jac[0, k, rows, :] = real[k]
            if imag[k] is not None:
                jac[1, k, rows, :] = imag[k]
    real = [jac[0, k] for k in range(9)]
    imag = [None] + [jac[1, k] for k in range(1, 8)] + [None]
    results = x_forward(real, imag, twiddle, table_ref)
    for half in range(2):
        for group in range(2):
            for j3 in range(3):
                for part in range(2):
                    rows = slice(32 * j3 + 16 * part, 32 * j3 + 16 * part + 16)
                    start = (32 * group + 16 * half) * CHUNK + 2 * j3 + part
                    out_ref[pl.ds(start, 16, stride=CHUNK), :] = results[half][
                        rows, 128 * group : 128 * group + 128
                    ]


def projection_kernel(in_ref, radix_ref, unradix_ref, turn_ref, project_ref, mean_ref, out_ref):
    def rows(part):
        return jnp.concatenate(
            [in_ref[pl.ds(2 * j3 + part, 64, stride=CHUNK), :] for j3 in range(3)], axis=1
        )

    mixed = matmul_deep(radix_ref, split(jnp.concatenate([rows(0), rows(1)], axis=0)))
    c, s = turn_ref[0], turn_ref[1]
    turned = []
    for j3 in range(3):
        lanes = slice(128 * j3, 128 * j3 + 128)
        turned.append(jnp.concatenate(turn_by(mixed[:KAP, lanes], mixed[KAP:, lanes], c, s), axis=1))
    left = split(jnp.concatenate(turned, axis=0))
    out = matmul(left, project_ref, NN)
    first = lax.broadcasted_iota(jnp.int32, (16, 1), 0) == 0
    lane = lax.broadcasted_iota(jnp.int32, (1, 128), 1)
    real, imag = [], []
    for j3 in range(3):
        own = out[64 * j3 : 64 * j3 + 64]
        mean = sum(
            lax.dot_general(
                left[i][64 * j3 : 64 * j3 + 16],
                mean_ref[...],
                (NN, ((), ())),
                preferred_element_type=F32,
            )
            for i in range(2)
        )
        own = jnp.concatenate([own[:16] - jnp.where(first, mean, 0.0), own[16:]], axis=0)
        re, im = turn_by(own[:, :128], own[:, 128:], c, -s)
        if j3 == 0:
            zero_wave = (lax.axis_index("row") == 0) & (lane < 32)
            weight = jnp.where(zero_wave, -0.5, -1.0)
            re, im = re * weight, im * weight
        else:
            re, im = -re, -im
        real.append(re)
        imag.append(im)
    right = jnp.concatenate([jnp.concatenate(real, axis=1), jnp.concatenate(imag, axis=1)], axis=0)
    out = matmul_deep(unradix_ref, split(right))
    for part in range(2):
        for j3 in range(3):
            out_ref[pl.ds(2 * j3 + part, 64, stride=CHUNK), :] = out[
                64 * part : 64 * part + 64, 128 * j3 : 128 * j3 + 128
            ]


def state_update_kernel(
    in_ref, damp_ref, state_ref, start_ref, twiddle_ref, untable_ref, tendency_ref, new_ref, z0, z1, z2
):
    sides = []
    for group in range(2):
        rows = []
        for half in range(2):
            for part in range(2):
                for j3 in range(3):
                    start = (32 * group + 16 * half) * CHUNK + 2 * j3 + part
                    rows.append(in_ref[pl.ds(start, 16, stride=CHUNK), :])
        damp = damp_ref[192 * group : 192 * group + 192, :]
        sides.append(jnp.concatenate(rows, axis=0) + damp)
    z0[...], z1[...], z2[...] = x_inverse(sides[0], sides[1], 1, untable_ref)
    twiddle = twiddle_ref[...]
    for block in range(4):
        rows = slice(8 * block, 8 * block + 8)
        tendency = real_synthesis(*modes_of(z0, z1, z2, 0, rows, twiddle))
        for a in range(16):
            columns = slice(128 * a, 128 * a + 128)
            tendency_ref[0, rows, columns] = tendency[a]
            new_ref[0, rows, columns] = 0.75 * start_ref[0, rows, columns] + 0.25 * (
                state_ref[0, rows, columns] + STEP_SIZE * tendency[a]
            )


VMEM = pl.BlockSpec(memory_space=pltpu.VMEM)
ANY = pl.BlockSpec(memory_space=pl.ANY)
MIB = 1024 * 1024


def call(kernel, outs, operands, scratch=(), fetched=False):
    if fetched:
        scratch_shapes = [pltpu.VMEM(operand.shape, operand.dtype) for operand in operands]
        scratch_shapes.append(pltpu.SemaphoreType.DMA((len(operands),)))
    else:
        scratch_shapes = [pltpu.VMEM(shape, F32) for shape in scratch]
    return pl.pallas_call(
        kernel,
        out_shape=[jax.ShapeDtypeStruct(shape, F32) for shape in outs],
        in_specs=[ANY if fetched else VMEM] * len(operands),
        out_specs=[VMEM] * len(outs),
        scratch_shapes=scratch_shapes,
        compiler_params=pltpu.CompilerParams(vmem_limit_bytes=(60 if fetched else 32) * MIB),
    )(*operands)


def row_exchange(chunks):
    length = chunks.shape[0]
    sent = chunks.reshape(64, 1, 2 * length)
    return lax.all_to_all(sent, "row", split_axis=0, concat_axis=0, tiled=True).reshape(length, 128)


def wide_exchange(chunks):
    length = chunks.shape[0]
    groups = [[(2 * z + core) * 64 + row for z in range(4) for row in range(64)] for core in range(2)]
    sent = chunks.reshape(WIDE, 1, length // 2)
    got = lax.all_to_all(
        sent, ("layer", "row"), split_axis=0, concat_axis=0, tiled=True, axis_index_groups=groups
    )
    return got.reshape(length, 128)


def pair_gather(spectrum):
    pairs = [[2 * z, 2 * z + 1] for z in range(4)]
    return lax.all_gather(spectrum, "layer", axis=0, tiled=False, axis_index_groups=pairs)


def per_device(state, start_state, to_modes, from_modes, deform):
    turn_x = jnp.asarray(x_twiddle())
    forward_x = jnp.asarray(x_forward_table(False))
    forward_apart = jnp.asarray(x_forward_table(True))
    inverse_x = jnp.asarray(x_inverse_table(False))
    inverse_ix = jnp.asarray(x_inverse_table(True))
    radix = jnp.asarray(y_radix_table())
    unradix = jnp.asarray(y_radix_inverse_table())
    turn_y = jnp.asarray(y_twiddle())
    lanes = jnp.asarray(y_lane_table())
    unlanes = jnp.asarray(y_lane_inverse_table())
    project = jnp.asarray(y_projection_table())
    mean = jnp.asarray(y_mean_table())
    facts = jnp.asarray(lane_facts())

    columns, scalars = call(
        state_kernel,
        [(2 * WIDE, 128), (136, 128)],
        [state, turn_x, forward_x, to_modes, from_modes, deform.reshape(1, 8)],
        fetched=True,
    )
    (spectrum,) = call(
        spectrum_kernel, [(WIDE, USED)], [wide_exchange(columns), radix, turn_y, lanes, facts]
    )
    (fields,) = call(
        stream_kernel,
        [(8 * WIDE, 128)],
        [scalars, pair_gather(spectrum), unradix, turn_y, unlanes, facts],
        scratch=[(2 * WIDE, 128)],
    )
    flux, damped = call(
        jacobian_kernel,
        [(64 * CHUNK, 128)] * 2,
        [wide_exchange(fields), turn_x, inverse_ix, forward_apart],
        scratch=[(512, 256)] * 3 + [(2, 9, ROWS, 128)],
    )
    (total,) = call(
        projection_kernel,
        [(64 * CHUNK, 128)],
        [row_exchange(flux), radix, unradix, turn_y, project, mean],
    )
    return tuple(
        call(
            state_update_kernel,
            [(1, ROWS, GRID)] * 2,
            [row_exchange(total), damped, state, start_state, turn_x, inverse_x],
            scratch=[(128, 256)] * 3,
        )
    )


def solution(mesh):
    in_specs = (P("layer", "row", None), P("layer", "row", None), P(), P(), P())
    out_specs = (P("layer", "row", None), P("layer", "row", None))
    return jax.shard_map(
        per_device, mesh=mesh, in_specs=in_specs, out_specs=out_specs, check_vma=False
    )
```

time: 121 us -> 124 us (1.025)
  blocking collectives: 108 us -> 114 us
  local copies, waits for them, and re-layouts: 3.41 us -> 0.1 us
  Pallas kernels: 7.67 us -> 9.02 us
    all_to_all x4, blocking collectives: 85.4 us -> 112 us  [the longest x2 79.3 us: wide_exchange(): lax.all_to_all(sent, ('layer', 'row'), split_axis=0, concat_axis=0, tiled...]
    all_gather x1, blocking collectives: 22.9 us -> 2.13 us  [pair_gather(): lax.all_gather(spectrum, 'layer', axis=0, tiled=False, axis_index_groups=...]
    unnamed x36 -> x30, local copies, waits for them, and re-layouts: 3.41 us -> 0.1 us
    pallas_call x6, Pallas kernels: 7.67 us -> 9.02 us  [call(): pl.pallas_call(kernel, out_shape=[jax.ShapeDtypeStruct(shape, F32) for sh...]
where the time goes in v3:
time: 124 us
  blocking collectives  114 us (92%)
  Pallas kernels  9.02 us (7%)
    all_to_all x2, blocking collectives, wide_exchange(): lax.all_to_all(sent, ('layer', 'row'), split_axis=0, concat_axis=0, tiled...  79.3 us
    all_to_all x2, blocking collectives, row_exchange(): lax.all_to_all(sent, 'row', split_axis=0, concat_axis=0, tiled=True)  32.8 us
    pallas_call x6, Pallas kernels, call(): pl.pallas_call(kernel, out_shape=[jax.ShapeDtypeStruct(shape, F32) for sh...  9.02 us

profile of v3, /device:TPU:8, one launch (start us, length us, event | category | flops | bytes accessed | tf_op | source)
XLA Modules:
  0.0 124.1 jit_solution(3364361039864710717)
XLA Ops:
  0.6 0.0 copy-start.2
  0.6 0.0 copy-start.4
  0.7 0.0 copy-start.11
  0.7 0.0 copy-start.14
  0.7 2.5 %shard_map.185 = (f32[512,128]{1,0:T(8,128)}, f32[136,128]{1,0:T(8,128)}) custom-call(f32[1,32,2048]{2,1,0:T(8,128)} %state_ref.1, f32[32,128]{1,0:T(8,128)} %constant.26.clone.twiddle_hbm.twiddle_ref, bf16[2,2,96,256]{3,2,1,0:T(8,128)(2,1)} %constant.27.clone.table_hbm, f32[8,8]{1,0:T(8,128)} %to_hbm.1, f32[8,8]{1,0:T(8,128)} %from_hbm.1, f32[1,8]{1,0:T(1,128)} %bitcast.19), custom_call_target="tpu_custom_call" | custom-call | tf_op jit(solution)/shard_map/pallas_call | solution.py:603
  3.2 0.0 copy-start.1
  3.2 38.0 %all_to_all.20 = f32[256,1,256]{2,1,0:T(1,128)S(1)} all-to-all(f32[256,1,256]{2,1,0:T(1,128)} %bitcast.18), channel_id=1, replica_groups={{0,1,2,3,4,5,6,7,8,9,10,11,12,13,14,15,16,17,18,19,20,21,22,23,24,25,26..., dimensions={0} | all-to-all | bytes 524288 | tf_op jit(solution)/shard_map/all_to_all | solution.py:623
  41.2 0.0 copy-done.2
  41.2 0.0 copy-done.4
  41.2 0.0 copy-done.11
  41.2 0.5 shard_map.186
  41.7 0.0 copy-start.3
  41.7 0.0 copy-start.13
  41.7 2.1 %all-gather = f32[512,126]{1,0:T(8,128)S(1)} all-gather(f32[256,126]{1,0:T(8,128)S(1)} %shard_map.186), channel_id=2, replica_groups={{0,64},{128,192},{256,320},{384,448},{1,65},{129,193},{257,321},{385,44..., dimensions={0}, use_global_device_ids=true | all-gather | bytes 387072 | tf_op jit(solution)/shard_map/all_gather | solution.py:631
  43.9 0.0 copy-done.1
  43.9 0.0 copy-done.13
  43.9 1.9 %shard_map.187 = f32[2048,128]{1,0:T(8,128)S(1)} custom-call(f32[136,128]{1,0:T(8,128)S(1)} %copy-done.13, f32[2,256,126]{2,1,0:T(8,128)S(1)} %bitcast.12, bf16[128,384]{1,0:T(8,128)(2,1)S(1)} %copy-done.3, f32[2,64,128]{2,1,0:T(8,128)S(1)} %copy-done.2, bf16[2,3,256,256]{3,2,1,0:T(8,128)(2,1)S(1)} %copy-done.1, f32[8,128]{1,0:T(8,128)S(1)} %copy-done.14), custom_call_target="tpu_custom_call" | custom-call | tf_op jit(solution)/shard_map/pallas_call | solution.py:603
  45.8 0.0 copy-start.8
  45.8 0.0 copy-start.9
  45.8 0.0 copy-start.10
  45.8 41.3 %all_to_all.21 = f32[256,1,1024]{2,1,0:T(1,128)S(1)} all-to-all(f32[256,1,1024]{2,1,0:T(1,128)S(1)} %bitcast.11), channel_id=1, replica_groups={{0,1,2,3,4,5,6,7,8,9,10,11,12,13,14,15,16,17,18,19,20,21,22,23,24,25,26..., dimensions={0} | all-to-all | bytes 2097152 | tf_op jit(solution)/shard_map/all_to_all | solution.py:623
  87.1 0.0 copy-done.9
  87.1 2.2 %shard_map.188 = (f32[384,128]{1,0:T(8,128)S(1)}, f32[384,128]{1,0:T(8,128)S(1)}) custom-call(f32[2048,128]{1,0:T(8,128)S(1)} %bitcast.10, f32[32,128]{1,0:T(8,128)S(1)} %copy-done.10, bf16[2,192,256]{2,1,0:T(8,128)(2,1)S(1)} %copy-done.8, bf16[2,2,96,256]{3,2,1,0:T(8,128)(2,1)S(1)} %copy-done.9), custom_call_target="tpu_custom_call" | custom-call | tf_op jit(solution)/shard_map/pallas_call | solution.py:603
  89.3 0.0 copy-start.6
  89.4 0.0 copy-start.12
  89.4 16.8 %all_to_all.22 = f32[64,1,768]{2,1,0:T(1,128)S(1)} all-to-all(f32[64,1,768]{2,1,0:T(1,128)S(1)} %bitcast.17), channel_id=1, replica_groups=mesh['layer'=8,'row'=64] {'row'}, dimensions={0} | all-to-all | bytes 393216 | tf_op jit(solution)/shard_map/all_to_all | solution.py:616
  106.2 0.0 copy-done.12
  106.2 0.7 shard_map.189
  107.0 0.0 copy-start
  107.0 15.9 %all_to_all.23 = f32[64,1,768]{2,1,0:T(1,128)S(1)} all-to-all(f32[64,1,768]{2,1,0:T(1,128)S(1)} %bitcast.15), channel_id=1, replica_groups=mesh['layer'=8,'row'=64] {'row'}, dimensions={0} | all-to-all | bytes 393216 | tf_op jit(solution)/shard_map/all_to_all | solution.py:616
  122.9 0.0 copy-done
  122.9 1.2 shard_map.190
  (9 shorter events, 0.0 us)
Async XLA Ops:
  0.6 40.6 %copy-start.2 = (f32[2,64,128]{2,1,0:T(8,128)S(1)}, f32[2,64,128]{2,1,0:T(8,128)}, u32[]{:S(2)}) copy-start(f32[2,64,128]{2,1,0:T(8,128)} %constant.33.clone.turn_ref) | copy-start | bytes 196612
  0.6 40.6 %copy-start.4 = (bf16[128,384]{1,0:T(8,128)(2,1)S(1)}, bf16[128,384]{1,0:T(8,128)(2,1)}, u32[]{:S(2)}) copy-start(bf16[128,384]{1,0:T(8,128)(2,1)} %constant.31.clone.radix_ref) | copy-start | bytes 294916
  0.7 40.5 %copy-start.11 = (bf16[2,256,128]{2,1,0:T(8,128)(2,1)S(1)}, bf16[2,256,128]{2,1,0:T(8,128)(2,1)}, u32[]{:S(2)}) copy-start(bf16[2,256,128]{2,1,0:T(8,128)(2,1)} %constant.34.clone.lanes_ref) | copy-start | bytes 393220
  0.7 40.5 %copy-start.14 = (f32[8,128]{1,0:T(8,128)S(1)}, f32[8,128]{1,0:T(8,128)}, u32[]{:S(2)}) copy-start(f32[8,128]{1,0:T(8,128)} %constant.38.clone.facts_ref) | copy-start | bytes 12292
  3.2 40.7 %copy-start.1 = (bf16[2,3,256,256]{3,2,1,0:T(8,128)(2,1)S(1)}, bf16[2,3,256,256]{3,2,1,0:T(8,128)(2,1)}, u32[]{:S(2)}) copy-start(bf16[2,3,256,256]{3,2,1,0:T(8,128)(2,1)} %constant.35.clone.unlanes_ref) | copy-start | bytes 2359300
  41.7 2.2 %copy-start.3 = (bf16[128,384]{1,0:T(8,128)(2,1)S(1)}, bf16[128,384]{1,0:T(8,128)(2,1)}, u32[]{:S(2)}) copy-start(bf16[128,384]{1,0:T(8,128)(2,1)} %constant.32.clone.unradix_ref) | copy-start | bytes 294916
  41.7 2.1 %copy-start.13 = (f32[136,128]{1,0:T(8,128)S(1)}, f32[136,128]{1,0:T(8,128)}, u32[]{:S(2)}) copy-start(f32[136,128]{1,0:T(8,128)} %get-tuple-element.6.scalars_ref) | copy-start | bytes 208900
  45.8 41.3 %copy-start.8 = (bf16[2,192,256]{2,1,0:T(8,128)(2,1)S(1)}, bf16[2,192,256]{2,1,0:T(8,128)(2,1)}, u32[]{:S(2)}) copy-start(bf16[2,192,256]{2,1,0:T(8,128)(2,1)} %constant.30.clone.untable_ref) | copy-start | bytes 589828
  45.8 41.3 %copy-start.9 = (bf16[2,2,96,256]{3,2,1,0:T(8,128)(2,1)S(1)}, bf16[2,2,96,256]{3,2,1,0:T(8,128)(2,1)}, u32[]{:S(2)}) copy-start(bf16[2,2,96,256]{3,2,1,0:T(8,128)(2,1)} %constant.28.clone.table_ref) | copy-start | bytes 589828
  45.8 41.3 %copy-start.10 = (f32[32,128]{1,0:T(8,128)S(1)}, f32[32,128]{1,0:T(8,128)}, u32[]{:S(2)}) copy-start(f32[32,128]{1,0:T(8,128)} %constant.26.clone.twiddle_hbm.twiddle_ref) | copy-start | bytes 49156
  89.3 16.9 %copy-start.6 = (bf16[2,256,256]{2,1,0:T(8,128)(2,1)S(1)}, bf16[2,256,256]{2,1,0:T(8,128)(2,1)}, u32[]{:S(2)}) copy-start(bf16[2,256,256]{2,1,0:T(8,128)(2,1)} %constant.36.clone.project_ref) | copy-start | bytes 786436
  89.4 16.9 %copy-start.12 = (bf16[256,256]{1,0:T(8,128)(2,1)S(1)}, bf16[256,256]{1,0:T(8,128)(2,1)}, u32[]{:S(2)}) copy-start(bf16[256,256]{1,0:T(8,128)(2,1)} %constant.37.clone.mean_ref) | copy-start | bytes 393220
  106.2 16.7 %copy-start.5 = (f32[1,32,2048]{2,1,0:T(8,128)S(1)}, f32[1,32,2048]{2,1,0:T(8,128)}, u32[]{:S(2)}) copy-start(f32[1,32,2048]{2,1,0:T(8,128)} %start_ref.1) | copy-start | bytes 786436
  106.2 16.7 %copy-start.7 = (bf16[2,192,256]{2,1,0:T(8,128)(2,1)S(1)}, bf16[2,192,256]{2,1,0:T(8,128)(2,1)}, u32[]{:S(2)}) copy-start(bf16[2,192,256]{2,1,0:T(8,128)(2,1)} %constant.29.clone.untable_ref) | copy-start | bytes 589828
  107.0 15.9 %copy-start = (f32[1,32,2048]{2,1,0:T(8,128)S(1)}, f32[1,32,2048]{2,1,0:T(8,128)}, u32[]{:S(2)}) copy-start(f32[1,32,2048]{2,1,0:T(8,128)} %state_ref.1) | copy-start | bytes 786436

commit v4 on v2

--- a/solution.py
+++ b/solution.py
@@ -75,14 +75,19 @@
     return table.astype(np.float32)
 
 
+def paired(table):
+    high, low = halves(table)
+    return np.concatenate([high, high, low], axis=1)
+
+
 def y_radix_table():
     c, s = turn(np.arange(KAP)[:, None] * np.arange(64)[None, :] + 32 * np.arange(64)[None, :], 64)
-    return halves(np.block([[c, s], [-s, c]]))
+    return paired(np.block([[c, s], [-s, c]]))
 
 
 def y_radix_inverse_table():
     c, s = turn(np.arange(64)[:, None] * np.arange(KAP)[None, :] + 32 * np.arange(64)[:, None], 64)
-    return halves(np.block([[c, -s], [s, c]]))
+    return paired(np.block([[c, -s], [s, c]]))
 
 
 def y_twiddle():
@@ -109,6 +114,17 @@
     return np.stack([np.swapaxes(high, 1, 2), np.swapaxes(low, 1, 2)])
 
 
+def y_projection_table():
+    difference = np.arange(ROWS)[None, :] - np.arange(ROWS)[:, None]
+    c, s = turn(difference[:, :, None] * np.arange(JP)[None, None, :], ROWS)
+    c, s = np.kron(np.eye(4), c.sum(-1)), np.kron(np.eye(4), s.sum(-1))
+    return halves(np.block([[c, s], [-s, c]]))
+
+
+def y_mean_table():
+    return np.kron(np.eye(8), np.ones((ROWS, ROWS))).astype(ml_dtypes.bfloat16)
+
+
 def lane_facts():
     lane = np.arange(SPAN)
     j3 = lane // PIECE
@@ -132,6 +148,16 @@
         return lax.dot_general(a, b, (dims, ((), ())), preferred_element_type=F32)
 
     return one(left[0], right[0]) + (one(left[0], right[1]) + one(left[1], right[0]))
+
+
+def matmul_deep(table, right):
+    depth = right[0].shape[0]
+
+    def one(a, b):
+        return lax.dot_general(a, b, (NN, ((), ())), preferred_element_type=F32)
+
+    both = jnp.concatenate(right, axis=0)
+    return one(table[:, : 2 * depth], both) + one(table[:, 2 * depth :], right[0])
 
 
 NN = ((1,), (0,))
@@ -201,6 +227,25 @@
     return [s[a] + d[a] for a in range(8)] + [s[a] - d[a] for a in range(8)]
 
 
+def regroup(blocks, wanted):
+    block = lax.broadcasted_iota(jnp.int32, (1, 128), 1) // 32
+    turned = [
+        b if b is None or i == 0 else pltpu.roll(b, 32 * i, 1) for i, b in enumerate(blocks)
+    ]
+    results = []
+    for p in wanted:
+        total = None
+        for i in range(4):
+            part = jnp.zeros_like(turned[0]) if turned[i] is None else turned[i]
+            total = part if total is None else jnp.where(block == (p + i) % 4, part, total)
+        results.append(total if p == 0 else pltpu.roll(total, 128 - 32 * p, 1))
+    return results
+
+
+def turn_by(re, im, c, s):
+    return re * c + im * s, im * c - re * s
+
+
 def x_forward(real, imag, twiddle, table):
     pieces = []
     for k in range(9):
@@ -222,32 +267,31 @@
     return results
 
 
-def x_inverse(left, right, fields, table):
-    left = split(left)
-    right = split(right)
-    upper = [table[i][:96] for i in range(2)]
-    lower = [table[i][96:] for i in range(2)]
-    first = matmul([part[:96] for part in left], upper, TN)
-    second = matmul([part[96:] for part in left], lower, TN)
-    rest = matmul(right, [table[i] for i in range(2)], TN)
-    return first, second, rest
+def x_inverse(left, right, table):
+    fields = len(left)
+    upper = [part[:96] for part in left]
+    own = regroup(upper, [0])[0] if fields == 4 else upper[0]
+    first = matmul(split(own), [table[i][:96] for i in range(2)], TN)
+    whole = [table[i] for i in range(2)]
+    sides = [split(jnp.concatenate(side, axis=1) if fields > 1 else side[0]) for side in (left, right)]
+    return first, matmul(sides[0], whole, TN), matmul(sides[1], whole, TN)
 
 
 def modes_of(first, second, rest, field, rows, twiddle):
     real, imag = [], []
+    size = rows.stop - rows.start
+    start = field * 32 + rows.start
+    own = first[start : start + size]
     for k in range(9):
         c, s = twiddle[k : k + 1], twiddle[16 + k : 17 + k]
-        base = field * 128 + rows.start
-        size = rows.stop - rows.start
-        if k in (0, 8):
-            source = first if k == 0 else second
-            z = source[base : base + size]
-        elif k < 4:
-            start = base + 32 * k
-            z = first[start : start + size] + second[start : start + size]
+        start = field * 128 + 32 * (k % 4) + rows.start
+        if k == 0:
+            z = own
+        elif k == 8:
+            z = second[start : start + size] - own
         else:
-            start = base + 32 * (k - 4)
-            z = rest[start : start + size]
+            source = second if k < 4 else rest
+            z = source[start : start + size]
         re, im = z[:, :128], z[:, 128:]
         if k == 0:
             real.append(re)
@@ -262,7 +306,7 @@
     stacked = jnp.concatenate(
         [jnp.concatenate(pieces[0], axis=1), jnp.concatenate(pieces[1], axis=1)], axis=0
     )
-    mixed = matmul([radix[0], radix[1]], split(stacked), NN)
+    mixed = matmul_deep(radix, split(stacked))
     c, s = twiddle[0], twiddle[1]
     windows = []
     for j3 in range(3):
@@ -313,25 +357,12 @@
     right = split(
         jnp.concatenate([jnp.concatenate(real, axis=1), jnp.concatenate(imag, axis=1)], axis=0)
     )
-    out = matmul([radix[0], radix[1]], right, NN)
+    out = matmul_deep(radix, right)
     fields = []
     for field in range(count):
         columns = [slice(128 * (count * j3 + field), 128 * (count * j3 + field) + 128) for j3 in range(3)]
         fields.append([[out[:64, own] for own in columns], [out[64:, own] for own in columns]])
     return fields
-
-
-def stream_function(gathered, to_modes, from_modes, deform, layer, square):
-    weights = [from_modes(layer, m) * (-1.0 / (square + deform(m))) for m in range(8)]
-    total = None
-    for n in range(8):
-        factor = None
-        for m in range(8):
-            term = weights[m] * to_modes(m, n)
-            factor = term if factor is None else factor + term
-        term = factor * gathered(n)
-        total = term if total is None else total + term
-    return total
 
 
 def store_x(out_ref, results):
@@ -378,11 +409,27 @@
     copies = [pltpu.make_async_copy(a, b, sems.at[i]) for i, (a, b) in enumerate(pairs)]
     for copy in copies:
         copy.start()
-    for copy in copies:
-        copy.wait()
+    copies[0].wait()
     x = [state_ref[0, :, 128 * a : 128 * a + 128] for a in range(16)]
     real, imag = real_analysis(x)
+    copies[1].wait()
+    copies[2].wait()
     store_x(out_ref, x_forward(real, imag, twiddle_ref[...], table_ref))
+
+
+def weights_kernel(to_ref, from_ref, deform_ref, facts_ref, out_ref):
+    facts = facts_ref[...]
+    wave_x = x_waves(facts, lax.axis_index("row"))
+    wave_y = y_waves(facts)
+    square = (wave_x * wave_x + wave_y * wave_y)[:, :USED]
+    layer = lax.axis_index("layer")
+    modes = [from_ref[layer, m] * (-1.0 / (square + deform_ref[m])) for m in range(8)]
+    for n in range(8):
+        total = None
+        for m in range(8):
+            term = modes[m] * to_ref[m, n]
+            total = term if total is None else total + term
+        out_ref[n] = total
 
 
 def spectrum_kernel(in_ref, radix_ref, turn_ref, lanes_ref, facts_ref, spec_ref, used_ref):
@@ -393,30 +440,15 @@
 
 
 def stream_kernel(
-    to_ref,
-    from_ref,
-    deform_ref,
-    all_ref,
-    spec_ref,
-    unradix_ref,
-    turn_ref,
-    unlanes_ref,
-    facts_ref,
-    out_ref,
-    stream_ref,
+    weights_ref, all_ref, spec_ref, unradix_ref, turn_ref, unlanes_ref, facts_ref, out_ref, stream_ref
 ):
     facts = facts_ref[...]
     wave_x = x_waves(facts, lax.axis_index("row"))
     wave_y = y_waves(facts)
-    square = (wave_x * wave_x + wave_y * wave_y)[:, :USED]
-    stream = stream_function(
-        lambda n: all_ref[n],
-        lambda m, n: to_ref[m, n],
-        lambda l, m: from_ref[l, m],
-        lambda m: deform_ref[m],
-        lax.axis_index("layer"),
-        square,
-    )
+    stream = None
+    for n in range(8):
+        term = weights_ref[n] * all_ref[n]
+        stream = term if stream is None else stream + term
     stream_ref[:, SPAN - 128 :] = jnp.zeros((KAP, 128), F32)
     stream_ref[:, :USED] = stream
     stream = stream_ref[...]
@@ -428,9 +460,7 @@
 
 def jacobian_kernel(in_ref, twiddle_ref, untable_ref, table_ref, out_ref, z0, z1, z2, jac):
     groups = load_x(in_ref, 4)
-    left = jnp.concatenate(groups[0], axis=1)
-    right = jnp.concatenate(groups[1], axis=1)
-    z0[...], z1[...], z2[...] = x_inverse(left, right, 4, untable_ref)
+    z0[...], z1[...], z2[...] = x_inverse(groups[0], groups[1], untable_ref)
     twiddle = twiddle_ref[...]
     for block in range(4):
         rows = slice(8 * block, 8 * block + 8)
@@ -452,26 +482,63 @@
     store_x(out_ref, x_forward(real, imag, twiddle, table_ref))
 
 
-def tendency_kernel(
-    in_ref, spec_ref, radix_ref, unradix_ref, turn_ref, lanes_ref, unlanes_ref, facts_ref, out_ref
+def projection_kernel(
+    in_ref, spec_ref, radix_ref, unradix_ref, turn_ref, project_ref, mean_ref, unlanes_ref, facts_ref, out_ref
 ):
     facts = facts_ref[...]
-    flux = y_forward(load_pieces(in_ref), radix_ref, turn_ref, lanes_ref, facts)
     wave_x = x_waves(facts, lax.axis_index("row"))
     wave_y = y_waves(facts)
     ratio = (wave_x * wave_x + wave_y * wave_y) * (1.0 / (KCUT * KCUT))
     ratio = ratio * ratio
-    damping = HYPER_RATE * (ratio * ratio)
-    weight = jnp.where(wave_x == 0.0, 0.5, 1.0)
-    total = -(flux + damping * spec_ref[...]) * weight
-    store_pieces(out_ref, y_inverse([total], unradix_ref, turn_ref, unlanes_ref))
+    damped = split((HYPER_RATE * (ratio * ratio)) * spec_ref[...])
+
+    pieces = load_pieces(in_ref)
+    stacked = [jnp.concatenate(pieces[part], axis=1) for part in range(2)]
+    mixed = matmul_deep(radix_ref, split(jnp.concatenate(stacked, axis=0)))
+    c, s = turn_ref[0], turn_ref[1]
+    turned = []
+    for j3 in range(3):
+        lanes = slice(128 * j3, 128 * j3 + 128)
+        turned.append(jnp.concatenate(turn_by(mixed[:KAP, lanes], mixed[KAP:, lanes], c, s), axis=1))
+    left = split(jnp.concatenate(turned, axis=0))
+    out = matmul(left, project_ref, NN)
+    first = lax.broadcasted_iota(jnp.int32, (16, 1), 0) == 0
+    lane = lax.broadcasted_iota(jnp.int32, (1, 128), 1)
+    real, imag = [], []
+    for j3 in range(3):
+        own = out[64 * j3 : 64 * j3 + 64]
+        mean = sum(
+            lax.dot_general(
+                left[i][64 * j3 : 64 * j3 + 16],
+                mean_ref[...],
+                (NN, ((), ())),
+                preferred_element_type=F32,
+            )
+            for i in range(2)
+        )
+        own = jnp.concatenate([own[:16] - jnp.where(first, mean, 0.0), own[16:]], axis=0)
+        window = [part[:, 128 * j3 : 128 * j3 + 256] for part in damped]
+        own = own + matmul(window, [unlanes_ref[i, j3] for i in range(2)], NN)
+        re, im = turn_by(own[:, :128], own[:, 128:], c, -s)
+        if j3 == 0:
+            zero_wave = (lax.axis_index("row") == 0) & (lane < 32)
+            weight = jnp.where(zero_wave, -0.5, -1.0)
+            re, im = re * weight, im * weight
+        else:
+            re, im = -re, -im
+        real.append(re)
+        imag.append(im)
+    right = jnp.concatenate([jnp.concatenate(real, axis=1), jnp.concatenate(imag, axis=1)], axis=0)
+    out = matmul_deep(unradix_ref, split(right))
+    columns = [slice(128 * j3, 128 * j3 + 128) for j3 in range(3)]
+    store_pieces(out_ref, [[[out[:64, own] for own in columns], [out[64:, own] for own in columns]]])
 
 
 def state_update_kernel(
     in_ref, state_ref, start_ref, twiddle_ref, untable_ref, tendency_ref, new_ref, z0, z1, z2
 ):
     groups = load_x(in_ref, 1)
-    z0[...], z1[...], z2[...] = x_inverse(groups[0][0], groups[1][0], 1, untable_ref)
+    z0[...], z1[...], z2[...] = x_inverse(groups[0], groups[1], untable_ref)
     twiddle = twiddle_ref[...]
     for block in range(4):
         rows = slice(8 * block, 8 * block + 8)
@@ -486,12 +553,12 @@
 
 VMEM = pl.BlockSpec(memory_space=pltpu.VMEM)
 SMEM = pl.BlockSpec(memory_space=pltpu.SMEM)
-ANY = pl.BlockSpec(memory_space=pl.ANY)
-
-
-def call(kernel, outs, operands, scalars=0, scratch=(), fetched=False):
+HBM = pl.BlockSpec(memory_space=pltpu.HBM)
+
+
+def call(kernel, outs, operands, scalars=0, scratch=(), fetched=False, cost=None):
     if fetched:
-        in_specs = [ANY] * len(operands)
+        in_specs = [HBM] * len(operands)
         scratch_shapes = [pltpu.VMEM(operand.shape, operand.dtype) for operand in operands]
         scratch_shapes.append(pltpu.SemaphoreType.DMA((len(operands),)))
     else:
@@ -503,7 +570,8 @@
         in_specs=in_specs,
         out_specs=[VMEM] * len(outs),
         scratch_shapes=scratch_shapes,
-        compiler_params=pltpu.CompilerParams(vmem_limit_bytes=40 * 1024 * 1024),
+        compiler_params=pltpu.CompilerParams(vmem_limit_bytes=32 * 1024 * 1024),
+        cost_estimate=cost,
     )(*operands)
 
 
@@ -524,6 +592,8 @@
     turn_y = jnp.asarray(y_twiddle())
     lanes = jnp.asarray(y_lane_table())
     unlanes = jnp.asarray(y_lane_inverse_table())
+    project = jnp.asarray(y_projection_table())
+    mean = jnp.asarray(y_mean_table())
     facts = jnp.asarray(lane_facts())
 
     one, four = (64 * CHUNK, 128), (256 * CHUNK, 128)
@@ -532,12 +602,18 @@
     spectrum, used = call(
         spectrum_kernel, [(KAP, SPAN), (KAP, USED)], [columns, radix, turn_y, lanes, facts]
     )
+    (weights,) = call(
+        weights_kernel,
+        [(8, KAP, USED)],
+        [to_modes, from_modes, deform, facts],
+        scalars=3,
+        cost=pl.CostEstimate(flops=8_000_000, bytes_accessed=2_000_000, transcendentals=0),
+    )
     gathered = lax.all_gather(used, "layer", axis=0, tiled=False)
     (fields,) = call(
         stream_kernel,
         [four],
-        [to_modes, from_modes, deform, gathered, spectrum, unradix, turn_y, unlanes, facts],
-        scalars=3,
+        [weights, gathered, spectrum, unradix, turn_y, unlanes, facts],
         scratch=[(KAP, SPAN)],
     )
     fields = exchange(fields, devices)
@@ -545,11 +621,13 @@
         jacobian_kernel,
         [one],
         [fields, turn_x, inverse_ix, forward_x],
-        scratch=[(512, 256)] * 3 + [(2, 9, ROWS, 128)],
+        scratch=[(128, 256), (512, 256), (512, 256), (2, 9, ROWS, 128)],
     )
     flux = exchange(flux, devices)
     (total,) = call(
-        tendency_kernel, [one], [flux, spectrum, radix, unradix, turn_y, lanes, unlanes, facts]
+        projection_kernel,
+        [one],
+        [flux, spectrum, radix, unradix, turn_y, project, mean, unlanes, facts],
     )
     total = exchange(total, devices)
     return tuple(

time: 121 us -> 119 us (0.983)
  blocking collectives: 108 us -> 85.2 us
  starting transfers between devices: 0 us -> 12.5 us
  waiting for transfers between devices: 0 us -> 9.58 us
    all_to_all x4 -> x3, blocking collectives: 85.4 us -> 62.3 us  [exchange(): lax.all_to_all(sent, 'row', split_axis=0, concat_axis=0, tiled=True)]
    all_to_all x0 -> x1, starting transfers between devices: none -> 12.5 us  [exchange(): lax.all_to_all(sent, 'row', split_axis=0, concat_axis=0, tiled=True)]
    all_to_all x0 -> x1, waiting for transfers between devices: none -> 9.58 us  [exchange(): lax.all_to_all(sent, 'row', split_axis=0, concat_axis=0, tiled=True)]
    unnamed x36 -> x38, local copies, waits for them, and re-layouts: 3.41 us -> 2.7 us
    pallas_call x6 -> x7, Pallas kernels: 7.67 us -> 7.8 us  [call(): pl.pallas_call(kernel, out_shape=[jax.ShapeDtypeStruct(shape, F32) for sh...]
  transfers between devices with their start and end apart: 0 -> 1, of which waited for: 0 -> 1; matrix products, arithmetic and copies ran while one was open for 0% -> 0% of each run, Pallas kernels for 0% -> 1%
where the time goes in v4:
time: 119 us
  blocking collectives  85.2 us (72%)
  starting transfers between devices  12.5 us (11%)
  waiting for transfers between devices  9.58 us (8%)
  Pallas kernels  7.8 us (7%)
  local copies, waits for them, and re-layouts  2.7 us (2%)
    all_to_all x3, blocking collectives, exchange(): lax.all_to_all(sent, 'row', split_axis=0, concat_axis=0, tiled=True)  62.3 us
    all_gather x1, blocking collectives, per_device(): gathered = lax.all_gather(used, 'layer', axis=0, tiled=False)  22.9 us
    all_to_all x1, starting transfers between devices, exchange(): lax.all_to_all(sent, 'row', split_axis=0, concat_axis=0, tiled=True)  12.5 us
    all_to_all x1, waiting for transfers between devices, exchange(): lax.all_to_all(sent, 'row', split_axis=0, concat_axis=0, tiled=True)  9.58 us
    pallas_call x7, Pallas kernels, call(): pl.pallas_call(kernel, out_shape=[jax.ShapeDtypeStruct(shape, F32) for sh...  7.8 us
    unnamed x38, local copies, waits for them, and re-layouts  2.7 us
  transfers between devices with their start and end apart: 1, of which 1 were waited for; matrix products, arithmetic and copies ran while one was open for 0% of the time, Pallas kernels for 1%

profile of v4, /device:TPU:8, one launch (start us, length us, event | category | flops | bytes accessed | tf_op | source)
XLA Modules:
  0.0 118.6 jit_solution(8465074578970043024)
XLA Ops:
  0.6 0.0 copy-start.14
  0.6 0.7 copy-done.14
  1.4 0.9 copy-done.1
  2.3 0.9 copy-done.3
  3.3 1.2 %shard_map.177 = f32[384,128]{1,0:T(8,128)} custom-call(f32[1,32,2048]{2,1,0:T(8,128)S(1)} %copy-done.1, f32[32,128]{1,0:T(8,128)S(1)} %copy-done.14, bf16[2,2,128,256]{3,2,1,0:T(8,128)(2,1)S(1)} %copy-done.3), custom_call_target="tpu_custom_call" | custom-call | tf_op jit(solution)/shard_map/pallas_call | solution.py:567
  4.5 0.0 copy-start.5
  4.5 12.5 %all-to-all-start = ((f32[64,1,768]{2,1,0:T(1,128)}), f32[64,1,768]{2,1,0:T(1,128)S(1)}, u32[]{:S(2)}, u32[]{:S(2)}) async-start(f32[64,1,768]{2,1,0:T(1,128)} %bitcast), calls=%async_computation | async-start | bytes 393216 | tf_op jit(solution)/shard_map/all_to_all | solution.py:581
  17.1 0.0 copy-start.6
  17.1 0.0 copy-start.7
  17.1 1.4 %shard_map.176.weights_ref = f32[8,64,504]{2,1,0:T(8,128)S(1)} custom-call(f32[8,8]{1,0:T(8,128)S(1)} %copy-done.16, f32[8,8]{1,0:T(8,128)S(1)} %copy-done.17, f32[8]{0:T(128)S(1)} %copy-done.18, f32[8,512]{1,0:T(8,128)S(1)} %copy-done.9), custom_call_target="tpu_custom_call" | custom-call | flops 8000000 | bytes 2000000 | tf_op jit(solution)/shard_map/pallas_call | solution.py:567
  18.5 9.6 %all-to-all-done = f32[64,1,768]{2,1,0:T(1,128)S(1)} async-done(((f32[64,1,768]{2,1,0:T(1,128)}), f32[64,1,768]{2,1,0:T(1,128)S(1)}, u32[]{:S(2)}, u32[]{:S(2)}) %all-to-all-start) | async-done | bytes 196640 | tf_op jit(solution)/shard_map/all_to_all | solution.py:581
  28.0 0.0 copy-done.5
  28.0 0.5 shard_map.178
  28.6 0.0 copy-start
  28.6 0.0 copy-start.8
  28.6 22.9 %all-gather = f32[512,504]{1,0:T(8,128)S(1)} all-gather(f32[64,504]{1,0:T(8,128)S(1)} %get-tuple-element.4), channel_id=2, replica_groups=mesh['layer'=8,'row'=64] {'layer'}, dimensions={0}, use_global_device_ids=true | all-gather | bytes 1161216 | tf_op jit(solution)/shard_map/all_gather | solution.py:612
  51.5 0.0 copy-done
  51.5 1.1 shard_map.179
  52.7 0.0 copy-start.4
  52.7 0.0 copy-start.13
  52.7 28.4 %all_to_all.20 = f32[64,1,3072]{2,1,0:T(1,128)S(1)} all-to-all(f32[64,1,3072]{2,1,0:T(1,128)S(1)} %bitcast.11), channel_id=1, replica_groups=mesh['layer'=8,'row'=64] {'row'}, dimensions={0} | all-to-all | bytes 1572864 | tf_op jit(solution)/shard_map/all_to_all | solution.py:581
  81.1 0.0 copy-done.13
  81.1 1.4 %shard_map.180 = f32[384,128]{1,0:T(8,128)S(1)} custom-call(f32[1536,128]{1,0:T(8,128)S(1)} %bitcast.10, f32[32,128]{1,0:T(8,128)S(1)} %copy-done.14, bf16[2,192,256]{2,1,0:T(8,128)(2,1)S(1)} %copy-done.13, bf16[2,2,128,256]{3,2,1,0:T(8,128)(2,1)S(1)} %copy-done.4), custom_call_target="tpu_custom_call" | custom-call | tf_op jit(solution)/shard_map/pallas_call | solution.py:567
  82.5 0.0 copy-start.11
  82.5 0.0 copy-start.15
  82.5 18.0 %all_to_all.21 = f32[64,1,768]{2,1,0:T(1,128)S(1)} all-to-all(f32[64,1,768]{2,1,0:T(1,128)S(1)} %bitcast.14), channel_id=1, replica_groups=mesh['layer'=8,'row'=64] {'row'}, dimensions={0} | all-to-all | bytes 393216 | tf_op jit(solution)/shard_map/all_to_all | solution.py:581
  100.5 0.0 copy-done.15
  100.5 1.0 shard_map.181
  101.5 0.0 copy-start.2
  101.5 15.9 %all_to_all.22 = f32[64,1,768]{2,1,0:T(1,128)S(1)} all-to-all(f32[64,1,768]{2,1,0:T(1,128)S(1)} %bitcast.16), channel_id=1, replica_groups=mesh['layer'=8,'row'=64] {'row'}, dimensions={0} | all-to-all | bytes 393216 | tf_op jit(solution)/shard_map/all_to_all | solution.py:581
  117.4 0.0 copy-done.12
  117.4 1.2 %shard_map.182 = (f32[1,32,2048]{2,1,0:T(8,128)}, f32[1,32,2048]{2,1,0:T(8,128)}) custom-call(f32[384,128]{1,0:T(8,128)S(1)} %bitcast.13, f32[1,32,2048]{2,1,0:T(8,128)S(1)} %copy-done.2, f32[1,32,2048]{2,1,0:T(8,128)S(1)} %copy-done.10, f32[32,128]{1,0:T(8,128)S(1)} %copy-done.14, bf16[2,192,256]{2,1,0:T(8,128)(2,1)S(1)} %copy-done.12), custom_call_target="tpu_custom_call" | custom-call | tf_op jit(solution)/shard_map/pallas_call | solution.py:567
  (19 shorter events, 0.0 us)
Async XLA Ops:
  0.6 0.7 copy-start.14
  1.4 0.9 copy-start.1
  2.3 0.9 copy-start.3
  3.3 13.8 %copy-start.9 = (f32[8,512]{1,0:T(8,128)S(1)}, f32[8,512]{1,0:T(8,128)}, u32[]{:S(2)}) copy-start(f32[8,512]{1,0:T(8,128)} %constant.35.clone.facts_ref) | copy-start | bytes 49156
  3.3 13.8 %copy-start.16 = (f32[8,8]{1,0:T(8,128)S(1)}, f32[8,8]{1,0:T(8,128)}, u32[]{:S(2)}) copy-start(f32[8,8]{1,0:T(8,128)} %to_ref.1) | copy-start | bytes 772
  3.3 13.8 %copy-start.17 = (f32[8,8]{1,0:T(8,128)S(1)}, f32[8,8]{1,0:T(8,128)}, u32[]{:S(2)}) copy-start(f32[8,8]{1,0:T(8,128)} %from_ref.1) | copy-start | bytes 772
  3.3 13.8 %copy-start.18 = (f32[8]{0:T(128)S(1)}, f32[8]{0:T(128)}, u32[]{:S(2)}) copy-start(f32[8]{0:T(128)} %deform_ref.1) | copy-start | bytes 100
  4.5 23.6 %copy-start.5 = (bf16[2,3,256,256]{3,2,1,0:T(8,128)(2,1)S(1)}, bf16[2,3,256,256]{3,2,1,0:T(8,128)(2,1)}, u32[]{:S(2)}) copy-start(bf16[2,3,256,256]{3,2,1,0:T(8,128)(2,1)} %constant.31.clone.lanes_ref) | copy-start | bytes 2359300
  4.5 23.5 %all-to-all-start = ((f32[64,1,768]{2,1,0:T(1,128)}), f32[64,1,768]{2,1,0:T(1,128)S(1)}, u32[]{:S(2)}, u32[]{:S(2)}) async-start(f32[64,1,768]{2,1,0:T(1,128)} %bitcast), calls=%async_computation | async-start | bytes 393216 | tf_op jit(solution)/shard_map/all_to_all | solution.py:581
  17.1 11.0 %copy-start.6 = (f32[2,64,128]{2,1,0:T(8,128)S(1)}, f32[2,64,128]{2,1,0:T(8,128)}, u32[]{:S(2)}) copy-start(f32[2,64,128]{2,1,0:T(8,128)} %constant.30.clone.turn_ref) | copy-start | bytes 196612
  17.1 11.0 %copy-start.7 = (bf16[128,384]{1,0:T(8,128)(2,1)S(1)}, bf16[128,384]{1,0:T(8,128)(2,1)}, u32[]{:S(2)}) copy-start(bf16[128,384]{1,0:T(8,128)(2,1)} %constant.28.clone.radix_ref) | copy-start | bytes 294916
  28.6 23.0 %copy-start = (bf16[2,3,256,256]{3,2,1,0:T(8,128)(2,1)S(1)}, bf16[2,3,256,256]{3,2,1,0:T(8,128)(2,1)}, u32[]{:S(2)}) copy-start(bf16[2,3,256,256]{3,2,1,0:T(8,128)(2,1)} %constant.32.clone.unlanes_ref) | copy-start | bytes 2359300
  28.6 22.9 %copy-start.8 = (bf16[128,384]{1,0:T(8,128)(2,1)S(1)}, bf16[128,384]{1,0:T(8,128)(2,1)}, u32[]{:S(2)}) copy-start(bf16[128,384]{1,0:T(8,128)(2,1)} %constant.29.clone.unradix_ref) | copy-start | bytes 294916
  52.7 28.4 %copy-start.4 = (bf16[2,2,128,256]{3,2,1,0:T(8,128)(2,1)S(1)}, bf16[2,2,128,256]{3,2,1,0:T(8,128)(2,1)}, u32[]{:S(2)}) copy-start(bf16[2,2,128,256]{3,2,1,0:T(8,128)(2,1)} %constant.25.clone.table_hbm.table_ref) | copy-start | bytes 786436
  52.7 28.4 %copy-start.13 = (bf16[2,192,256]{2,1,0:T(8,128)(2,1)S(1)}, bf16[2,192,256]{2,1,0:T(8,128)(2,1)}, u32[]{:S(2)}) copy-start(bf16[2,192,256]{2,1,0:T(8,128)(2,1)} %constant.27.clone.untable_ref) | copy-start | bytes 589828
  82.5 18.0 %copy-start.11 = (bf16[2,256,256]{2,1,0:T(8,128)(2,1)S(1)}, bf16[2,256,256]{2,1,0:T(8,128)(2,1)}, u32[]{:S(2)}) copy-start(bf16[2,256,256]{2,1,0:T(8,128)(2,1)} %constant.33.clone.project_ref) | copy-start | bytes 786436
  82.5 18.0 %copy-start.15 = (bf16[256,256]{1,0:T(8,128)(2,1)S(1)}, bf16[256,256]{1,0:T(8,128)(2,1)}, u32[]{:S(2)}) copy-start(bf16[256,256]{1,0:T(8,128)(2,1)} %constant.34.clone.mean_ref) | copy-start | bytes 393220
  100.5 16.9 %copy-start.10 = (f32[1,32,2048]{2,1,0:T(8,128)S(1)}, f32[1,32,2048]{2,1,0:T(8,128)}, u32[]{:S(2)}) copy-start(f32[1,32,2048]{2,1,0:T(8,128)} %start_ref.1) | copy-start | bytes 786436
  100.5 16.9 %copy-start.12 = (bf16[2,192,256]{2,1,0:T(8,128)(2,1)S(1)}, bf16[2,192,256]{2,1,0:T(8,128)(2,1)}, u32[]{:S(2)}) copy-start(bf16[2,192,256]{2,1,0:T(8,128)(2,1)} %constant.26.clone.untable_ref) | copy-start | bytes 589828
  101.5 15.9 %copy-start.2 = (f32[1,32,2048]{2,1,0:T(8,128)S(1)}, f32[1,32,2048]{2,1,0:T(8,128)}, u32[]{:S(2)}) copy-start(f32[1,32,2048]{2,1,0:T(8,128)} %state_ref.1) | copy-start | bytes 786436

commit v5 on v4

--- a/solution.py
+++ b/solution.py
@@ -365,8 +365,8 @@
     return fields
 
 
-def store_x(out_ref, results):
-    for half in range(2):
+def store_x(out_ref, results, halves_done=(0, 1)):
+    for half in halves_done:
         for group in range(2):
             block = results[half][:, 128 * group : 128 * group + 128]
             for tau in range(16):
@@ -404,7 +404,9 @@
     return groups
 
 
-def state_kernel(state_hbm, twiddle_hbm, table_hbm, out_ref, state_ref, twiddle_ref, table_ref, sems):
+def state_kernel(
+    state_hbm, twiddle_hbm, table_hbm, out_hbm, state_ref, twiddle_ref, table_ref, out_ref, sems
+):
     pairs = ((state_hbm, state_ref), (twiddle_hbm, twiddle_ref), (table_hbm, table_ref))
     copies = [pltpu.make_async_copy(a, b, sems.at[i]) for i, (a, b) in enumerate(pairs)]
     for copy in copies:
@@ -414,7 +416,17 @@
     real, imag = real_analysis(x)
     copies[1].wait()
     copies[2].wait()
-    store_x(out_ref, x_forward(real, imag, twiddle_ref[...], table_ref))
+    results = x_forward(real, imag, twiddle_ref[...], table_ref)
+    sends = []
+    for half in range(2):
+        store_x(out_ref, results, (half,))
+        for group in range(2):
+            rows = pl.ds((32 * group + 16 * half) * CHUNK, 16 * CHUNK)
+            sem = sems.at[3 + 2 * half + group]
+            sends.append(pltpu.make_async_copy(out_ref.at[rows], out_hbm.at[rows], sem))
+            sends[-1].start()
+    for send in sends:
+        send.wait()
 
 
 def weights_kernel(to_ref, from_ref, deform_ref, facts_ref, out_ref):
@@ -535,11 +547,24 @@
 
 
 def state_update_kernel(
-    in_ref, state_ref, start_ref, twiddle_ref, untable_ref, tendency_ref, new_ref, z0, z1, z2
+    in_ref,
+    state_ref,
+    start_ref,
+    twiddle_ref,
+    untable_ref,
+    tendency_hbm,
+    new_hbm,
+    z0,
+    z1,
+    z2,
+    tendency_ref,
+    new_ref,
+    sems,
 ):
     groups = load_x(in_ref, 1)
     z0[...], z1[...], z2[...] = x_inverse(groups[0], groups[1], untable_ref)
     twiddle = twiddle_ref[...]
+    sends = []
     for block in range(4):
         rows = slice(8 * block, 8 * block + 8)
         tendency = real_synthesis(*modes_of(z0, z1, z2, 0, rows, twiddle))
@@ -549,28 +574,33 @@
             new_ref[0, rows, columns] = 0.75 * start_ref[0, rows, columns] + 0.25 * (
                 state_ref[0, rows, columns] + STEP_SIZE * tendency[a]
             )
+        for i, (near, far) in enumerate(((tendency_ref, tendency_hbm), (new_ref, new_hbm))):
+            own = (slice(None), pl.ds(8 * block, 8))
+            sends.append(pltpu.make_async_copy(near.at[own], far.at[own], sems.at[2 * block + i]))
+            sends[-1].start()
+    for send in sends:
+        send.wait()
 
 
 VMEM = pl.BlockSpec(memory_space=pltpu.VMEM)
 SMEM = pl.BlockSpec(memory_space=pltpu.SMEM)
-HBM = pl.BlockSpec(memory_space=pltpu.HBM)
-
-
-def call(kernel, outs, operands, scalars=0, scratch=(), fetched=False, cost=None):
-    if fetched:
-        in_specs = [HBM] * len(operands)
-        scratch_shapes = [pltpu.VMEM(operand.shape, operand.dtype) for operand in operands]
-        scratch_shapes.append(pltpu.SemaphoreType.DMA((len(operands),)))
-    else:
-        in_specs = [SMEM] * scalars + [VMEM] * (len(operands) - scalars)
-        scratch_shapes = [pltpu.VMEM(shape, F32) for shape in scratch]
+ANY = pl.BlockSpec(memory_space=pl.ANY)
+MIB = 1024 * 1024
+
+
+def call(kernel, outs, operands, scalars=0, scratch=(), far_in=False, far_out=False, copies=0, cost=None):
+    scratch_shapes = [pltpu.VMEM(operand.shape, operand.dtype) for operand in operands] if far_in else []
+    scratch_shapes += [pltpu.VMEM(shape, F32) for shape in scratch]
+    scratch_shapes += [pltpu.VMEM(shape, F32) for shape in outs] if far_out else []
+    scratch_shapes += [pltpu.SemaphoreType.DMA((copies,))] if copies else []
+    near = [SMEM] * scalars + [VMEM] * (len(operands) - scalars)
     return pl.pallas_call(
         kernel,
         out_shape=[jax.ShapeDtypeStruct(shape, F32) for shape in outs],
-        in_specs=in_specs,
-        out_specs=[VMEM] * len(outs),
+        in_specs=[ANY] * len(operands) if far_in else near,
+        out_specs=[ANY if far_out else VMEM] * len(outs),
         scratch_shapes=scratch_shapes,
-        compiler_params=pltpu.CompilerParams(vmem_limit_bytes=32 * 1024 * 1024),
+        compiler_params=pltpu.CompilerParams(vmem_limit_bytes=(60 if far_in else 32) * MIB),
         cost_estimate=cost,
     )(*operands)
 
@@ -597,7 +627,7 @@
     facts = jnp.asarray(lane_facts())
 
     one, four = (64 * CHUNK, 128), (256 * CHUNK, 128)
-    (columns,) = call(state_kernel, [one], [state, turn_x, forward_x], fetched=True)
+    (columns,) = call(state_kernel, [one], [state, turn_x, forward_x], far_in=True, far_out=True, copies=7)
     columns = exchange(columns, devices)
     spectrum, used = call(
         spectrum_kernel, [(KAP, SPAN), (KAP, USED)], [columns, radix, turn_y, lanes, facts]
@@ -636,6 +666,8 @@
             [(1, ROWS, GRID)] * 2,
             [total, state, start_state, turn_x, inverse_x],
             scratch=[(128, 256)] * 3,
+            far_out=True,
+            copies=8,
         )
     )
 

time: 119 us -> 117 us (0.983)
  local copies, waits for them, and re-layouts: 2.7 us -> 0.1 us
    unnamed x38 -> x34, local copies, waits for them, and re-layouts: 2.7 us -> 0.1 us
where the time goes in v5:
time: 117 us
  blocking collectives  85.2 us (73%)
  starting transfers between devices  12.5 us (11%)
  waiting for transfers between devices  9.59 us (8%)
  Pallas kernels  8.78 us (8%)
    all_to_all x3, blocking collectives, exchange(): lax.all_to_all(sent, 'row', split_axis=0, concat_axis=0, tiled=True)  62.3 us
    all_gather x1, blocking collectives, per_device(): gathered = lax.all_gather(used, 'layer', axis=0, tiled=False)  22.9 us
    all_to_all x1, starting transfers between devices, exchange(): lax.all_to_all(sent, 'row', split_axis=0, concat_axis=0, tiled=True)  12.5 us
    all_to_all x1, waiting for transfers between devices, exchange(): lax.all_to_all(sent, 'row', split_axis=0, concat_axis=0, tiled=True)  9.59 us
    pallas_call x7, Pallas kernels, call(): pl.pallas_call(kernel, out_shape=[jax.ShapeDtypeStruct(shape, F32) for sh...  8.78 us
  transfers between devices with their start and end apart: 1, of which 1 were waited for; matrix products, arithmetic and copies ran while one was open for 0% of the time, Pallas kernels for 1%

profile of v5, /device:TPU:8, one launch (start us, length us, event | category | flops | bytes accessed | tf_op | source)
XLA Modules:
  0.0 117.0 jit_solution(9339926371578643721)
XLA Ops:
  0.6 0.0 copy-start.7
  0.6 0.0 copy-start.14
  0.7 0.0 copy-start.15
  0.7 0.0 copy-start.16
  0.7 2.2 %shard_map.177 = f32[384,128]{1,0:T(8,128)} custom-call(f32[1,32,2048]{2,1,0:T(8,128)} %state_ref.1, f32[32,128]{1,0:T(8,128)} %constant.24.clone.twiddle_hbm.twiddle_ref, bf16[2,2,128,256]{3,2,1,0:T(8,128)(2,1)} %constant.25.clone.table_hbm.table_ref), custom_call_target="tpu_custom_call" | custom-call | tf_op jit(solution)/shard_map/pallas_call | solution.py:597
  2.9 0.0 copy-start.3
  2.9 12.5 %all-to-all-start = ((f32[64,1,768]{2,1,0:T(1,128)}), f32[64,1,768]{2,1,0:T(1,128)S(1)}, u32[]{:S(2)}, u32[]{:S(2)}) async-start(f32[64,1,768]{2,1,0:T(1,128)} %bitcast.17), calls=%async_computation | async-start | bytes 393216 | tf_op jit(solution)/shard_map/all_to_all | solution.py:611
  15.4 0.0 copy-done.7
  15.4 0.0 copy-start.4
  15.5 0.0 copy-start.5
  15.5 1.4 %shard_map.176.weights_ref = f32[8,64,504]{2,1,0:T(8,128)S(1)} custom-call(f32[8,8]{1,0:T(8,128)S(1)} %copy-done.14, f32[8,8]{1,0:T(8,128)S(1)} %copy-done.15, f32[8]{0:T(128)S(1)} %copy-done.16, f32[8,512]{1,0:T(8,128)S(1)} %copy-done.7), custom_call_target="tpu_custom_call" | custom-call | flops 8000000 | bytes 2000000 | tf_op jit(solution)/shard_map/pallas_call | solution.py:597
  16.8 9.6 %all-to-all-done = f32[64,1,768]{2,1,0:T(1,128)S(1)} async-done(((f32[64,1,768]{2,1,0:T(1,128)}), f32[64,1,768]{2,1,0:T(1,128)S(1)}, u32[]{:S(2)}, u32[]{:S(2)}) %all-to-all-start) | async-done | bytes 196640 | tf_op jit(solution)/shard_map/all_to_all | solution.py:611
  26.4 0.0 copy-done.5
  26.4 0.5 shard_map.178
  27.0 0.0 copy-start
  27.0 0.0 copy-start.6
  27.0 22.9 %all-gather = f32[512,504]{1,0:T(8,128)S(1)} all-gather(f32[64,504]{1,0:T(8,128)S(1)} %get-tuple-element.4), channel_id=2, replica_groups=mesh['layer'=8,'row'=64] {'layer'}, dimensions={0}, use_global_device_ids=true | all-gather | bytes 1161216 | tf_op jit(solution)/shard_map/all_gather | solution.py:642
  49.9 0.0 copy-done
  49.9 1.1 shard_map.179
  51.0 0.0 copy-start.2
  51.0 0.0 copy-start.11
  51.0 0.0 copy-start.12
  51.1 28.4 %all_to_all.20 = f32[64,1,3072]{2,1,0:T(1,128)S(1)} all-to-all(f32[64,1,3072]{2,1,0:T(1,128)S(1)} %bitcast.11), channel_id=1, replica_groups=mesh['layer'=8,'row'=64] {'row'}, dimensions={0} | all-to-all | bytes 1572864 | tf_op jit(solution)/shard_map/all_to_all | solution.py:611
  79.5 1.4 %shard_map.180 = f32[384,128]{1,0:T(8,128)S(1)} custom-call(f32[1536,128]{1,0:T(8,128)S(1)} %bitcast.10, f32[32,128]{1,0:T(8,128)S(1)} %copy-done.12, bf16[2,192,256]{2,1,0:T(8,128)(2,1)S(1)} %copy-done.11, bf16[2,2,128,256]{3,2,1,0:T(8,128)(2,1)S(1)} %copy-done.2), custom_call_target="tpu_custom_call" | custom-call | tf_op jit(solution)/shard_map/pallas_call | solution.py:597
  80.9 0.0 copy-start.9
  80.9 0.0 copy-start.13
  80.9 18.0 %all_to_all.21 = f32[64,1,768]{2,1,0:T(1,128)S(1)} all-to-all(f32[64,1,768]{2,1,0:T(1,128)S(1)} %bitcast.14), channel_id=1, replica_groups=mesh['layer'=8,'row'=64] {'row'}, dimensions={0} | all-to-all | bytes 393216 | tf_op jit(solution)/shard_map/all_to_all | solution.py:611
  98.9 1.0 shard_map.181
  99.8 0.0 copy-start.1
  99.9 15.9 %all_to_all.22 = f32[64,1,768]{2,1,0:T(1,128)S(1)} all-to-all(f32[64,1,768]{2,1,0:T(1,128)S(1)} %bitcast.16), channel_id=1, replica_groups=mesh['layer'=8,'row'=64] {'row'}, dimensions={0} | all-to-all | bytes 393216 | tf_op jit(solution)/shard_map/all_to_all | solution.py:611
  115.8 0.0 copy-done.8
  115.8 1.2 %shard_map.182 = (f32[1,32,2048]{2,1,0:T(8,128)}, f32[1,32,2048]{2,1,0:T(8,128)}) custom-call(f32[384,128]{1,0:T(8,128)S(1)} %bitcast.13, f32[1,32,2048]{2,1,0:T(8,128)S(1)} %copy-done.1, f32[1,32,2048]{2,1,0:T(8,128)S(1)} %copy-done.8, f32[32,128]{1,0:T(8,128)S(1)} %copy-done.12, bf16[2,192,256]{2,1,0:T(8,128)(2,1)S(1)} %copy-done.10), custom_call_target="tpu_custom_call" | custom-call | tf_op jit(solution)/shard_map/pallas_call | solution.py:597
  (15 shorter events, 0.0 us)
Async XLA Ops:
  0.6 14.8 %copy-start.7 = (f32[8,512]{1,0:T(8,128)S(1)}, f32[8,512]{1,0:T(8,128)}, u32[]{:S(2)}) copy-start(f32[8,512]{1,0:T(8,128)} %constant.35.clone.facts_ref) | copy-start | bytes 49156
  0.6 14.8 %copy-start.14 = (f32[8,8]{1,0:T(8,128)S(1)}, f32[8,8]{1,0:T(8,128)}, u32[]{:S(2)}) copy-start(f32[8,8]{1,0:T(8,128)} %to_ref.1) | copy-start | bytes 772
  0.7 14.8 %copy-start.15 = (f32[8,8]{1,0:T(8,128)S(1)}, f32[8,8]{1,0:T(8,128)}, u32[]{:S(2)}) copy-start(f32[8,8]{1,0:T(8,128)} %from_ref.1) | copy-start | bytes 772
  0.7 14.8 %copy-start.16 = (f32[8]{0:T(128)S(1)}, f32[8]{0:T(128)}, u32[]{:S(2)}) copy-start(f32[8]{0:T(128)} %deform_ref.1) | copy-start | bytes 100
  2.9 23.6 %copy-start.3 = (bf16[2,3,256,256]{3,2,1,0:T(8,128)(2,1)S(1)}, bf16[2,3,256,256]{3,2,1,0:T(8,128)(2,1)}, u32[]{:S(2)}) copy-start(bf16[2,3,256,256]{3,2,1,0:T(8,128)(2,1)} %constant.31.clone.lanes_ref) | copy-start | bytes 2359300
  2.9 23.6 %all-to-all-start = ((f32[64,1,768]{2,1,0:T(1,128)}), f32[64,1,768]{2,1,0:T(1,128)S(1)}, u32[]{:S(2)}, u32[]{:S(2)}) async-start(f32[64,1,768]{2,1,0:T(1,128)} %bitcast.17), calls=%async_computation | async-start | bytes 393216 | tf_op jit(solution)/shard_map/all_to_all | solution.py:611
  15.4 11.0 %copy-start.4 = (f32[2,64,128]{2,1,0:T(8,128)S(1)}, f32[2,64,128]{2,1,0:T(8,128)}, u32[]{:S(2)}) copy-start(f32[2,64,128]{2,1,0:T(8,128)} %constant.30.clone.turn_ref) | copy-start | bytes 196612
  15.5 11.0 %copy-start.5 = (bf16[128,384]{1,0:T(8,128)(2,1)S(1)}, bf16[128,384]{1,0:T(8,128)(2,1)}, u32[]{:S(2)}) copy-start(bf16[128,384]{1,0:T(8,128)(2,1)} %constant.28.clone.radix_ref) | copy-start | bytes 294916
  27.0 22.9 %copy-start = (bf16[2,3,256,256]{3,2,1,0:T(8,128)(2,1)S(1)}, bf16[2,3,256,256]{3,2,1,0:T(8,128)(2,1)}, u32[]{:S(2)}) copy-start(bf16[2,3,256,256]{3,2,1,0:T(8,128)(2,1)} %constant.32.clone.unlanes_ref) | copy-start | bytes 2359300
  27.0 22.9 %copy-start.6 = (bf16[128,384]{1,0:T(8,128)(2,1)S(1)}, bf16[128,384]{1,0:T(8,128)(2,1)}, u32[]{:S(2)}) copy-start(bf16[128,384]{1,0:T(8,128)(2,1)} %constant.29.clone.unradix_ref) | copy-start | bytes 294916
  51.0 28.5 %copy-start.2 = (bf16[2,2,128,256]{3,2,1,0:T(8,128)(2,1)S(1)}, bf16[2,2,128,256]{3,2,1,0:T(8,128)(2,1)}, u32[]{:S(2)}) copy-start(bf16[2,2,128,256]{3,2,1,0:T(8,128)(2,1)} %constant.25.clone.table_hbm.table_ref) | copy-start | bytes 786436
  51.0 28.4 %copy-start.11 = (bf16[2,192,256]{2,1,0:T(8,128)(2,1)S(1)}, bf16[2,192,256]{2,1,0:T(8,128)(2,1)}, u32[]{:S(2)}) copy-start(bf16[2,192,256]{2,1,0:T(8,128)(2,1)} %constant.27.clone.untable_ref) | copy-start | bytes 589828
  51.0 28.4 %copy-start.12 = (f32[32,128]{1,0:T(8,128)S(1)}, f32[32,128]{1,0:T(8,128)}, u32[]{:S(2)}) copy-start(f32[32,128]{1,0:T(8,128)} %constant.24.clone.twiddle_hbm.twiddle_ref) | copy-start | bytes 49156
  80.9 18.0 %copy-start.9 = (bf16[2,256,256]{2,1,0:T(8,128)(2,1)S(1)}, bf16[2,256,256]{2,1,0:T(8,128)(2,1)}, u32[]{:S(2)}) copy-start(bf16[2,256,256]{2,1,0:T(8,128)(2,1)} %constant.33.clone.project_ref) | copy-start | bytes 786436
  80.9 18.0 %copy-start.13 = (bf16[256,256]{1,0:T(8,128)(2,1)S(1)}, bf16[256,256]{1,0:T(8,128)(2,1)}, u32[]{:S(2)}) copy-start(bf16[256,256]{1,0:T(8,128)(2,1)} %constant.34.clone.mean_ref) | copy-start | bytes 393220
  98.8 16.9 %copy-start.8 = (f32[1,32,2048]{2,1,0:T(8,128)S(1)}, f32[1,32,2048]{2,1,0:T(8,128)}, u32[]{:S(2)}) copy-start(f32[1,32,2048]{2,1,0:T(8,128)} %start_ref.1) | copy-start | bytes 786436
  98.8 16.9 %copy-start.10 = (bf16[2,192,256]{2,1,0:T(8,128)(2,1)S(1)}, bf16[2,192,256]{2,1,0:T(8,128)(2,1)}, u32[]{:S(2)}) copy-start(bf16[2,192,256]{2,1,0:T(8,128)(2,1)} %constant.26.clone.untable_ref) | copy-start | bytes 589828
  99.8 15.9 %copy-start.1 = (f32[1,32,2048]{2,1,0:T(8,128)S(1)}, f32[1,32,2048]{2,1,0:T(8,128)}, u32[]{:S(2)}) copy-start(f32[1,32,2048]{2,1,0:T(8,128)} %state_ref.1) | copy-start | bytes 786436

commit v6 on v5

v6 whole, which is shorter than its diff:
```python
import functools
import math

import jax
import jax.numpy as jnp
import ml_dtypes
import numpy as np
from jax import lax
from jax.experimental import pallas as pl
from jax.experimental.pallas import tpu as pltpu
from jax.sharding import PartitionSpec as P

GRID = 2048
KCUT = 672
ROWS = 32
MINE = 21
CHUNK = 6
KAP = 64
JP = 11
SPAN = 512
USED = MINE * 2 * JP
TILES = ((0, 0), (1, 0), (1, 1), (2, 1), (2, 2), (3, 2), (4, 2), (4, 3), (5, 3))
WINDOW = (0, 0, 1, 2, 2, 2)
HYPER_RATE = 0.2
STEP_SIZE = 0.5
BF16 = jnp.bfloat16
F32 = jnp.float32


def halves(table):
    high = table.astype(ml_dtypes.bfloat16)
    low = (table - high.astype(np.float64)).astype(ml_dtypes.bfloat16)
    return np.stack([high, low])


def turn(numerator, denominator):
    angle = 2.0 * math.pi * (np.mod(numerator, denominator) / denominator)
    return np.cos(angle), np.sin(angle)


def column_j(h, i):
    return 21 * h + i - 84 * (h // 2)


def x_forward_table():
    b = np.arange(128)
    table = np.zeros((2, 4, 2, 2, 8, 2, 128))
    for h in range(4):
        for i in range(MINE):
            c, s = turn(column_j(h, i) * b, 128)
            own = table[h // 2, i % 4, h % 2, :, i // 4]
            own[0, 0], own[0, 1], own[1, 0], own[1, 1] = c, s, -s, c
    return halves(table.reshape(2, 128, 256))


def x_inverse_table(by_chunk, times_i):
    b = np.arange(128)
    table = np.zeros((4, 4, 2, 6, 2, 128)) if by_chunk else np.zeros((4, 2, MINE, 2, 128))
    for h in range(4):
        for i in range(MINE):
            c, s = turn(column_j(h, i) * b, 128)
            if times_i:
                c, s = -s, c
            own = table[i % 4, h, :, i // 4] if by_chunk else table[h, :, i]
            own[0, 0], own[0, 1], own[1, 0], own[1, 1] = c, s, -s, c
    table = table.reshape(-1, 256) * (2.0 / (GRID * GRID))
    return halves(table if by_chunk else np.pad(table, ((0, 8), (0, 0))))


def x_twiddle():
    table = np.zeros((32, 128))
    c, s = turn(np.arange(9)[:, None] * np.arange(128)[None, :], GRID)
    table[0:9] = c
    table[16:25] = s
    return table.astype(np.float32)


def y_radix_table():
    c, s = turn(np.arange(KAP)[:, None] * np.arange(64)[None, :], 64)
    high, low = halves(np.concatenate([c, -s], axis=0))
    return np.concatenate([high, high, low], axis=1)


def y_radix_inverse_table():
    c, s = turn(np.arange(64)[:, None] * np.arange(KAP)[None, :], 64)
    high, low = halves(np.concatenate([c, -s], axis=1))
    return np.concatenate([high, high, low], axis=1)


def y_twiddle():
    c, s = turn(np.arange(KAP)[:, None] * np.arange(ROWS)[None, :], GRID)
    return np.stack([np.tile(c, (1, 4)), np.tile(s, (1, 4))]).astype(np.float32)


def lanes_of(jr):
    c, s = turn(np.arange(ROWS)[:, None] * np.arange(JP)[None, :], ROWS)
    table = np.zeros((2, 4, ROWS, SPAN))
    for jb in range(4):
        i = 4 * jr + jb
        if i < MINE:
            re = slice(2 * JP * i, 2 * JP * i + JP)
            im = slice(2 * JP * i + JP, 2 * JP * i + 2 * JP)
            table[0, jb, :, re], table[1, jb, :, re] = c, s
            table[0, jb, :, im], table[1, jb, :, im] = -s, c
    return table.reshape(256, SPAN)


def y_lane_table():
    return halves(np.stack([lanes_of(jr)[:, 128 * tile : 128 * tile + 128] for jr, tile in TILES]))


def y_lane_inverse_table(times_i):
    tables = []
    for jr in range(6):
        table = 2.0 * lanes_of(jr)[:, 128 * WINDOW[jr] : 128 * WINDOW[jr] + 256].T
        if times_i:
            table = np.concatenate([-table[:, 128:], table[:, :128]], axis=1)
        tables.append(table)
    return halves(np.stack(tables))


def y_projection_table():
    difference = np.arange(ROWS)[None, :] - np.arange(ROWS)[:, None]
    tables = []
    for count in (JP, JP - 1):
        c, s = turn(difference[:, :, None] * np.arange(count)[None, None, :], ROWS)
        c, s = np.kron(np.eye(4), 2 * c.sum(-1)), np.kron(np.eye(4), 2 * s.sum(-1))
        tables.append(np.block([[c, s], [-s, c]]))
    return halves(np.stack(tables))


def y_mean_table():
    return np.kron(np.eye(8), np.ones((ROWS, ROWS))).astype(ml_dtypes.bfloat16)


def lane_facts():
    lane = np.arange(SPAN)
    facts = np.zeros((8, SPAN))
    facts[0] = 16 * (lane // (2 * JP))
    facts[1] = 64 * (lane % JP)
    return facts.astype(np.float32)


def split(value):
    high = value.astype(BF16)
    low = (value - high.astype(F32)).astype(BF16)
    return high, low


def matmul(left, right, dims):
    def one(a, b):
        return lax.dot_general(a, b, (dims, ((), ())), preferred_element_type=F32)

    return one(left[0], right[0]) + (one(left[0], right[1]) + one(left[1], right[0]))


def matmul_deep(table, right):
    depth = right[0].shape[0]

    def one(a, b):
        return lax.dot_general(a, b, (NN, ((), ())), preferred_element_type=F32)

    both = jnp.concatenate(right, axis=0)
    return one(table[:, : 2 * depth], both) + one(table[:, 2 * depth :], right[0])


NN = ((1,), (0,))
NT = ((1,), (1,))
TN = ((0,), (0,))

C1 = math.cos(math.pi / 8)
C2 = math.cos(math.pi / 4)
C3 = math.cos(3 * math.pi / 8)


def real_analysis(x):
    s = [x[a] + x[a + 8] for a in range(8)]
    d = [x[a] - x[a + 8] for a in range(8)]
    e = [None] + [d[a] - d[8 - a] for a in range(1, 4)]
    f = [None] + [d[a] + d[8 - a] for a in range(1, 4)]
    e2, f2 = e[2] * C2, f[2] * C2
    plus, minus = d[0] + e2, d[0] - e2
    first, second = e[1] * C1 + e[3] * C3, e[1] * C3 - e[3] * C1
    third, fourth = f[1] * C3 + f[3] * C1, f[1] * C1 - f[3] * C3
    u, v = d[4] + f2, f2 - d[4]
    p = [s[a] + s[a + 4] for a in range(4)]
    q = [s[a] - s[a + 4] for a in range(4)]
    even, odd = p[0] + p[2], p[1] + p[3]
    hd, hs = (q[1] - q[3]) * C2, (q[1] + q[3]) * C2
    real = [
        even + odd,
        plus + first,
        q[0] + hd,
        minus + second,
        p[0] - p[2],
        minus - second,
        q[0] - hd,
        plus - first,
        even - odd,
    ]
    imag = [
        None,
        -(third + u),
        -(q[2] + hs),
        -(fourth + v),
        p[3] - p[1],
        v - fourth,
        q[2] - hs,
        u - third,
        None,
    ]
    return real, imag


def real_synthesis(real, imag):
    plus, first = real[1] + real[7], real[1] - real[7]
    minus, second = real[3] + real[5], real[3] - real[5]
    third, u = -(imag[1] + imag[7]), imag[7] - imag[1]
    fourth, v = -(imag[3] + imag[5]), imag[5] - imag[3]
    d = [None] * 8
    d[0], d[4] = plus + minus, u - v
    e = [None, first * C1 + second * C3, (plus - minus) * C2, first * C3 - second * C1]
    f = [None, third * C3 + fourth * C1, (u + v) * C2, third * C1 - fourth * C3]
    for a in range(1, 4):
        d[a], d[8 - a] = f[a] + e[a], f[a] - e[a]
    even, odd = real[0] + real[8], real[0] - real[8]
    p = [even + real[4], odd - imag[4], even - real[4], odd + imag[4]]
    hr, hi = (real[2] - real[6]) * C2, (imag[2] + imag[6]) * C2
    q = [real[2] + real[6], hr - hi, imag[6] - imag[2], -(hr + hi)]
    s = [p[a] + q[a] for a in range(4)] + [p[a] - q[a] for a in range(4)]
    return [s[a] + d[a] for a in range(8)] + [s[a] - d[a] for a in range(8)]


def regroup(blocks, wanted):
    block = lax.broadcasted_iota(jnp.int32, (1, 128), 1) // 32
    turned = [
        b if b is None or i == 0 else pltpu.roll(b, 32 * i, 1) for i, b in enumerate(blocks)
    ]
    results = []
    for p in wanted:
        total = None
        for i in range(4):
            part = jnp.zeros_like(turned[0]) if turned[i] is None else turned[i]
            total = part if total is None else jnp.where(block == (p + i) % 4, part, total)
        results.append(total if p == 0 else pltpu.roll(total, 128 - 32 * p, 1))
    return results


def turn_by(re, im, c, s):
    return re * c + im * s, im * c - re * s


def x_forward(real, imag, twiddle, table):
    pieces = []
    for k in range(9):
        if k == 0:
            pieces.append(jnp.concatenate([real[0], jnp.zeros_like(real[0])], axis=1))
            continue
        c, s = twiddle[k : k + 1], twiddle[16 + k : 17 + k]
        if k == 8:
            re, im = real[8] * c, -(real[8] * s)
        else:
            re, im = real[k] * c + imag[k] * s, imag[k] * c - real[k] * s
        pieces.append(jnp.concatenate([re, im], axis=1))
    shared = split(jnp.concatenate(pieces[1:8], axis=0))
    results = []
    for half, own in enumerate((pieces[0], pieces[8])):
        own = split(own)
        right = [jnp.concatenate([own[i], shared[i]], axis=0) for i in range(2)]
        results.append(matmul([table[0, half], table[1, half]], right, NT))
    return results


def modes_of(source, twiddle):
    real, imag = [], []
    for k in range(9):
        c, s = twiddle[k : k + 1], twiddle[16 + k : 17 + k]
        z = source(k)
        re, im = z[:, :128], z[:, 128:]
        if k == 0:
            real.append(re)
            imag.append(None)
        else:
            real.append(re * c - im * s)
            imag.append(None if k == 8 else re * s + im * c)
    return real, imag


def y_turned(in_ref, radix, twiddle):
    columns = [in_ref[pl.ds(jr, 64, stride=CHUNK), :] for jr in range(6)]
    high, low = split(jnp.concatenate(columns, axis=1))
    mixed = lax.dot_general(
        radix[...],
        jnp.concatenate([high, low, high], axis=0),
        (NN, ((), ())),
        preferred_element_type=F32,
    )
    results = []
    for jr in range(6):
        lanes = slice(128 * jr, 128 * jr + 128)
        re, im = turn_by(mixed[:KAP, lanes], mixed[KAP:, lanes], twiddle[0], twiddle[1])
        results.append(jnp.concatenate([re, im], axis=1))
    return results


def y_returned(pairs, radix, twiddle):
    turned = [turn_by(pair[:, :128], pair[:, 128:], twiddle[0], -twiddle[1]) for pair in pairs]
    right = [jnp.concatenate([pair[part] for pair in turned], axis=1) for part in range(2)]
    return matmul_deep(radix, split(jnp.concatenate(right, axis=0)))


def y_waves(facts):
    kap = lax.broadcasted_iota(jnp.int32, (KAP, 1), 0).astype(F32)
    return kap + facts[1:2]


def x_waves(facts, owner):
    slot = owner // 8
    h = (owner % 8) // 2
    eight = jnp.where(slot == 0, 8 * (h // 2), 0)
    return facts[0:1] + (slot + eight + 16 * (21 * h - 84 * (h // 2))).astype(F32)


def half_of_zero(wave):
    return jnp.where(wave == 0.0, 0.5, 1.0)


def store_x(out_ref, results, group):
    for half in range(2):
        lanes = slice(128 * group, 128 * group + 128)
        blocks = [results[half][32 * jb : 32 * jb + 32, lanes] for jb in range(4)]
        for slot, block in enumerate(regroup(blocks, range(4))):
            for own in range(4):
                start = (8 * (4 * group + slot) + 4 * half + own) * CHUNK
                out_ref[start : start + CHUNK, :] = block[8 * own : 8 * own + CHUNK]


def state_kernel(
    state_hbm, twiddle_hbm, table_hbm, out_hbm, state_ref, twiddle_ref, table_ref, out_ref, sems
):
    pairs = ((state_hbm, state_ref), (twiddle_hbm, twiddle_ref), (table_hbm, table_ref))
    copies = [pltpu.make_async_copy(a, b, sems.at[i]) for i, (a, b) in enumerate(pairs)]
    for copy in copies:
        copy.start()
    copies[0].wait()
    x = [state_ref[0, :, 128 * a : 128 * a + 128] for a in range(16)]
    real, imag = real_analysis(x)
    copies[1].wait()
    copies[2].wait()
    results = x_forward(real, imag, twiddle_ref[...], table_ref)
    sends = []
    for group in range(2):
        store_x(out_ref, results, group)
        rows = pl.ds(32 * group * CHUNK, 32 * CHUNK)
        sends.append(pltpu.make_async_copy(out_ref.at[rows], out_hbm.at[rows], sems.at[3 + group]))
        sends[-1].start()
    for send in sends:
        send.wait()


def weights_kernel(to_ref, from_ref, deform_ref, facts_ref, out_ref):
    facts = facts_ref[...]
    wave_x = x_waves(facts, lax.axis_index("row"))
    wave_y = y_waves(facts)
    square = (wave_x * wave_x + wave_y * wave_y)[:, :USED]
    layer = lax.axis_index("layer")
    modes = [from_ref[layer, m] * (-1.0 / (square + deform_ref[m])) for m in range(8)]
    for n in range(8):
        total = None
        for m in range(8):
            term = modes[m] * to_ref[m, n]
            total = term if total is None else total + term
        out_ref[n] = total


def spectrum_kernel(in_ref, radix_ref, turn_ref, lanes_ref, facts_ref, spec_ref, used_ref):
    turned = [split(pair) for pair in y_turned(in_ref, radix_ref, turn_ref)]
    wave_y = y_waves(facts_ref[...])
    for tile in range(4):
        total = None
        for index, (jr, own) in enumerate(TILES):
            if own == tile:
                part = matmul(turned[jr], [lanes_ref[0, index], lanes_ref[1, index]], NN)
                total = part if total is None else total + part
        lanes = slice(128 * tile, 128 * tile + 128)
        total = jnp.where(wave_y[:, lanes] < KCUT, total, 0.0)
        spec_ref[:, lanes] = total
        used = min(USED - 128 * tile, 128)
        used_ref[:, 128 * tile : 128 * tile + used] = total[:, :used]


def stream_kernel(
    weights_ref,
    all_ref,
    spec_ref,
    unradix_ref,
    turn_ref,
    unlanes_ref,
    unlanes_i_ref,
    facts_ref,
    out_ref,
    stream_ref,
):
    facts = facts_ref[...]
    wave_x = x_waves(facts, lax.axis_index("row"))
    wave_y = y_waves(facts)
    stream = None
    for n in range(8):
        term = weights_ref[n] * all_ref[n]
        stream = term if stream is None else stream + term
    stream_ref[:, SPAN - 128 :] = jnp.zeros((KAP, 128), F32)
    stream_ref[:, :USED] = stream
    stream = stream_ref[...]
    spectrum = spec_ref[...]
    along_y = wave_y * half_of_zero(wave_x)
    along_x = wave_x * half_of_zero(wave_y)
    both_y = split(jnp.concatenate([-along_y * stream, along_y * spectrum], axis=0))
    both_x = split(jnp.concatenate([along_x * stream, along_x * spectrum], axis=0))
    pairs = []
    for jr in range(6):
        lanes = slice(128 * WINDOW[jr], 128 * WINDOW[jr] + 256)
        for both, table in ((both_y, unlanes_i_ref), (both_x, unlanes_ref)):
            out = matmul([part[:, lanes] for part in both], [table[0, jr], table[1, jr]], NN)
            pairs += [out[:KAP], out[KAP:]]
    out = y_returned(pairs, unradix_ref, turn_ref)
    for jr in range(6):
        blocks = [out[:, 128 * (4 * jr + f) : 128 * (4 * jr + f) + 128] for f in range(4)]
        count = min(MINE - 4 * jr, 4)
        for jb, block in enumerate(regroup(blocks, range(count))):
            out_ref[pl.ds(4 * jr + jb, 64, stride=MINE), :] = block


def jacobian_kernel(
    in_ref, twiddle_ref, untable_ref, untable_i_ref, table_ref, out_ref, first0, first1, whole0, whole1, jac
):
    depth = 8 * MINE
    lane = lax.broadcasted_iota(jnp.int32, (1, 128), 1)
    row = lax.broadcasted_iota(jnp.int32, (depth, 1), 0)
    slots = [in_ref[depth * slot : depth * slot + depth, :] for slot in range(8)]
    spare = jnp.zeros((8, 128), F32)
    lower, upper = [], []
    for a, b in zip(slots[0::2], slots[1::2]):
        pair = [jnp.where(lane < 64, a, pltpu.roll(b, 64, 1)), jnp.where(lane < 64, pltpu.roll(a, 64, 1), b)]
        lower.append(jnp.concatenate([pair[0], spare], axis=0))
        upper.append(jnp.concatenate([pair[1], spare], axis=0))
    own = jnp.concatenate([jnp.where(row < depth // 2, slots[0], 0.0), spare], axis=0)
    own = split(own)
    tables = [[ref[0], ref[1]] for ref in (untable_ref, untable_i_ref)]
    first0[...] = matmul(own, tables[0], TN)
    first1[...] = matmul(own, tables[1], TN)
    whole0[...] = matmul(split(jnp.concatenate(lower, axis=1)), tables[0], TN)
    whole1[...] = matmul(split(jnp.concatenate(upper, axis=1)), tables[1], TN)
    twiddle = twiddle_ref[...]
    for block in range(4):
        rows = slice(8 * block, 8 * block + 8)

        def physical(field):
            first, whole = ((first0, whole0), (first1, whole1))[field // 2]

            def source(k):
                start = 32 * field + rows.start
                if k == 0:
                    return first[start : start + 8, :]
                start = 32 * (field % 2) + 64 * (k % 8) + rows.start
                z = whole[start : start + 8, :]
                return z if k < 8 else z - source(0)

            return real_synthesis(*modes_of(source, twiddle))

        east, slope_x = physical(0), physical(3)
        product = [a * b for a, b in zip(east, slope_x)]
        north, slope_y = physical(2), physical(1)
        product = [p + a * b for p, a, b in zip(product, north, slope_y)]
        real, imag = real_analysis(product)
        for k in range(9):
            jac[0, k, rows, :] = real[k]
            if imag[k] is not None:
                jac[1, k, rows, :] = imag[k]
    real = [jac[0, k] for k in range(9)]
    imag = [None] + [jac[1, k] for k in range(1, 8)] + [None]
    results = x_forward(real, imag, twiddle, table_ref)
    for group in range(2):
        store_x(out_ref, results, group)


def projection_kernel(
    in_ref, spec_ref, radix_ref, unradix_ref, turn_ref, project_ref, mean_ref, unlanes_ref, facts_ref, out_ref
):
    facts = facts_ref[...]
    wave_x = x_waves(facts, lax.axis_index("row"))
    wave_y = y_waves(facts)
    ratio = (wave_x * wave_x + wave_y * wave_y) * (1.0 / (KCUT * KCUT))
    ratio = ratio * ratio
    damped = split(((HYPER_RATE * (ratio * ratio)) * half_of_zero(wave_y)) * spec_ref[...])
    left = [split(pair) for pair in y_turned(in_ref, radix_ref, turn_ref)]
    sides = []
    for side in range(2):
        rows = slice(32 * side, 32 * side + 32)
        stacked = [jnp.concatenate([pair[i][rows] for pair in left], axis=0) for i in range(2)]
        sides.append(matmul(stacked, [project_ref[i, side] for i in range(2)], NN))
    first = lax.broadcasted_iota(jnp.int32, (16, 1), 0) == 0
    lane = lax.broadcasted_iota(jnp.int32, (1, 256), 1)
    zero_wave = (lax.axis_index("row") < 2) & (lane % 128 < 32)
    pairs = []
    for jr in range(6):
        mean = sum(
            lax.dot_general(
                left[jr][i][:16], mean_ref[...], (NN, ((), ())), preferred_element_type=F32
            )
            for i in range(2)
        )
        low, high = [side[32 * jr : 32 * jr + 32] for side in sides]
        low = jnp.concatenate([low[:16] - jnp.where(first, mean, 0.0), low[16:]], axis=0)
        window = [part[:, 128 * WINDOW[jr] : 128 * WINDOW[jr] + 256] for part in damped]
        damping = matmul(window, [unlanes_ref[i, jr] for i in range(2)], NN)
        total = jnp.concatenate([low, high], axis=0) + damping
        pairs.append(total * jnp.where(zero_wave, -0.5, -1.0) if jr == 0 else -total)
    out = y_returned(pairs, unradix_ref, turn_ref)
    for jr in range(6):
        out_ref[pl.ds(jr, 64, stride=CHUNK), :] = out[:, 128 * jr : 128 * jr + 128]


def state_update_kernel(
    in_ref,
    state_ref,
    start_ref,
    twiddle_ref,
    untable_ref,
    tendency_hbm,
    new_hbm,
    first,
    whole,
    tendency_ref,
    new_ref,
    sems,
):
    depth = 8 * CHUNK
    table = [untable_ref[0], untable_ref[1]]
    for group in range(2):
        blocks = [in_ref[depth * slot : depth * slot + depth, :] for slot in range(4 * group, 4 * group + 4)]
        side = jnp.concatenate(regroup(blocks, range(4)), axis=0)
        whole[128 * group : 128 * group + 128, :] = matmul(split(side), table, TN)
        if group == 0:
            row = lax.broadcasted_iota(jnp.int32, (4 * depth, 1), 0)
            own = jnp.where(row % depth < depth // 2, side, 0.0)
            first[...] = matmul(split(own), table, TN)
    twiddle = twiddle_ref[...]
    sends = []
    for block in range(4):
        rows = slice(8 * block, 8 * block + 8)

        def source(k):
            if k == 0:
                return first[rows, :]
            start = 32 * (k % 8) + rows.start
            z = whole[start : start + 8, :]
            return z if k < 8 else z - source(0)

        tendency = real_synthesis(*modes_of(source, twiddle))
        for a in range(16):
            columns = slice(128 * a, 128 * a + 128)
            tendency_ref[0, rows, columns] = tendency[a]
            new_ref[0, rows, columns] = 0.75 * start_ref[0, rows, columns] + 0.25 * (
                state_ref[0, rows, columns] + STEP_SIZE * tendency[a]
            )
        for i, (near, far) in enumerate(((tendency_ref, tendency_hbm), (new_ref, new_hbm))):
            own = (slice(None), pl.ds(8 * block, 8))
            sends.append(pltpu.make_async_copy(near.at[own], far.at[own], sems.at[2 * block + i]))
            sends[-1].start()
    for send in sends:
        send.wait()


VMEM = pl.BlockSpec(memory_space=pltpu.VMEM)
SMEM = pl.BlockSpec(memory_space=pltpu.SMEM)
ANY = pl.BlockSpec(memory_space=pl.ANY)
MIB = 1024 * 1024


def call(kernel, outs, operands, scalars=0, scratch=(), far_in=False, far_out=False, copies=0, cost=None):
    scratch_shapes = [pltpu.VMEM(operand.shape, operand.dtype) for operand in operands] if far_in else []
    scratch_shapes += [pltpu.VMEM(shape, F32) for shape in scratch]
    scratch_shapes += [pltpu.VMEM(shape, F32) for shape in outs] if far_out else []
    scratch_shapes += [pltpu.SemaphoreType.DMA((copies,))] if copies else []
    near = [SMEM] * scalars + [VMEM] * (len(operands) - scalars)
    return pl.pallas_call(
        kernel,
        out_shape=[jax.ShapeDtypeStruct(shape, F32) for shape in outs],
        in_specs=[ANY] * len(operands) if far_in else near,
        out_specs=[ANY if far_out else VMEM] * len(outs),
        scratch_shapes=scratch_shapes,
        compiler_params=pltpu.CompilerParams(vmem_limit_bytes=(60 if far_in else 32) * MIB),
        cost_estimate=cost,
    )(*operands)


def exchange(chunks, devices):
    length = chunks.shape[0]
    sent = chunks.reshape(devices, 1, length * 128 // devices)
    return lax.all_to_all(sent, "row", split_axis=0, concat_axis=0, tiled=True).reshape(length, 128)


def per_device(state, start_state, to_modes, from_modes, deform):
    devices = lax.axis_size("row")
    turn_x = jnp.asarray(x_twiddle())
    forward_x = jnp.asarray(x_forward_table())
    inverse_x = jnp.asarray(x_inverse_table(False, False))
    inverse_ix = jnp.asarray(x_inverse_table(False, True))
    inverse_chunk = jnp.asarray(x_inverse_table(True, False))
    radix = jnp.asarray(y_radix_table())
    unradix = jnp.asarray(y_radix_inverse_table())
    turn_y = jnp.asarray(y_twiddle())
    lanes = jnp.asarray(y_lane_table())
    unlanes = jnp.asarray(y_lane_inverse_table(False))
    unlanes_i = jnp.asarray(y_lane_inverse_table(True))
    project = jnp.asarray(y_projection_table())
    mean = jnp.asarray(y_mean_table())
    facts = jnp.asarray(lane_facts())

    one, four = (64 * CHUNK, 128), (64 * MINE, 128)
    (columns,) = call(state_kernel, [one], [state, turn_x, forward_x], far_in=True, far_out=True, copies=5)
    columns = exchange(columns, devices)
    spectrum, used = call(
        spectrum_kernel, [(KAP, SPAN), (KAP, USED)], [columns, radix, turn_y, lanes, facts]
    )
    (weights,) = call(
        weights_kernel,
        [(8, KAP, USED)],
        [to_modes, from_modes, deform, facts],
        scalars=3,
        cost=pl.CostEstimate(flops=8_000_000, bytes_accessed=2_000_000, transcendentals=0),
    )
    gathered = lax.all_gather(used, "layer", axis=0, tiled=False)
    (fields,) = call(
        stream_kernel,
        [four],
        [weights, gathered, spectrum, unradix, turn_y, unlanes, unlanes_i, facts],
        scratch=[(KAP, SPAN)],
    )
    fields = exchange(fields, devices)
    (flux,) = call(
        jacobian_kernel,
        [one],
        [fields, turn_x, inverse_x, inverse_ix, forward_x],
        scratch=[(128, 256)] * 2 + [(512, 256)] * 2 + [(2, 9, ROWS, 128)],
    )
    flux = exchange(flux, devices)
    (total,) = call(
        projection_kernel,
        [one],
        [flux, spectrum, radix, unradix, turn_y, project, mean, unlanes, facts],
    )
    total = exchange(total, devices)
    return tuple(
        call(
            state_update_kernel,
            [(1, ROWS, GRID)] * 2,
            [total, state, start_state, turn_x, inverse_chunk],
            scratch=[(128, 256), (256, 256)],
            far_out=True,
            copies=8,
        )
    )


def solution(mesh):
    in_specs = (P("layer", "row", None), P("layer", "row", None), P(), P(), P())
    out_specs = (P("layer", "row", None), P("layer", "row", None))
    return jax.shard_map(
        per_device, mesh=mesh, in_specs=in_specs, out_specs=out_specs, check_vma=False
    )
```

time: 117 us -> 119 us (1.017)
  local copies, waits for them, and re-layouts: 0.1 us -> 5.49 us
  waiting for transfers between devices: 9.59 us -> 6.89 us
  blocking collectives: 85.2 us -> 82.7 us
  Pallas kernels: 8.78 us -> 10.5 us
    unnamed x34 -> x40, local copies, waits for them, and re-layouts: 0.1 us -> 5.49 us
    all_to_all x1, waiting for transfers between devices: 9.59 us -> 6.89 us  [exchange(): lax.all_to_all(sent, 'row', split_axis=0, concat_axis=0, tiled=True)]
    all_to_all x3, blocking collectives: 62.3 us -> 59.9 us  [exchange(): lax.all_to_all(sent, 'row', split_axis=0, concat_axis=0, tiled=True)]
    pallas_call x7, Pallas kernels: 8.78 us -> 10.5 us  [call(): pl.pallas_call(kernel, out_shape=[jax.ShapeDtypeStruct(shape, F32) for sh...]
where the time goes in v6:
time: 119 us
  blocking collectives  82.7 us (69%)
  starting transfers between devices  12.4 us (10%)
  Pallas kernels  10.5 us (9%)
  waiting for transfers between devices  6.89 us (6%)
  local copies, waits for them, and re-layouts  5.49 us (5%)
    all_to_all x3, blocking collectives, exchange(): lax.all_to_all(sent, 'row', split_axis=0, concat_axis=0, tiled=True)  59.9 us
    all_gather x1, blocking collectives, per_device(): gathered = lax.all_gather(used, 'layer', axis=0, tiled=False)  22.7 us
    all_to_all x1, starting transfers between devices, exchange(): lax.all_to_all(sent, 'row', split_axis=0, concat_axis=0, tiled=True)  12.4 us
    pallas_call x7, Pallas kernels, call(): pl.pallas_call(kernel, out_shape=[jax.ShapeDtypeStruct(shape, F32) for sh...  10.5 us
    all_to_all x1, waiting for transfers between devices, exchange(): lax.all_to_all(sent, 'row', split_axis=0, concat_axis=0, tiled=True)  6.89 us
    unnamed x40, local copies, waits for them, and re-layouts  5.49 us
  transfers between devices with their start and end apart: 1, of which 1 were waited for; matrix products, arithmetic and copies ran while one was open for 0% of the time, Pallas kernels for 1%

profile of v6, /device:TPU:8, one launch (start us, length us, event | category | flops | bytes accessed | tf_op | source)
XLA Modules:
  0.0 118.7 jit_solution(13224195735007939891)
XLA Ops:
  0.6 0.0 copy-start.8
  0.6 0.0 copy-start.5
  0.7 0.0 copy-start.10
  0.7 2.4 %shard_map.195 = f32[384,128]{1,0:T(8,128)} custom-call(f32[1,32,2048]{2,1,0:T(8,128)} %state_ref.1, f32[32,128]{1,0:T(8,128)} %constant.28.clone.twiddle_hbm.twiddle_ref, bf16[2,2,128,256]{3,2,1,0:T(8,128)(2,1)} %constant.29.clone.table_hbm.table_ref), custom_call_target="tpu_custom_call" | custom-call | tf_op jit(solution)/shard_map/pallas_call | solution.py:586
  3.0 12.4 %all-to-all-start = ((f32[64,1,768]{2,1,0:T(1,128)}), f32[64,1,768]{2,1,0:T(1,128)S(1)}, u32[]{:S(2)}, u32[]{:S(2)}) async-start(f32[64,1,768]{2,1,0:T(1,128)} %bitcast.17), calls=%async_computation | async-start | bytes 393216 | tf_op jit(solution)/shard_map/all_to_all | solution.py:600
  15.4 0.0 copy-start.7
  15.5 0.7 copy-done.7
  16.2 0.7 copy-done.17
  16.9 0.7 copy-done.18
  17.5 0.7 copy-done.19
  18.2 1.4 %shard_map.194.weights_ref = f32[8,64,462]{2,1,0:T(8,128)S(1)} custom-call(f32[8,8]{1,0:T(8,128)S(1)} %copy-done.17, f32[8,8]{1,0:T(8,128)S(1)} %copy-done.18, f32[8]{0:T(128)S(1)} %copy-done.19, f32[8,512]{1,0:T(8,128)S(1)} %copy-done.7), custom_call_target="tpu_custom_call" | custom-call | flops 8000000 | bytes 2000000 | tf_op jit(solution)/shard_map/pallas_call | solution.py:586
  19.6 0.0 copy-start
  19.6 6.9 %all-to-all-done = f32[64,1,768]{2,1,0:T(1,128)S(1)} async-done(((f32[64,1,768]{2,1,0:T(1,128)}), f32[64,1,768]{2,1,0:T(1,128)S(1)}, u32[]{:S(2)}, u32[]{:S(2)}) %all-to-all-start) | async-done | bytes 196640 | tf_op jit(solution)/shard_map/all_to_all | solution.py:600
  26.5 0.0 copy-done.8
  26.5 0.0 copy-done.10
  26.5 0.0 copy-start.2
  26.5 1.3 %copy-done.2 = bf16[2,9,256,128]{3,2,1,0:T(8,128)(2,1)S(1)} copy-done((bf16[2,9,256,128]{3,2,1,0:T(8,128)(2,1)S(1)}, bf16[2,9,256,128]{3,2,1,0:T(8,128)(2,1)}, u32[]{:S(2)}) %copy-start.2) | copy-done | bytes 1179672
  27.8 0.6 shard_map.196
  28.3 22.7 %all-gather = f32[512,462]{1,0:T(8,128)S(1)} all-gather(f32[64,462]{1,0:T(8,128)S(1)} %get-tuple-element.4), channel_id=2, replica_groups=mesh['layer'=8,'row'=64] {'layer'}, dimensions={0}, use_global_device_ids=true | all-gather | bytes 1064448 | tf_op jit(solution)/shard_map/all_gather | solution.py:633
  51.1 1.4 %copy-done.1 = bf16[2,6,256,256]{3,2,1,0:T(8,128)(2,1)S(1)} copy-done((bf16[2,6,256,256]{3,2,1,0:T(8,128)(2,1)S(1)}, bf16[2,6,256,256]{3,2,1,0:T(8,128)(2,1)}, u32[]{:S(2)}) %copy-start.1) | copy-done | bytes 1572888
  52.5 1.6 %shard_map.197 = f32[1344,128]{1,0:T(8,128)S(1)} custom-call(f32[8,64,462]{2,1,0:T(8,128)S(1)} %shard_map.194.weights_ref, f32[8,64,462]{2,1,0:T(8,128)S(1)} %bitcast.9, f32[64,512]{1,0:T(8,128)S(1)} %get-tuple-element.5.spec_ref, bf16[64,384]{1,0:T(8,128)(2,1)S(1)} %copy-done.11, f32[2,64,128]{2,1,0:T(8,128)S(1)} %copy-done.5, ...), custom_call_target="tpu_custom_call" | custom-call | tf_op jit(solution)/shard_map/pallas_call | solution.py:586
  54.1 0.0 copy-start.6
  54.1 0.0 copy-start.16
  54.1 26.4 %all_to_all.20 = f32[64,1,2688]{2,1,0:T(1,128)S(1)} all-to-all(f32[64,1,2688]{2,1,0:T(1,128)S(1)} %bitcast.10), channel_id=1, replica_groups=mesh['layer'=8,'row'=64] {'row'}, dimensions={0} | all-to-all | bytes 1376256 | tf_op jit(solution)/shard_map/all_to_all | solution.py:600
  80.5 0.0 copy-done.15
  80.5 1.8 %shard_map.198 = f32[384,128]{1,0:T(8,128)S(1)} custom-call(f32[1344,128]{1,0:T(8,128)S(1)} %bitcast.11, f32[32,128]{1,0:T(8,128)S(1)} %copy-done.15, bf16[2,176,256]{2,1,0:T(8,128)(2,1)S(1)} %copy-done.14, bf16[2,176,256]{2,1,0:T(8,128)(2,1)S(1)} %copy-done.13, bf16[2,2,128,256]{3,2,1,0:T(8,128)(2,1)S(1)} %copy-done.4), custom_call_target="tpu_custom_call" | custom-call | tf_op jit(solution)/shard_map/pallas_call | solution.py:586
  82.3 17.8 %all_to_all.21 = f32[64,1,768]{2,1,0:T(1,128)S(1)} all-to-all(f32[64,1,768]{2,1,0:T(1,128)S(1)} %bitcast.16), channel_id=1, replica_groups=mesh['layer'=8,'row'=64] {'row'}, dimensions={0} | all-to-all | bytes 393216 | tf_op jit(solution)/shard_map/all_to_all | solution.py:600
  100.2 0.0 copy-start.12
  100.2 1.4 %shard_map.199 = f32[384,128]{1,0:T(8,128)S(1)} custom-call(f32[384,128]{1,0:T(8,128)S(1)} %bitcast.13, f32[64,512]{1,0:T(8,128)S(1)} %get-tuple-element.5.spec_ref, bf16[128,192]{1,0:T(8,128)(2,1)S(1)} %copy-done.10, bf16[64,384]{1,0:T(8,128)(2,1)S(1)} %copy-done.11, f32[2,64,128]{2,1,0:T(8,128)S(1)} %copy-done.5, bf16[2,2,256,256]{3,2,1,0:T(8,128)(2,1)S(1)} %copy-done.6, ...), custom_call_target="tpu_custom_call" | custom-call | tf_op jit(solution)/shard_map/pallas_call | solution.py:586
  101.6 15.7 %all_to_all.22 = f32[64,1,768]{2,1,0:T(1,128)S(1)} all-to-all(f32[64,1,768]{2,1,0:T(1,128)S(1)} %bitcast.14), channel_id=1, replica_groups=mesh['layer'=8,'row'=64] {'row'}, dimensions={0} | all-to-all | bytes 393216 | tf_op jit(solution)/shard_map/all_to_all | solution.py:600
  117.3 0.0 copy-done.12
  117.3 1.4 %shard_map.200 = (f32[1,32,2048]{2,1,0:T(8,128)}, f32[1,32,2048]{2,1,0:T(8,128)}) custom-call(f32[384,128]{1,0:T(8,128)S(1)} %bitcast.15, f32[1,32,2048]{2,1,0:T(8,128)S(1)} %copy-done.3, f32[1,32,2048]{2,1,0:T(8,128)S(1)} %copy-done.9, f32[32,128]{1,0:T(8,128)S(1)} %copy-done.15, bf16[2,192,256]{2,1,0:T(8,128)(2,1)S(1)} %copy-done.12), custom_call_target="tpu_custom_call" | custom-call | tf_op jit(solution)/shard_map/pallas_call | solution.py:586
  (21 shorter events, 0.0 us)
Async XLA Ops:
  0.6 25.8 %copy-start.8 = (f32[8,512]{1,0:T(8,128)S(1)}, f32[8,512]{1,0:T(8,128)}, u32[]{:S(2)}) copy-start(f32[8,512]{1,0:T(8,128)} %constant.41.clone.facts_ref) | copy-start | bytes 49156
  0.6 25.8 %copy-start.5 = (f32[2,64,128]{2,1,0:T(8,128)S(1)}, f32[2,64,128]{2,1,0:T(8,128)}, u32[]{:S(2)}) copy-start(f32[2,64,128]{2,1,0:T(8,128)} %constant.35.clone.turn_ref) | copy-start | bytes 196612
  0.7 25.8 %copy-start.10 = (bf16[128,192]{1,0:T(8,128)(2,1)S(1)}, bf16[128,192]{1,0:T(8,128)(2,1)}, u32[]{:S(2)}) copy-start(bf16[128,192]{1,0:T(8,128)(2,1)} %constant.33.clone.radix_ref) | copy-start | bytes 147460
  3.0 23.4 %all-to-all-start = ((f32[64,1,768]{2,1,0:T(1,128)}), f32[64,1,768]{2,1,0:T(1,128)S(1)}, u32[]{:S(2)}, u32[]{:S(2)}) async-start(f32[64,1,768]{2,1,0:T(1,128)} %bitcast.17), calls=%async_computation | async-start | bytes 393216 | tf_op jit(solution)/shard_map/all_to_all | solution.py:600
  15.4 0.7 copy-start.7
  16.2 0.7 copy-start.17
  16.9 0.7 copy-start.18
  17.5 0.7 copy-start.19
  18.2 32.9 %copy-start.11 = (bf16[64,384]{1,0:T(8,128)(2,1)S(1)}, bf16[64,384]{1,0:T(8,128)(2,1)}, u32[]{:S(2)}) copy-start(bf16[64,384]{1,0:T(8,128)(2,1)} %constant.34.clone.unradix_ref) | copy-start | bytes 147460
  19.6 31.5 %copy-start = (bf16[2,6,256,256]{3,2,1,0:T(8,128)(2,1)S(1)}, bf16[2,6,256,256]{3,2,1,0:T(8,128)(2,1)}, u32[]{:S(2)}) copy-start(bf16[2,6,256,256]{3,2,1,0:T(8,128)(2,1)} %constant.37.clone.unlanes_ref) | copy-start | bytes 4718596
  26.5 1.3 %copy-start.2 = (bf16[2,9,256,128]{3,2,1,0:T(8,128)(2,1)S(1)}, bf16[2,9,256,128]{3,2,1,0:T(8,128)(2,1)}, u32[]{:S(2)}) copy-start(bf16[2,9,256,128]{3,2,1,0:T(8,128)(2,1)} %constant.36.clone.lanes_ref) | copy-start | bytes 3538948
  51.1 1.4 %copy-start.1 = (bf16[2,6,256,256]{3,2,1,0:T(8,128)(2,1)S(1)}, bf16[2,6,256,256]{3,2,1,0:T(8,128)(2,1)}, u32[]{:S(2)}) copy-start(bf16[2,6,256,256]{3,2,1,0:T(8,128)(2,1)} %constant.38.clone.unlanes_i_ref) | copy-start | bytes 4718596
  52.5 28.0 %copy-start.4 = (bf16[2,2,128,256]{3,2,1,0:T(8,128)(2,1)S(1)}, bf16[2,2,128,256]{3,2,1,0:T(8,128)(2,1)}, u32[]{:S(2)}) copy-start(bf16[2,2,128,256]{3,2,1,0:T(8,128)(2,1)} %constant.29.clone.table_hbm.table_ref) | copy-start | bytes 786436
  52.5 28.0 %copy-start.13 = (bf16[2,176,256]{2,1,0:T(8,128)(2,1)S(1)}, bf16[2,176,256]{2,1,0:T(8,128)(2,1)}, u32[]{:S(2)}) copy-start(bf16[2,176,256]{2,1,0:T(8,128)(2,1)} %constant.31.clone.untable_i_ref) | copy-start | bytes 540676
  52.5 28.0 %copy-start.14 = (bf16[2,176,256]{2,1,0:T(8,128)(2,1)S(1)}, bf16[2,176,256]{2,1,0:T(8,128)(2,1)}, u32[]{:S(2)}) copy-start(bf16[2,176,256]{2,1,0:T(8,128)(2,1)} %constant.30.clone.untable_ref) | copy-start | bytes 540676
  52.5 28.0 %copy-start.15 = (f32[32,128]{1,0:T(8,128)S(1)}, f32[32,128]{1,0:T(8,128)}, u32[]{:S(2)}) copy-start(f32[32,128]{1,0:T(8,128)} %constant.28.clone.twiddle_hbm.twiddle_ref) | copy-start | bytes 49156
  54.1 46.1 %copy-start.6 = (bf16[2,2,256,256]{3,2,1,0:T(8,128)(2,1)S(1)}, bf16[2,2,256,256]{3,2,1,0:T(8,128)(2,1)}, u32[]{:S(2)}) copy-start(bf16[2,2,256,256]{3,2,1,0:T(8,128)(2,1)} %constant.39.clone.project_ref) | copy-start | bytes 1572868
  54.1 46.1 %copy-start.16 = (bf16[256,256]{1,0:T(8,128)(2,1)S(1)}, bf16[256,256]{1,0:T(8,128)(2,1)}, u32[]{:S(2)}) copy-start(bf16[256,256]{1,0:T(8,128)(2,1)} %constant.40.clone.mean_ref) | copy-start | bytes 393220
  100.2 17.1 %copy-start.3 = (f32[1,32,2048]{2,1,0:T(8,128)S(1)}, f32[1,32,2048]{2,1,0:T(8,128)}, u32[]{:S(2)}) copy-start(f32[1,32,2048]{2,1,0:T(8,128)} %state_ref.1) | copy-start | bytes 786436
  100.2 17.1 %copy-start.9 = (f32[1,32,2048]{2,1,0:T(8,128)S(1)}, f32[1,32,2048]{2,1,0:T(8,128)}, u32[]{:S(2)}) copy-start(f32[1,32,2048]{2,1,0:T(8,128)} %start_ref.1) | copy-start | bytes 786436
  100.2 17.1 %copy-start.12 = (bf16[2,192,256]{2,1,0:T(8,128)(2,1)S(1)}, bf16[2,192,256]{2,1,0:T(8,128)(2,1)}, u32[]{:S(2)}) copy-start(bf16[2,192,256]{2,1,0:T(8,128)(2,1)} %constant.32.clone.untable_ref) | copy-start | bytes 589828

commit v7 on v6

--- a/solution.py
+++ b/solution.py
@@ -17,10 +17,8 @@
 CHUNK = 6
 KAP = 64
 JP = 11
-SPAN = 512
+PIECE = 4 * 2 * JP
 USED = MINE * 2 * JP
-TILES = ((0, 0), (1, 0), (1, 1), (2, 1), (2, 2), (3, 2), (4, 2), (4, 3), (5, 3))
-WINDOW = (0, 0, 1, 2, 2, 2)
 HYPER_RATE = 0.2
 STEP_SIZE = 0.5
 BF16 = jnp.bfloat16
@@ -53,14 +51,12 @@
     return halves(table.reshape(2, 128, 256))
 
 
-def x_inverse_table(by_chunk, times_i):
+def x_inverse_table(by_chunk):
     b = np.arange(128)
     table = np.zeros((4, 4, 2, 6, 2, 128)) if by_chunk else np.zeros((4, 2, MINE, 2, 128))
     for h in range(4):
         for i in range(MINE):
             c, s = turn(column_j(h, i) * b, 128)
-            if times_i:
-                c, s = -s, c
             own = table[i % 4, h, :, i // 4] if by_chunk else table[h, :, i]
             own[0, 0], own[0, 1], own[1, 0], own[1, 1] = c, s, -s, c
     table = table.reshape(-1, 256) * (2.0 / (GRID * GRID))
@@ -92,31 +88,24 @@
     return np.stack([np.tile(c, (1, 4)), np.tile(s, (1, 4))]).astype(np.float32)
 
 
-def lanes_of(jr):
+def lanes_of():
     c, s = turn(np.arange(ROWS)[:, None] * np.arange(JP)[None, :], ROWS)
-    table = np.zeros((2, 4, ROWS, SPAN))
+    table = np.zeros((2, 4, ROWS, 128))
     for jb in range(4):
-        i = 4 * jr + jb
-        if i < MINE:
-            re = slice(2 * JP * i, 2 * JP * i + JP)
-            im = slice(2 * JP * i + JP, 2 * JP * i + 2 * JP)
-            table[0, jb, :, re], table[1, jb, :, re] = c, s
-            table[0, jb, :, im], table[1, jb, :, im] = -s, c
-    return table.reshape(256, SPAN)
+        re = slice(2 * JP * jb, 2 * JP * jb + JP)
+        im = slice(2 * JP * jb + JP, 2 * JP * jb + 2 * JP)
+        table[0, jb, :, re], table[1, jb, :, re] = c, s
+        table[0, jb, :, im], table[1, jb, :, im] = -s, c
+    return table.reshape(256, 128)
 
 
 def y_lane_table():
-    return halves(np.stack([lanes_of(jr)[:, 128 * tile : 128 * tile + 128] for jr, tile in TILES]))
-
-
-def y_lane_inverse_table(times_i):
-    tables = []
-    for jr in range(6):
-        table = 2.0 * lanes_of(jr)[:, 128 * WINDOW[jr] : 128 * WINDOW[jr] + 256].T
-        if times_i:
-            table = np.concatenate([-table[:, 128:], table[:, :128]], axis=1)
-        tables.append(table)
-    return halves(np.stack(tables))
+    return halves(lanes_of())
+
+
+def y_lane_inverse_table():
+    high, low = halves(2.0 * lanes_of().T)
+    return np.concatenate([high, high, low], axis=0)
 
 
 def y_projection_table():
@@ -133,9 +122,9 @@
     return np.kron(np.eye(8), np.ones((ROWS, ROWS))).astype(ml_dtypes.bfloat16)
 
 
-def lane_facts():
-    lane = np.arange(SPAN)
-    facts = np.zeros((8, SPAN))
+def lane_facts(packed):
+    lane = np.arange(512 if packed else 128)
+    facts = np.zeros((8, lane.size))
     facts[0] = 16 * (lane // (2 * JP))
     facts[1] = 64 * (lane % JP)
     return facts.astype(np.float32)
@@ -162,6 +151,16 @@
 
     both = jnp.concatenate(right, axis=0)
     return one(table[:, : 2 * depth], both) + one(table[:, 2 * depth :], right[0])
+
+
+def matmul_wide(left, table):
+    depth = left[0].shape[1]
+
+    def one(a, b):
+        return lax.dot_general(a, b, (NN, ((), ())), preferred_element_type=F32)
+
+    both = jnp.concatenate(left, axis=1)
+    return one(both, table[: 2 * depth]) + one(left[0], table[2 * depth :])
 
 
 NN = ((1,), (0,))
@@ -271,18 +270,21 @@
     return results
 
 
-def modes_of(source, twiddle):
+def modes_of(source, twiddle, turned=False):
     real, imag = [], []
     for k in range(9):
         c, s = twiddle[k : k + 1], twiddle[16 + k : 17 + k]
         z = source(k)
         re, im = z[:, :128], z[:, 128:]
         if k == 0:
-            real.append(re)
+            real.append(im if turned else re)
+            imag.append(None)
+            continue
+        real.append(im * c + re * s if turned else re * c - im * s)
+        if k == 8:
             imag.append(None)
         else:
-            real.append(re * c - im * s)
-            imag.append(None if k == 8 else re * s + im * c)
+            imag.append(im * s - re * c if turned else re * s + im * c)
     return real, imag
 
 
@@ -304,9 +306,43 @@
 
 
 def y_returned(pairs, radix, twiddle):
-    turned = [turn_by(pair[:, :128], pair[:, 128:], twiddle[0], -twiddle[1]) for pair in pairs]
-    right = [jnp.concatenate([pair[part] for pair in turned], axis=1) for part in range(2)]
-    return matmul_deep(radix, split(jnp.concatenate(right, axis=0)))
+    c, s = twiddle[0], twiddle[1]
+    real, imag = [], []
+    for pair, turned in pairs:
+        re, im = pair[:, :128], pair[:, 128:]
+        real.append(im * c + re * s if turned else re * c - im * s)
+        imag.append(im * s - re * c if turned else re * s + im * c)
+    right = jnp.concatenate([jnp.concatenate(real, axis=1), jnp.concatenate(imag, axis=1)], axis=0)
+    return matmul_deep(radix, split(right))
+
+
+def pack(tiles):
+    lane = lax.broadcasted_iota(jnp.int32, (1, 128), 1)
+    packed = [None] * 4
+    for jr, tile in enumerate(tiles):
+        index, offset = divmod(PIECE * jr, 128)
+        moved = pltpu.roll(tile, offset, 1) if offset else tile
+        parts = [(index, moved)]
+        if offset + PIECE > 128:
+            parts = [(index, jnp.where(lane >= offset, moved, 0.0))]
+            parts.append((index + 1, jnp.where(lane < offset, moved, 0.0)))
+        for own, part in parts:
+            if own < 4:
+                packed[own] = part if packed[own] is None else packed[own] + part
+    return packed
+
+
+def unpack(packed):
+    lane = lax.broadcasted_iota(jnp.int32, (1, 128), 1)
+    tiles = []
+    for jr in range(6):
+        index, offset = divmod(PIECE * jr, 128)
+        tile = packed[:, 128 * index : 128 * index + 128]
+        if offset + PIECE > 128:
+            later = packed[:, 128 * index + 128 : 128 * index + 256] if index < 3 else 0.0
+            tile = jnp.where(lane >= offset, tile, later)
+        tiles.append(pltpu.roll(tile, 128 - offset, 1) if offset else tile)
+    return tiles
 
 
 def y_waves(facts):
@@ -374,54 +410,36 @@
 
 
 def spectrum_kernel(in_ref, radix_ref, turn_ref, lanes_ref, facts_ref, spec_ref, used_ref):
-    turned = [split(pair) for pair in y_turned(in_ref, radix_ref, turn_ref)]
-    wave_y = y_waves(facts_ref[...])
-    for tile in range(4):
-        total = None
-        for index, (jr, own) in enumerate(TILES):
-            if own == tile:
-                part = matmul(turned[jr], [lanes_ref[0, index], lanes_ref[1, index]], NN)
-                total = part if total is None else total + part
-        lanes = slice(128 * tile, 128 * tile + 128)
-        total = jnp.where(wave_y[:, lanes] < KCUT, total, 0.0)
-        spec_ref[:, lanes] = total
-        used = min(USED - 128 * tile, 128)
-        used_ref[:, 128 * tile : 128 * tile + used] = total[:, :used]
+    turned = split(jnp.concatenate(y_turned(in_ref, radix_ref, turn_ref), axis=0))
+    spectrum = matmul(turned, lanes_ref, NN)
+    kept = y_waves(facts_ref[...]) < KCUT
+    tiles = [jnp.where(kept, spectrum[KAP * jr : KAP * jr + KAP], 0.0) for jr in range(6)]
+    spec_ref[...] = jnp.concatenate(tiles, axis=0)
+    for index, tile in enumerate(pack(tiles)):
+        used = min(USED - 128 * index, 128)
+        used_ref[:, 128 * index : 128 * index + used] = tile[:, :used]
 
 
 def stream_kernel(
-    weights_ref,
-    all_ref,
-    spec_ref,
-    unradix_ref,
-    turn_ref,
-    unlanes_ref,
-    unlanes_i_ref,
-    facts_ref,
-    out_ref,
-    stream_ref,
+    weights_ref, all_ref, spec_ref, unradix_ref, turn_ref, unlanes_ref, facts_ref, out_ref, stream_ref
 ):
-    facts = facts_ref[...]
-    wave_x = x_waves(facts, lax.axis_index("row"))
-    wave_y = y_waves(facts)
     stream = None
     for n in range(8):
         term = weights_ref[n] * all_ref[n]
         stream = term if stream is None else stream + term
-    stream_ref[:, SPAN - 128 :] = jnp.zeros((KAP, 128), F32)
+    stream_ref[:, 384:] = jnp.zeros((KAP, 128), F32)
     stream_ref[:, :USED] = stream
-    stream = stream_ref[...]
-    spectrum = spec_ref[...]
-    along_y = wave_y * half_of_zero(wave_x)
-    along_x = wave_x * half_of_zero(wave_y)
-    both_y = split(jnp.concatenate([-along_y * stream, along_y * spectrum], axis=0))
-    both_x = split(jnp.concatenate([along_x * stream, along_x * spectrum], axis=0))
-    pairs = []
-    for jr in range(6):
-        lanes = slice(128 * WINDOW[jr], 128 * WINDOW[jr] + 256)
-        for both, table in ((both_y, unlanes_i_ref), (both_x, unlanes_ref)):
-            out = matmul([part[:, lanes] for part in both], [table[0, jr], table[1, jr]], NN)
-            pairs += [out[:KAP], out[KAP:]]
+    facts = facts_ref[...]
+    wave_y = y_waves(facts)
+    once = half_of_zero(wave_y)
+    pieces = []
+    for jr, tile in enumerate(unpack(stream_ref[...])):
+        wave_x = x_waves(facts, lax.axis_index("row")) + 64 * jr
+        along_y, along_x = wave_y * half_of_zero(wave_x), wave_x * once
+        own = spec_ref[KAP * jr : KAP * jr + KAP, :]
+        pieces += [along_y * tile, -along_y * own, along_x * tile, along_x * own]
+    out = matmul_wide(split(jnp.concatenate(pieces, axis=0)), unlanes_ref)
+    pairs = [(out[KAP * i : KAP * i + KAP], i % 4 < 2) for i in range(24)]
     out = y_returned(pairs, unradix_ref, turn_ref)
     for jr in range(6):
         blocks = [out[:, 128 * (4 * jr + f) : 128 * (4 * jr + f) + 128] for f in range(4)]
@@ -430,42 +448,34 @@
             out_ref[pl.ds(4 * jr + jb, 64, stride=MINE), :] = block
 
 
-def jacobian_kernel(
-    in_ref, twiddle_ref, untable_ref, untable_i_ref, table_ref, out_ref, first0, first1, whole0, whole1, jac
-):
+def jacobian_kernel(in_ref, twiddle_ref, untable_ref, table_ref, out_ref, first_ref, whole_ref, jac):
     depth = 8 * MINE
-    lane = lax.broadcasted_iota(jnp.int32, (1, 128), 1)
     row = lax.broadcasted_iota(jnp.int32, (depth, 1), 0)
-    slots = [in_ref[depth * slot : depth * slot + depth, :] for slot in range(8)]
-    spare = jnp.zeros((8, 128), F32)
-    lower, upper = [], []
-    for a, b in zip(slots[0::2], slots[1::2]):
-        pair = [jnp.where(lane < 64, a, pltpu.roll(b, 64, 1)), jnp.where(lane < 64, pltpu.roll(a, 64, 1), b)]
-        lower.append(jnp.concatenate([pair[0], spare], axis=0))
-        upper.append(jnp.concatenate([pair[1], spare], axis=0))
-    own = jnp.concatenate([jnp.where(row < depth // 2, slots[0], 0.0), spare], axis=0)
-    own = split(own)
-    tables = [[ref[0], ref[1]] for ref in (untable_ref, untable_i_ref)]
-    first0[...] = matmul(own, tables[0], TN)
-    first1[...] = matmul(own, tables[1], TN)
-    whole0[...] = matmul(split(jnp.concatenate(lower, axis=1)), tables[0], TN)
-    whole1[...] = matmul(split(jnp.concatenate(upper, axis=1)), tables[1], TN)
+    spare = jnp.zeros((8, 4 * 128), F32)
+    table = [untable_ref[0], untable_ref[1]]
+    for part in range(2):
+        slots = [
+            in_ref[depth * slot : depth * slot + depth, :] for slot in range(4 * part, 4 * part + 4)
+        ]
+        side = jnp.concatenate([jnp.concatenate(slots, axis=1), spare], axis=0)
+        whole_ref[512 * part : 512 * part + 512, :] = matmul(split(side), table, TN)
+        if part == 0:
+            own = jnp.concatenate([jnp.where(row < depth // 2, slots[0], 0.0), spare[:, :128]], axis=0)
+            first_ref[...] = matmul(split(own), table, TN)
     twiddle = twiddle_ref[...]
     for block in range(4):
         rows = slice(8 * block, 8 * block + 8)
 
         def physical(field):
-            first, whole = ((first0, whole0), (first1, whole1))[field // 2]
-
             def source(k):
                 start = 32 * field + rows.start
                 if k == 0:
-                    return first[start : start + 8, :]
-                start = 32 * (field % 2) + 64 * (k % 8) + rows.start
-                z = whole[start : start + 8, :]
+                    return first_ref[start : start + 8, :]
+                start += 128 * (k % 8)
+                z = whole_ref[start : start + 8, :]
                 return z if k < 8 else z - source(0)
 
-            return real_synthesis(*modes_of(source, twiddle))
+            return real_synthesis(*modes_of(source, twiddle, field > 1))
 
         east, slope_x = physical(0), physical(3)
         product = [a * b for a, b in zip(east, slope_x)]
@@ -487,34 +497,36 @@
     in_ref, spec_ref, radix_ref, unradix_ref, turn_ref, project_ref, mean_ref, unlanes_ref, facts_ref, out_ref
 ):
     facts = facts_ref[...]
-    wave_x = x_waves(facts, lax.axis_index("row"))
     wave_y = y_waves(facts)
-    ratio = (wave_x * wave_x + wave_y * wave_y) * (1.0 / (KCUT * KCUT))
-    ratio = ratio * ratio
-    damped = split(((HYPER_RATE * (ratio * ratio)) * half_of_zero(wave_y)) * spec_ref[...])
+    once = half_of_zero(wave_y)
+    damped = []
+    for jr in range(6):
+        wave_x = x_waves(facts, lax.axis_index("row")) + 64 * jr
+        ratio = (wave_x * wave_x + wave_y * wave_y) * (1.0 / (KCUT * KCUT))
+        ratio = ratio * ratio
+        damped.append(((HYPER_RATE * (ratio * ratio)) * once) * spec_ref[KAP * jr : KAP * jr + KAP, :])
+    damping = matmul_wide(split(jnp.concatenate(damped, axis=0)), unlanes_ref)
     left = [split(pair) for pair in y_turned(in_ref, radix_ref, turn_ref)]
     sides = []
     for side in range(2):
         rows = slice(32 * side, 32 * side + 32)
         stacked = [jnp.concatenate([pair[i][rows] for pair in left], axis=0) for i in range(2)]
         sides.append(matmul(stacked, [project_ref[i, side] for i in range(2)], NN))
+    heads = [jnp.concatenate([pair[i][:16] for pair in left], axis=0) for i in range(2)]
+    mean = sum(
+        lax.dot_general(head, mean_ref[...], (NN, ((), ())), preferred_element_type=F32)
+        for head in heads
+    )
     first = lax.broadcasted_iota(jnp.int32, (16, 1), 0) == 0
     lane = lax.broadcasted_iota(jnp.int32, (1, 256), 1)
     zero_wave = (lax.axis_index("row") < 2) & (lane % 128 < 32)
     pairs = []
     for jr in range(6):
-        mean = sum(
-            lax.dot_general(
-                left[jr][i][:16], mean_ref[...], (NN, ((), ())), preferred_element_type=F32
-            )
-            for i in range(2)
-        )
         low, high = [side[32 * jr : 32 * jr + 32] for side in sides]
-        low = jnp.concatenate([low[:16] - jnp.where(first, mean, 0.0), low[16:]], axis=0)
-        window = [part[:, 128 * WINDOW[jr] : 128 * WINDOW[jr] + 256] for part in damped]
-        damping = matmul(window, [unlanes_ref[i, jr] for i in range(2)], NN)
-        total = jnp.concatenate([low, high], axis=0) + damping
-        pairs.append(total * jnp.where(zero_wave, -0.5, -1.0) if jr == 0 else -total)
+        own = jnp.where(first, mean[16 * jr : 16 * jr + 16], 0.0)
+        flux = jnp.concatenate([low[:16] - own, low[16:], high], axis=0)
+        total = flux - damping[KAP * jr : KAP * jr + KAP]
+        pairs.append((total * jnp.where(zero_wave, 0.5, 1.0) if jr == 0 else total, False))
     out = y_returned(pairs, unradix_ref, turn_ref)
     for jr in range(6):
         out_ref[pl.ds(jr, 64, stride=CHUNK), :] = out[:, 128 * jr : 128 * jr + 128]
@@ -604,29 +616,28 @@
     devices = lax.axis_size("row")
     turn_x = jnp.asarray(x_twiddle())
     forward_x = jnp.asarray(x_forward_table())
-    inverse_x = jnp.asarray(x_inverse_table(False, False))
-    inverse_ix = jnp.asarray(x_inverse_table(False, True))
-    inverse_chunk = jnp.asarray(x_inverse_table(True, False))
+    inverse_x = jnp.asarray(x_inverse_table(False))
+    inverse_chunk = jnp.asarray(x_inverse_table(True))
     radix = jnp.asarray(y_radix_table())
     unradix = jnp.asarray(y_radix_inverse_table())
     turn_y = jnp.asarray(y_twiddle())
     lanes = jnp.asarray(y_lane_table())
-    unlanes = jnp.asarray(y_lane_inverse_table(False))
-    unlanes_i = jnp.asarray(y_lane_inverse_table(True))
+    unlanes = jnp.asarray(y_lane_inverse_table())
     project = jnp.asarray(y_projection_table())
     mean = jnp.asarray(y_mean_table())
-    facts = jnp.asarray(lane_facts())
+    facts = jnp.asarray(lane_facts(False))
+    packed_facts = jnp.asarray(lane_facts(True))
 
     one, four = (64 * CHUNK, 128), (64 * MINE, 128)
     (columns,) = call(state_kernel, [one], [state, turn_x, forward_x], far_in=True, far_out=True, copies=5)
     columns = exchange(columns, devices)
     spectrum, used = call(
-        spectrum_kernel, [(KAP, SPAN), (KAP, USED)], [columns, radix, turn_y, lanes, facts]
+        spectrum_kernel, [(6 * KAP, 128), (KAP, USED)], [columns, radix, turn_y, lanes, facts]
     )
     (weights,) = call(
         weights_kernel,
         [(8, KAP, USED)],
-        [to_modes, from_modes, deform, facts],
+        [to_modes, from_modes, deform, packed_facts],
         scalars=3,
         cost=pl.CostEstimate(flops=8_000_000, bytes_accessed=2_000_000, transcendentals=0),
     )
@@ -634,15 +645,15 @@
     (fields,) = call(
         stream_kernel,
         [four],
-        [weights, gathered, spectrum, unradix, turn_y, unlanes, unlanes_i, facts],
-        scratch=[(KAP, SPAN)],
+        [weights, gathered, spectrum, unradix, turn_y, unlanes, facts],
+        scratch=[(KAP, 512)],
     )
     fields = exchange(fields, devices)
     (flux,) = call(
         jacobian_kernel,
         [one],
-        [fields, turn_x, inverse_x, inverse_ix, forward_x],
-        scratch=[(128, 256)] * 2 + [(512, 256)] * 2 + [(2, 9, ROWS, 128)],
+        [fields, turn_x, inverse_x, forward_x],
+        scratch=[(128, 256), (1024, 256), (2, 9, ROWS, 128)],
     )
     flux = exchange(flux, devices)
     (total,) = call(

time: 119 us -> 116 us (0.975)
  local copies, waits for them, and re-layouts: 5.49 us -> 0.11 us
  waiting for transfers between devices: 6.89 us -> 9.56 us
    unnamed x40 -> x36, local copies, waits for them, and re-layouts: 5.49 us -> 0.11 us
    all_to_all x1, waiting for transfers between devices: 6.89 us -> 9.56 us  [exchange(): lax.all_to_all(sent, 'row', split_axis=0, concat_axis=0, tiled=True)]
where the time goes in v7:
time: 116 us
  blocking collectives  83.1 us (72%)
  starting transfers between devices  12.5 us (11%)
  Pallas kernels  9.62 us (8%)
  waiting for transfers between devices  9.56 us (8%)
    all_to_all x3, blocking collectives, exchange(): lax.all_to_all(sent, 'row', split_axis=0, concat_axis=0, tiled=True)  60.2 us
    all_gather x1, blocking collectives, per_device(): gathered = lax.all_gather(used, 'layer', axis=0, tiled=False)  22.9 us
    all_to_all x1, starting transfers between devices, exchange(): lax.all_to_all(sent, 'row', split_axis=0, concat_axis=0, tiled=True)  12.5 us
    pallas_call x7, Pallas kernels, call(): pl.pallas_call(kernel, out_shape=[jax.ShapeDtypeStruct(shape, F32) for sh...  9.62 us
    all_to_all x1, waiting for transfers between devices, exchange(): lax.all_to_all(sent, 'row', split_axis=0, concat_axis=0, tiled=True)  9.56 us
  transfers between devices with their start and end apart: 1, of which 1 were waited for; matrix products, arithmetic and copies ran while one was open for 0% of the time, Pallas kernels for 1%

profile of v7, /device:TPU:8, one launch (start us, length us, event | category | flops | bytes accessed | tf_op | source)
XLA Modules:
  0.0 115.8 jit_solution(4598773420224518557)
XLA Ops:
  0.6 2.3 %shard_map.186 = f32[384,128]{1,0:T(8,128)} custom-call(f32[1,32,2048]{2,1,0:T(8,128)} %state_ref.1, f32[32,128]{1,0:T(8,128)} %constant.26.clone.twiddle_hbm.twiddle_ref, bf16[2,2,128,256]{3,2,1,0:T(8,128)(2,1)} %constant.27.clone.table_hbm.table_ref), custom_call_target="tpu_custom_call" | custom-call | tf_op jit(solution)/shard_map/pallas_call | solution.py:598
  3.0 0.0 copy-start.14
  3.0 0.0 copy-start.15
  3.0 0.0 copy-start.16
  3.0 0.0 copy-start.17
  3.0 12.5 %all-to-all-start = ((f32[64,1,768]{2,1,0:T(1,128)}), f32[64,1,768]{2,1,0:T(1,128)S(1)}, u32[]{:S(2)}, u32[]{:S(2)}) async-start(f32[64,1,768]{2,1,0:T(1,128)} %bitcast.17), calls=%async_computation | async-start | bytes 393216 | tf_op jit(solution)/shard_map/all_to_all | solution.py:612
  15.5 0.0 copy-done.14
  15.6 0.0 copy-start.3
  15.6 0.0 copy-start.6
  15.6 0.0 copy-start.12
  15.6 0.0 copy-start.13
  15.6 1.4 %shard_map.185.weights_ref = f32[8,64,462]{2,1,0:T(8,128)S(1)} custom-call(f32[8,8]{1,0:T(8,128)S(1)} %copy-done.15, f32[8,8]{1,0:T(8,128)S(1)} %copy-done.16, f32[8]{0:T(128)S(1)} %copy-done.17, f32[8,512]{1,0:T(8,128)S(1)} %copy-done.14), custom_call_target="tpu_custom_call" | custom-call | flops 8000000 | bytes 2000000 | tf_op jit(solution)/shard_map/pallas_call | solution.py:598
  17.0 9.6 %all-to-all-done = f32[64,1,768]{2,1,0:T(1,128)S(1)} async-done(((f32[64,1,768]{2,1,0:T(1,128)}), f32[64,1,768]{2,1,0:T(1,128)S(1)}, u32[]{:S(2)}, u32[]{:S(2)}) %all-to-all-start) | async-done | bytes 196640 | tf_op jit(solution)/shard_map/all_to_all | solution.py:612
  26.6 0.6 shard_map.187
  27.2 0.0 copy-start.2
  27.2 0.0 copy-start.8
  27.2 22.9 %all-gather = f32[512,462]{1,0:T(8,128)S(1)} all-gather(f32[64,462]{1,0:T(8,128)S(1)} %get-tuple-element.4), channel_id=2, replica_groups=mesh['layer'=8,'row'=64] {'layer'}, dimensions={0}, use_global_device_ids=true | all-gather | bytes 1064448 | tf_op jit(solution)/shard_map/all_gather | solution.py:644
  50.1 1.7 %shard_map.188 = f32[1344,128]{1,0:T(8,128)S(1)} custom-call(f32[8,64,462]{2,1,0:T(8,128)S(1)} %shard_map.185.weights_ref, f32[8,64,462]{2,1,0:T(8,128)S(1)} %bitcast.9, f32[384,128]{1,0:T(8,128)S(1)} %get-tuple-element.5.spec_ref, bf16[64,384]{1,0:T(8,128)(2,1)S(1)} %copy-done.8, f32[2,64,128]{2,1,0:T(8,128)S(1)} %copy-done.3, ...), custom_call_target="tpu_custom_call" | custom-call | tf_op jit(solution)/shard_map/pallas_call | solution.py:598
  51.8 0.0 copy-start.1
  51.8 0.0 copy-start.9
  51.9 0.0 copy-start.10
  51.9 26.3 %all_to_all.20 = f32[64,1,2688]{2,1,0:T(1,128)S(1)} all-to-all(f32[64,1,2688]{2,1,0:T(1,128)S(1)} %bitcast.10), channel_id=1, replica_groups=mesh['layer'=8,'row'=64] {'row'}, dimensions={0} | all-to-all | bytes 1376256 | tf_op jit(solution)/shard_map/all_to_all | solution.py:612
  78.2 0.0 copy-done.1
  78.2 0.0 copy-start.4
  78.2 1.5 %shard_map.189 = f32[384,128]{1,0:T(8,128)S(1)} custom-call(f32[1344,128]{1,0:T(8,128)S(1)} %bitcast.11, f32[32,128]{1,0:T(8,128)S(1)} %copy-done.10, bf16[2,176,256]{2,1,0:T(8,128)(2,1)S(1)} %copy-done.9, bf16[2,2,128,256]{3,2,1,0:T(8,128)(2,1)S(1)} %copy-done.1), custom_call_target="tpu_custom_call" | custom-call | tf_op jit(solution)/shard_map/pallas_call | solution.py:598
  79.7 0.0 copy-start.11
  79.7 17.9 %all_to_all.21 = f32[64,1,768]{2,1,0:T(1,128)S(1)} all-to-all(f32[64,1,768]{2,1,0:T(1,128)S(1)} %bitcast.16), channel_id=1, replica_groups=mesh['layer'=8,'row'=64] {'row'}, dimensions={0} | all-to-all | bytes 393216 | tf_op jit(solution)/shard_map/all_to_all | solution.py:612
  97.7 0.8 shard_map.190
  98.5 0.0 copy-start
  98.5 15.9 %all_to_all.22 = f32[64,1,768]{2,1,0:T(1,128)S(1)} all-to-all(f32[64,1,768]{2,1,0:T(1,128)S(1)} %bitcast.14), channel_id=1, replica_groups=mesh['layer'=8,'row'=64] {'row'}, dimensions={0} | all-to-all | bytes 393216 | tf_op jit(solution)/shard_map/all_to_all | solution.py:612
  114.4 0.0 copy-done.5
  114.4 1.4 %shard_map.191 = (f32[1,32,2048]{2,1,0:T(8,128)}, f32[1,32,2048]{2,1,0:T(8,128)}) custom-call(f32[384,128]{1,0:T(8,128)S(1)} %bitcast.15, f32[1,32,2048]{2,1,0:T(8,128)S(1)} %copy-done, f32[1,32,2048]{2,1,0:T(8,128)S(1)} %copy-done.5, f32[32,128]{1,0:T(8,128)S(1)} %copy-done.10, bf16[2,192,256]{2,1,0:T(8,128)(2,1)S(1)} %copy-done.7), custom_call_target="tpu_custom_call" | custom-call | tf_op jit(solution)/shard_map/pallas_call | solution.py:598
  (17 shorter events, 0.0 us)
Async XLA Ops:
  3.0 12.6 %copy-start.14 = (f32[8,512]{1,0:T(8,128)S(1)}, f32[8,512]{1,0:T(8,128)}, u32[]{:S(2)}) copy-start(f32[8,512]{1,0:T(8,128)} %constant.38.clone.facts_ref) | copy-start | bytes 49156
  3.0 12.6 %copy-start.15 = (f32[8,8]{1,0:T(8,128)S(1)}, f32[8,8]{1,0:T(8,128)}, u32[]{:S(2)}) copy-start(f32[8,8]{1,0:T(8,128)} %to_ref.1) | copy-start | bytes 772
  3.0 12.6 %copy-start.16 = (f32[8,8]{1,0:T(8,128)S(1)}, f32[8,8]{1,0:T(8,128)}, u32[]{:S(2)}) copy-start(f32[8,8]{1,0:T(8,128)} %from_ref.1) | copy-start | bytes 772
  3.0 12.6 %copy-start.17 = (f32[8]{0:T(128)S(1)}, f32[8]{0:T(128)}, u32[]{:S(2)}) copy-start(f32[8]{0:T(128)} %deform_ref.1) | copy-start | bytes 100
  3.0 23.6 %all-to-all-start = ((f32[64,1,768]{2,1,0:T(1,128)}), f32[64,1,768]{2,1,0:T(1,128)S(1)}, u32[]{:S(2)}, u32[]{:S(2)}) async-start(f32[64,1,768]{2,1,0:T(1,128)} %bitcast.17), calls=%async_computation | async-start | bytes 393216 | tf_op jit(solution)/shard_map/all_to_all | solution.py:612
  15.6 11.0 %copy-start.3 = (f32[2,64,128]{2,1,0:T(8,128)S(1)}, f32[2,64,128]{2,1,0:T(8,128)}, u32[]{:S(2)}) copy-start(f32[2,64,128]{2,1,0:T(8,128)} %constant.32.clone.turn_ref) | copy-start | bytes 196612
  15.6 11.0 %copy-start.6 = (bf16[128,192]{1,0:T(8,128)(2,1)S(1)}, bf16[128,192]{1,0:T(8,128)(2,1)}, u32[]{:S(2)}) copy-start(bf16[128,192]{1,0:T(8,128)(2,1)} %constant.30.clone.radix_ref) | copy-start | bytes 147460
  15.6 11.0 %copy-start.12 = (bf16[2,256,128]{2,1,0:T(8,128)(2,1)S(1)}, bf16[2,256,128]{2,1,0:T(8,128)(2,1)}, u32[]{:S(2)}) copy-start(bf16[2,256,128]{2,1,0:T(8,128)(2,1)} %constant.33.clone.lanes_ref) | copy-start | bytes 393220
  15.6 11.0 %copy-start.13 = (f32[8,128]{1,0:T(8,128)S(1)}, f32[8,128]{1,0:T(8,128)}, u32[]{:S(2)}) copy-start(f32[8,128]{1,0:T(8,128)} %constant.37.clone.facts_ref) | copy-start | bytes 12292
  27.2 22.9 %copy-start.2 = (bf16[384,256]{1,0:T(8,128)(2,1)S(1)}, bf16[384,256]{1,0:T(8,128)(2,1)}, u32[]{:S(2)}) copy-start(bf16[384,256]{1,0:T(8,128)(2,1)} %constant.34.clone.unlanes_ref) | copy-start | bytes 589828
  27.2 22.9 %copy-start.8 = (bf16[64,384]{1,0:T(8,128)(2,1)S(1)}, bf16[64,384]{1,0:T(8,128)(2,1)}, u32[]{:S(2)}) copy-start(bf16[64,384]{1,0:T(8,128)(2,1)} %constant.31.clone.unradix_ref) | copy-start | bytes 147460
  51.8 26.4 %copy-start.1 = (bf16[2,2,128,256]{3,2,1,0:T(8,128)(2,1)S(1)}, bf16[2,2,128,256]{3,2,1,0:T(8,128)(2,1)}, u32[]{:S(2)}) copy-start(bf16[2,2,128,256]{3,2,1,0:T(8,128)(2,1)} %constant.27.clone.table_hbm.table_ref) | copy-start | bytes 786436
  51.8 26.4 %copy-start.9 = (bf16[2,176,256]{2,1,0:T(8,128)(2,1)S(1)}, bf16[2,176,256]{2,1,0:T(8,128)(2,1)}, u32[]{:S(2)}) copy-start(bf16[2,176,256]{2,1,0:T(8,128)(2,1)} %constant.28.clone.untable_ref) | copy-start | bytes 540676
  51.9 26.4 %copy-start.10 = (f32[32,128]{1,0:T(8,128)S(1)}, f32[32,128]{1,0:T(8,128)}, u32[]{:S(2)}) copy-start(f32[32,128]{1,0:T(8,128)} %constant.26.clone.twiddle_hbm.twiddle_ref) | copy-start | bytes 49156
  78.2 19.5 %copy-start.4 = (bf16[2,2,256,256]{3,2,1,0:T(8,128)(2,1)S(1)}, bf16[2,2,256,256]{3,2,1,0:T(8,128)(2,1)}, u32[]{:S(2)}) copy-start(bf16[2,2,256,256]{3,2,1,0:T(8,128)(2,1)} %constant.35.clone.project_ref) | copy-start | bytes 1572868
  79.7 18.0 %copy-start.11 = (bf16[256,256]{1,0:T(8,128)(2,1)S(1)}, bf16[256,256]{1,0:T(8,128)(2,1)}, u32[]{:S(2)}) copy-start(bf16[256,256]{1,0:T(8,128)(2,1)} %constant.36.clone.mean_ref) | copy-start | bytes 393220
  97.7 16.7 %copy-start.5 = (f32[1,32,2048]{2,1,0:T(8,128)S(1)}, f32[1,32,2048]{2,1,0:T(8,128)}, u32[]{:S(2)}) copy-start(f32[1,32,2048]{2,1,0:T(8,128)} %start_ref.1) | copy-start | bytes 786436
  97.7 16.7 %copy-start.7 = (bf16[2,192,256]{2,1,0:T(8,128)(2,1)S(1)}, bf16[2,192,256]{2,1,0:T(8,128)(2,1)}, u32[]{:S(2)}) copy-start(bf16[2,192,256]{2,1,0:T(8,128)(2,1)} %constant.29.clone.untable_ref) | copy-start | bytes 589828
  98.5 15.9 %copy-start = (f32[1,32,2048]{2,1,0:T(8,128)S(1)}, f32[1,32,2048]{2,1,0:T(8,128)}, u32[]{:S(2)}) copy-start(f32[1,32,2048]{2,1,0:T(8,128)} %state_ref.1) | copy-start | bytes 786436

commit v8 on v7

--- a/solution.py
+++ b/solution.py
@@ -42,13 +42,13 @@
 
 def x_forward_table():
     b = np.arange(128)
-    table = np.zeros((2, 4, 2, 2, 8, 2, 128))
+    table = np.zeros((2, 4, 2, 2, 6, 2, 128))
     for h in range(4):
         for i in range(MINE):
             c, s = turn(column_j(h, i) * b, 128)
             own = table[h // 2, i % 4, h % 2, :, i // 4]
             own[0, 0], own[0, 1], own[1, 0], own[1, 1] = c, s, -s, c
-    return halves(table.reshape(2, 128, 256))
+    return np.concatenate(list(halves(table.reshape(2, 96, 256))), axis=1)
 
 
 def x_inverse_table(by_chunk):
@@ -80,7 +80,7 @@
 def y_radix_inverse_table():
     c, s = turn(np.arange(64)[:, None] * np.arange(KAP)[None, :], 64)
     high, low = halves(np.concatenate([c, -s], axis=1))
-    return np.concatenate([high, high, low], axis=1)
+    return np.block([[high, high], [low, np.zeros_like(low)]])
 
 
 def y_twiddle():
@@ -100,7 +100,7 @@
 
 
 def y_lane_table():
-    return halves(lanes_of())
+    return np.concatenate(list(halves(lanes_of())), axis=1)
 
 
 def y_lane_inverse_table():
@@ -136,31 +136,30 @@
     return high, low
 
 
+def dot(a, b, dims):
+    return lax.dot_general(a, b, (dims, ((), ())), preferred_element_type=F32)
+
+
 def matmul(left, right, dims):
-    def one(a, b):
-        return lax.dot_general(a, b, (dims, ((), ())), preferred_element_type=F32)
-
-    return one(left[0], right[0]) + (one(left[0], right[1]) + one(left[1], right[0]))
-
-
-def matmul_deep(table, right):
-    depth = right[0].shape[0]
-
-    def one(a, b):
-        return lax.dot_general(a, b, (NN, ((), ())), preferred_element_type=F32)
-
-    both = jnp.concatenate(right, axis=0)
-    return one(table[:, : 2 * depth], both) + one(table[:, 2 * depth :], right[0])
+    return dot(left[0], right[0], dims) + (dot(left[0], right[1], dims) + dot(left[1], right[0], dims))
+
+
+def matmul_tall(table, right):
+    out = dot(table[...], jnp.concatenate(right, axis=0), NN)
+    size = table.shape[0] // 2
+    return out[:size] + out[size:]
 
 
 def matmul_wide(left, table):
     depth = left[0].shape[1]
-
-    def one(a, b):
-        return lax.dot_general(a, b, (NN, ((), ())), preferred_element_type=F32)
-
     both = jnp.concatenate(left, axis=1)
-    return one(both, table[: 2 * depth]) + one(left[0], table[2 * depth :])
+    return dot(both, table[: 2 * depth], NN) + dot(left[0], table[2 * depth :], NN)
+
+
+def matmul_beside(left, table):
+    size = table.shape[1] // 2
+    out = dot(left[0], table[...], NN)
+    return out[:, :size] + (out[:, size:] + dot(left[1], table[:, :size], NN))
 
 
 NN = ((1,), (0,))
@@ -266,7 +265,8 @@
     for half, own in enumerate((pieces[0], pieces[8])):
         own = split(own)
         right = [jnp.concatenate([own[i], shared[i]], axis=0) for i in range(2)]
-        results.append(matmul([table[0, half], table[1, half]], right, NT))
+        out = dot(table[half], right[0], NT)
+        results.append(out[:96] + (out[96:] + dot(table[half, :96], right[1], NT)))
     return results
 
 
@@ -291,12 +291,7 @@
 def y_turned(in_ref, radix, twiddle):
     columns = [in_ref[pl.ds(jr, 64, stride=CHUNK), :] for jr in range(6)]
     high, low = split(jnp.concatenate(columns, axis=1))
-    mixed = lax.dot_general(
-        radix[...],
-        jnp.concatenate([high, low, high], axis=0),
-        (NN, ((), ())),
-        preferred_element_type=F32,
-    )
+    mixed = dot(radix[...], jnp.concatenate([high, low, high], axis=0), NN)
     results = []
     for jr in range(6):
         lanes = slice(128 * jr, 128 * jr + 128)
@@ -313,7 +308,7 @@
         real.append(im * c + re * s if turned else re * c - im * s)
         imag.append(im * s - re * c if turned else re * s + im * c)
     right = jnp.concatenate([jnp.concatenate(real, axis=1), jnp.concatenate(imag, axis=1)], axis=0)
-    return matmul_deep(radix, split(right))
+    return matmul_tall(radix, split(right))
 
 
 def pack(tiles):
@@ -364,11 +359,10 @@
 def store_x(out_ref, results, group):
     for half in range(2):
         lanes = slice(128 * group, 128 * group + 128)
-        blocks = [results[half][32 * jb : 32 * jb + 32, lanes] for jb in range(4)]
+        blocks = [results[half][24 * jb : 24 * jb + 24, lanes] for jb in range(4)]
         for slot, block in enumerate(regroup(blocks, range(4))):
-            for own in range(4):
-                start = (8 * (4 * group + slot) + 4 * half + own) * CHUNK
-                out_ref[start : start + CHUNK, :] = block[8 * own : 8 * own + CHUNK]
+            start = (8 * (4 * group + slot) + 4 * half) * CHUNK
+            out_ref[start : start + 4 * CHUNK, :] = block
 
 
 def state_kernel(
@@ -411,7 +405,7 @@
 
 def spectrum_kernel(in_ref, radix_ref, turn_ref, lanes_ref, facts_ref, spec_ref, used_ref):
     turned = split(jnp.concatenate(y_turned(in_ref, radix_ref, turn_ref), axis=0))
-    spectrum = matmul(turned, lanes_ref, NN)
+    spectrum = matmul_beside(turned, lanes_ref)
     kept = y_waves(facts_ref[...]) < KCUT
     tiles = [jnp.where(kept, spectrum[KAP * jr : KAP * jr + KAP], 0.0) for jr in range(6)]
     spec_ref[...] = jnp.concatenate(tiles, axis=0)
@@ -513,10 +507,7 @@
         stacked = [jnp.concatenate([pair[i][rows] for pair in left], axis=0) for i in range(2)]
         sides.append(matmul(stacked, [project_ref[i, side] for i in range(2)], NN))
     heads = [jnp.concatenate([pair[i][:16] for pair in left], axis=0) for i in range(2)]
-    mean = sum(
-        lax.dot_general(head, mean_ref[...], (NN, ((), ())), preferred_element_type=F32)
-        for head in heads
-    )
+    mean = dot(heads[0], mean_ref[...], NN) + dot(heads[1], mean_ref[...], NN)
     first = lax.broadcasted_iota(jnp.int32, (16, 1), 0) == 0
     lane = lax.broadcasted_iota(jnp.int32, (1, 256), 1)
     zero_wave = (lax.axis_index("row") < 2) & (lane % 128 < 32)

time: 116 us -> 115 us (level)
  no operation moved by 1% of the time
where the time goes in v8:
time: 115 us
  blocking collectives  83.1 us (72%)
  starting transfers between devices  12.5 us (11%)
  waiting for transfers between devices  9.56 us (8%)
  Pallas kernels  8.79 us (8%)
    all_to_all x3, blocking collectives, exchange(): lax.all_to_all(sent, 'row', split_axis=0, concat_axis=0, tiled=True)  60.2 us
    all_gather x1, blocking collectives, per_device(): gathered = lax.all_gather(used, 'layer', axis=0, tiled=False)  22.9 us
    all_to_all x1, starting transfers between devices, exchange(): lax.all_to_all(sent, 'row', split_axis=0, concat_axis=0, tiled=True)  12.5 us
    all_to_all x1, waiting for transfers between devices, exchange(): lax.all_to_all(sent, 'row', split_axis=0, concat_axis=0, tiled=True)  9.56 us
    pallas_call x7, Pallas kernels, call(): pl.pallas_call(kernel, out_shape=[jax.ShapeDtypeStruct(shape, F32) for sh...  8.79 us
  transfers between devices with their start and end apart: 1, of which 1 were waited for; matrix products, arithmetic and copies ran while one was open for 0% of the time, Pallas kernels for 1%

profile of v8, /device:TPU:8, one launch (start us, length us, event | category | flops | bytes accessed | tf_op | source)
XLA Modules:
  0.0 114.9 jit_solution(2835886507904492259)
XLA Ops:
  0.6 2.2 %shard_map.186 = f32[384,128]{1,0:T(8,128)} custom-call(f32[1,32,2048]{2,1,0:T(8,128)} %state_ref.1, f32[32,128]{1,0:T(8,128)} %constant.26.clone.twiddle_hbm.twiddle_ref, bf16[2,192,256]{2,1,0:T(8,128)(2,1)} %constant.27.clone.table_hbm.table_ref), custom_call_target="tpu_custom_call" | custom-call | tf_op jit(solution)/shard_map/pallas_call | solution.py:589
  2.8 0.0 copy-start.14
  2.9 0.0 copy-start.15
  2.9 0.0 copy-start.16
  2.9 0.0 copy-start.17
  2.9 12.5 %all-to-all-start = ((f32[64,1,768]{2,1,0:T(1,128)}), f32[64,1,768]{2,1,0:T(1,128)S(1)}, u32[]{:S(2)}, u32[]{:S(2)}) async-start(f32[64,1,768]{2,1,0:T(1,128)} %bitcast.17), calls=%async_computation | async-start | bytes 393216 | tf_op jit(solution)/shard_map/all_to_all | solution.py:603
  15.5 0.0 copy-start.3
  15.5 0.0 copy-start.6
  15.5 0.0 copy-start.12
  15.5 0.0 copy-start.13
  15.5 1.4 %shard_map.185.weights_ref = f32[8,64,462]{2,1,0:T(8,128)S(1)} custom-call(f32[8,8]{1,0:T(8,128)S(1)} %copy-done.15, f32[8,8]{1,0:T(8,128)S(1)} %copy-done.16, f32[8]{0:T(128)S(1)} %copy-done.17, f32[8,512]{1,0:T(8,128)S(1)} %copy-done.14), custom_call_target="tpu_custom_call" | custom-call | flops 8000000 | bytes 2000000 | tf_op jit(solution)/shard_map/pallas_call | solution.py:589
  16.9 9.6 %all-to-all-done = f32[64,1,768]{2,1,0:T(1,128)S(1)} async-done(((f32[64,1,768]{2,1,0:T(1,128)}), f32[64,1,768]{2,1,0:T(1,128)S(1)}, u32[]{:S(2)}, u32[]{:S(2)}) %all-to-all-start) | async-done | bytes 196640 | tf_op jit(solution)/shard_map/all_to_all | solution.py:603
  26.5 0.0 copy-done.12
  26.5 0.0 copy-done.13
  26.5 0.5 shard_map.187
  27.0 0.0 copy-start.1
  27.0 0.0 copy-start.7
  27.0 22.9 %all-gather = f32[512,462]{1,0:T(8,128)S(1)} all-gather(f32[64,462]{1,0:T(8,128)S(1)} %get-tuple-element.4), channel_id=2, replica_groups=mesh['layer'=8,'row'=64] {'layer'}, dimensions={0}, use_global_device_ids=true | all-gather | bytes 1064448 | tf_op jit(solution)/shard_map/all_gather | solution.py:635
  49.9 0.0 copy-done.7
  49.9 1.2 %shard_map.188 = f32[1344,128]{1,0:T(8,128)S(1)} custom-call(f32[8,64,462]{2,1,0:T(8,128)S(1)} %shard_map.185.weights_ref, f32[8,64,462]{2,1,0:T(8,128)S(1)} %bitcast.9, f32[384,128]{1,0:T(8,128)S(1)} %get-tuple-element.5.spec_ref, bf16[128,256]{1,0:T(8,128)(2,1)S(1)} %copy-done.7, f32[2,64,128]{2,1,0:T(8,128)S(1)} %copy-done.3, ...), custom_call_target="tpu_custom_call" | custom-call | tf_op jit(solution)/shard_map/pallas_call | solution.py:589
  51.1 0.0 copy-start.9
  51.1 0.0 copy-start.10
  51.2 26.3 %all_to_all.20 = f32[64,1,2688]{2,1,0:T(1,128)S(1)} all-to-all(f32[64,1,2688]{2,1,0:T(1,128)S(1)} %bitcast.11), channel_id=1, replica_groups=mesh['layer'=8,'row'=64] {'row'}, dimensions={0} | all-to-all | bytes 1376256 | tf_op jit(solution)/shard_map/all_to_all | solution.py:603
  77.5 0.0 copy-done.10
  77.5 0.0 copy-start.4
  77.5 1.4 %shard_map.189 = f32[384,128]{1,0:T(8,128)S(1)} custom-call(f32[1344,128]{1,0:T(8,128)S(1)} %bitcast.10, f32[32,128]{1,0:T(8,128)S(1)} %copy-done.10, bf16[2,176,256]{2,1,0:T(8,128)(2,1)S(1)} %copy-done.9, bf16[2,192,256]{2,1,0:T(8,128)(2,1)S(1)} %copy-done.2), custom_call_target="tpu_custom_call" | custom-call | tf_op jit(solution)/shard_map/pallas_call | solution.py:589
  78.9 0.0 copy-start.11
  78.9 18.0 %all_to_all.21 = f32[64,1,768]{2,1,0:T(1,128)S(1)} all-to-all(f32[64,1,768]{2,1,0:T(1,128)S(1)} %bitcast.16), channel_id=1, replica_groups=mesh['layer'=8,'row'=64] {'row'}, dimensions={0} | all-to-all | bytes 393216 | tf_op jit(solution)/shard_map/all_to_all | solution.py:603
  96.9 0.8 shard_map.190
  97.6 0.0 copy-start
  97.6 15.9 %all_to_all.22 = f32[64,1,768]{2,1,0:T(1,128)S(1)} all-to-all(f32[64,1,768]{2,1,0:T(1,128)S(1)} %bitcast.14), channel_id=1, replica_groups=mesh['layer'=8,'row'=64] {'row'}, dimensions={0} | all-to-all | bytes 393216 | tf_op jit(solution)/shard_map/all_to_all | solution.py:603
  113.5 1.4 %shard_map.191 = (f32[1,32,2048]{2,1,0:T(8,128)}, f32[1,32,2048]{2,1,0:T(8,128)}) custom-call(f32[384,128]{1,0:T(8,128)S(1)} %bitcast.15, f32[1,32,2048]{2,1,0:T(8,128)S(1)} %copy-done, f32[1,32,2048]{2,1,0:T(8,128)S(1)} %copy-done.5, f32[32,128]{1,0:T(8,128)S(1)} %copy-done.10, bf16[2,192,256]{2,1,0:T(8,128)(2,1)S(1)} %copy-done.8), custom_call_target="tpu_custom_call" | custom-call | tf_op jit(solution)/shard_map/pallas_call | solution.py:589
  (17 shorter events, 0.0 us)
Async XLA Ops:
  2.8 12.6 %copy-start.14 = (f32[8,512]{1,0:T(8,128)S(1)}, f32[8,512]{1,0:T(8,128)}, u32[]{:S(2)}) copy-start(f32[8,512]{1,0:T(8,128)} %constant.38.clone.facts_ref) | copy-start | bytes 49156
  2.9 12.6 %copy-start.15 = (f32[8,8]{1,0:T(8,128)S(1)}, f32[8,8]{1,0:T(8,128)}, u32[]{:S(2)}) copy-start(f32[8,8]{1,0:T(8,128)} %to_ref.1) | copy-start | bytes 772
  2.9 12.6 %copy-start.16 = (f32[8,8]{1,0:T(8,128)S(1)}, f32[8,8]{1,0:T(8,128)}, u32[]{:S(2)}) copy-start(f32[8,8]{1,0:T(8,128)} %from_ref.1) | copy-start | bytes 772
  2.9 12.6 %copy-start.17 = (f32[8]{0:T(128)S(1)}, f32[8]{0:T(128)}, u32[]{:S(2)}) copy-start(f32[8]{0:T(128)} %deform_ref.1) | copy-start | bytes 100
  2.9 23.6 %all-to-all-start = ((f32[64,1,768]{2,1,0:T(1,128)}), f32[64,1,768]{2,1,0:T(1,128)S(1)}, u32[]{:S(2)}, u32[]{:S(2)}) async-start(f32[64,1,768]{2,1,0:T(1,128)} %bitcast.17), calls=%async_computation | async-start | bytes 393216 | tf_op jit(solution)/shard_map/all_to_all | solution.py:603
  15.5 11.0 %copy-start.3 = (f32[2,64,128]{2,1,0:T(8,128)S(1)}, f32[2,64,128]{2,1,0:T(8,128)}, u32[]{:S(2)}) copy-start(f32[2,64,128]{2,1,0:T(8,128)} %constant.32.clone.turn_ref) | copy-start | bytes 196612
  15.5 11.0 %copy-start.6 = (bf16[128,192]{1,0:T(8,128)(2,1)S(1)}, bf16[128,192]{1,0:T(8,128)(2,1)}, u32[]{:S(2)}) copy-start(bf16[128,192]{1,0:T(8,128)(2,1)} %constant.30.clone.radix_ref) | copy-start | bytes 147460
  15.5 11.0 %copy-start.12 = (bf16[256,256]{1,0:T(8,128)(2,1)S(1)}, bf16[256,256]{1,0:T(8,128)(2,1)}, u32[]{:S(2)}) copy-start(bf16[256,256]{1,0:T(8,128)(2,1)} %constant.33.clone.lanes_ref) | copy-start | bytes 393220
  15.5 11.0 %copy-start.13 = (f32[8,128]{1,0:T(8,128)S(1)}, f32[8,128]{1,0:T(8,128)}, u32[]{:S(2)}) copy-start(f32[8,128]{1,0:T(8,128)} %constant.37.clone.facts_ref) | copy-start | bytes 12292
  27.0 22.9 %copy-start.1 = (bf16[384,256]{1,0:T(8,128)(2,1)S(1)}, bf16[384,256]{1,0:T(8,128)(2,1)}, u32[]{:S(2)}) copy-start(bf16[384,256]{1,0:T(8,128)(2,1)} %constant.34.clone.unlanes_ref) | copy-start | bytes 589828
  27.0 22.9 %copy-start.7 = (bf16[128,256]{1,0:T(8,128)(2,1)S(1)}, bf16[128,256]{1,0:T(8,128)(2,1)}, u32[]{:S(2)}) copy-start(bf16[128,256]{1,0:T(8,128)(2,1)} %constant.31.clone.unradix_ref) | copy-start | bytes 196612
  51.1 26.4 %copy-start.2 = (bf16[2,192,256]{2,1,0:T(8,128)(2,1)S(1)}, bf16[2,192,256]{2,1,0:T(8,128)(2,1)}, u32[]{:S(2)}) copy-start(bf16[2,192,256]{2,1,0:T(8,128)(2,1)} %constant.27.clone.table_hbm.table_ref) | copy-start | bytes 589828
  51.1 26.4 %copy-start.9 = (bf16[2,176,256]{2,1,0:T(8,128)(2,1)S(1)}, bf16[2,176,256]{2,1,0:T(8,128)(2,1)}, u32[]{:S(2)}) copy-start(bf16[2,176,256]{2,1,0:T(8,128)(2,1)} %constant.28.clone.untable_ref) | copy-start | bytes 540676
  51.1 26.4 %copy-start.10 = (f32[32,128]{1,0:T(8,128)S(1)}, f32[32,128]{1,0:T(8,128)}, u32[]{:S(2)}) copy-start(f32[32,128]{1,0:T(8,128)} %constant.26.clone.twiddle_hbm.twiddle_ref) | copy-start | bytes 49156
  77.5 19.3 %copy-start.4 = (bf16[2,2,256,256]{3,2,1,0:T(8,128)(2,1)S(1)}, bf16[2,2,256,256]{3,2,1,0:T(8,128)(2,1)}, u32[]{:S(2)}) copy-start(bf16[2,2,256,256]{3,2,1,0:T(8,128)(2,1)} %constant.35.clone.project_ref) | copy-start | bytes 1572868
  78.9 18.0 %copy-start.11 = (bf16[256,256]{1,0:T(8,128)(2,1)S(1)}, bf16[256,256]{1,0:T(8,128)(2,1)}, u32[]{:S(2)}) copy-start(bf16[256,256]{1,0:T(8,128)(2,1)} %constant.36.clone.mean_ref) | copy-start | bytes 393220
  96.9 16.7 %copy-start.5 = (f32[1,32,2048]{2,1,0:T(8,128)S(1)}, f32[1,32,2048]{2,1,0:T(8,128)}, u32[]{:S(2)}) copy-start(f32[1,32,2048]{2,1,0:T(8,128)} %start_ref.1) | copy-start | bytes 786436
  96.9 16.7 %copy-start.8 = (bf16[2,192,256]{2,1,0:T(8,128)(2,1)S(1)}, bf16[2,192,256]{2,1,0:T(8,128)(2,1)}, u32[]{:S(2)}) copy-start(bf16[2,192,256]{2,1,0:T(8,128)(2,1)} %constant.29.clone.untable_ref) | copy-start | bytes 589828
  97.6 15.9 %copy-start = (f32[1,32,2048]{2,1,0:T(8,128)S(1)}, f32[1,32,2048]{2,1,0:T(8,128)}, u32[]{:S(2)}) copy-start(f32[1,32,2048]{2,1,0:T(8,128)} %state_ref.1) | copy-start | bytes 786436

commit v9 on v8

--- a/solution.py
+++ b/solution.py
@@ -18,7 +18,8 @@
 KAP = 64
 JP = 11
 PIECE = 4 * 2 * JP
-USED = MINE * 2 * JP
+USED = 8 * MINE * 2 * JP
+TILES = -(-USED // 128)
 HYPER_RATE = 0.2
 STEP_SIZE = 0.5
 BF16 = jnp.bfloat16
@@ -122,11 +123,20 @@
     return np.kron(np.eye(8), np.ones((ROWS, ROWS))).astype(ml_dtypes.bfloat16)
 
 
-def lane_facts(packed):
-    lane = np.arange(512 if packed else 128)
-    facts = np.zeros((8, lane.size))
+def lane_facts():
+    lane = np.arange(128)
+    facts = np.zeros((8, 128))
     facts[0] = 16 * (lane // (2 * JP))
     facts[1] = 64 * (lane % JP)
+    return facts.astype(np.float32)
+
+
+def packed_facts():
+    lane = np.arange(USED)
+    own = lane % (USED // 8)
+    facts = np.zeros((8, USED))
+    facts[0] = 16 * (own // (2 * JP))
+    facts[1] = 64 * (own % JP) + 8 * (lane // (USED // 8))
     return facts.astype(np.float32)
 
 
@@ -311,38 +321,42 @@
     return matmul_tall(radix, split(right))
 
 
+def pieces_of():
+    for rows in range(8):
+        for jr in range(6):
+            index, offset = divmod(rows * (USED // 8) + PIECE * jr, 128)
+            yield rows, jr, index, offset, PIECE if jr < 5 else 2 * JP
+
+
 def pack(tiles):
     lane = lax.broadcasted_iota(jnp.int32, (1, 128), 1)
-    packed = [None] * 4
-    for jr, tile in enumerate(tiles):
-        index, offset = divmod(PIECE * jr, 128)
-        moved = pltpu.roll(tile, offset, 1) if offset else tile
+    packed = [None] * TILES
+    for rows, jr, index, offset, used in pieces_of():
+        moved = tiles[jr][8 * rows : 8 * rows + 8]
+        moved = pltpu.roll(moved, offset, 1) if offset else moved
         parts = [(index, moved)]
-        if offset + PIECE > 128:
+        if offset + used > 128:
             parts = [(index, jnp.where(lane >= offset, moved, 0.0))]
             parts.append((index + 1, jnp.where(lane < offset, moved, 0.0)))
         for own, part in parts:
-            if own < 4:
-                packed[own] = part if packed[own] is None else packed[own] + part
+            packed[own] = part if packed[own] is None else packed[own] + part
     return packed
 
 
 def unpack(packed):
     lane = lax.broadcasted_iota(jnp.int32, (1, 128), 1)
-    tiles = []
-    for jr in range(6):
-        index, offset = divmod(PIECE * jr, 128)
+    tiles = [[] for _ in range(6)]
+    for rows, jr, index, offset, used in pieces_of():
         tile = packed[:, 128 * index : 128 * index + 128]
-        if offset + PIECE > 128:
-            later = packed[:, 128 * index + 128 : 128 * index + 256] if index < 3 else 0.0
-            tile = jnp.where(lane >= offset, tile, later)
-        tiles.append(pltpu.roll(tile, 128 - offset, 1) if offset else tile)
-    return tiles
-
-
-def y_waves(facts):
-    kap = lax.broadcasted_iota(jnp.int32, (KAP, 1), 0).astype(F32)
-    return kap + facts[1:2]
+        if offset + used > 128:
+            tile = jnp.where(lane >= offset, tile, packed[:, 128 * index + 128 : 128 * index + 256])
+        tiles[jr].append(pltpu.roll(tile, 128 - offset, 1) if offset else tile)
+    return [jnp.concatenate(tile, axis=0) for tile in tiles]
+
+
+def y_waves(facts, count=KAP):
+    row = lax.broadcasted_iota(jnp.int32, (count, 1), 0).astype(F32)
+    return row + facts[1:2]
 
 
 def x_waves(facts, owner):
@@ -391,8 +405,8 @@
 def weights_kernel(to_ref, from_ref, deform_ref, facts_ref, out_ref):
     facts = facts_ref[...]
     wave_x = x_waves(facts, lax.axis_index("row"))
-    wave_y = y_waves(facts)
-    square = (wave_x * wave_x + wave_y * wave_y)[:, :USED]
+    wave_y = y_waves(facts, 8)
+    square = wave_x * wave_x + wave_y * wave_y
     layer = lax.axis_index("layer")
     modes = [from_ref[layer, m] * (-1.0 / (square + deform_ref[m])) for m in range(8)]
     for n in range(8):
@@ -410,8 +424,8 @@
     tiles = [jnp.where(kept, spectrum[KAP * jr : KAP * jr + KAP], 0.0) for jr in range(6)]
     spec_ref[...] = jnp.concatenate(tiles, axis=0)
     for index, tile in enumerate(pack(tiles)):
-        used = min(USED - 128 * index, 128)
-        used_ref[:, 128 * index : 128 * index + used] = tile[:, :used]
+        lanes = slice(128 * index, min(USED, 128 * index + 128))
+        used_ref[:, lanes] = tile[:, : lanes.stop - lanes.start]
 
 
 def stream_kernel(
@@ -421,7 +435,7 @@
     for n in range(8):
         term = weights_ref[n] * all_ref[n]
         stream = term if stream is None else stream + term
-    stream_ref[:, 384:] = jnp.zeros((KAP, 128), F32)
+    stream_ref[:, 128 * TILES - 128 :] = jnp.zeros((8, 128), F32)
     stream_ref[:, :USED] = stream
     facts = facts_ref[...]
     wave_y = y_waves(facts)
@@ -616,19 +630,18 @@
     unlanes = jnp.asarray(y_lane_inverse_table())
     project = jnp.asarray(y_projection_table())
     mean = jnp.asarray(y_mean_table())
-    facts = jnp.asarray(lane_facts(False))
-    packed_facts = jnp.asarray(lane_facts(True))
+    facts = jnp.asarray(lane_facts())
 
     one, four = (64 * CHUNK, 128), (64 * MINE, 128)
     (columns,) = call(state_kernel, [one], [state, turn_x, forward_x], far_in=True, far_out=True, copies=5)
     columns = exchange(columns, devices)
     spectrum, used = call(
-        spectrum_kernel, [(6 * KAP, 128), (KAP, USED)], [columns, radix, turn_y, lanes, facts]
+        spectrum_kernel, [(6 * KAP, 128), (8, USED)], [columns, radix, turn_y, lanes, facts]
     )
     (weights,) = call(
         weights_kernel,
-        [(8, KAP, USED)],
-        [to_modes, from_modes, deform, packed_facts],
+        [(8, 8, USED)],
+        [to_modes, from_modes, deform, jnp.asarray(packed_facts())],
         scalars=3,
         cost=pl.CostEstimate(flops=8_000_000, bytes_accessed=2_000_000, transcendentals=0),
     )
@@ -637,7 +650,7 @@
         stream_kernel,
         [four],
         [weights, gathered, spectrum, unradix, turn_y, unlanes, facts],
-        scratch=[(KAP, 512)],
+        scratch=[(8, 128 * TILES)],
     )
     fields = exchange(fields, devices)
     (flux,) = call(

time: 115 us -> 115 us (level)
    all_gather x1, blocking collectives: 22.9 us -> 21.8 us  [per_device(): gathered = lax.all_gather(used, 'layer', axis=0, tiled=False)]
where the time goes in v9:
time: 115 us; the launch traced here: 114 us
  blocking collectives  82.4 us (72%)
  starting transfers between devices  12.5 us (11%)
  waiting for transfers between devices  9.61 us (8%)
  Pallas kernels  8.7 us (8%)
    all_to_all x3, blocking collectives, exchange(): lax.all_to_all(sent, 'row', split_axis=0, concat_axis=0, tiled=True)  60.6 us
    all_gather x1, blocking collectives, per_device(): gathered = lax.all_gather(used, 'layer', axis=0, tiled=False)  21.8 us
    all_to_all x1, starting transfers between devices, exchange(): lax.all_to_all(sent, 'row', split_axis=0, concat_axis=0, tiled=True)  12.5 us
    all_to_all x1, waiting for transfers between devices, exchange(): lax.all_to_all(sent, 'row', split_axis=0, concat_axis=0, tiled=True)  9.61 us
    pallas_call x7, Pallas kernels, call(): pl.pallas_call(kernel, out_shape=[jax.ShapeDtypeStruct(shape, F32) for sh...  8.7 us
  transfers between devices with their start and end apart: 1, of which 1 were waited for; matrix products, arithmetic and copies ran while one was open for 0% of the time, Pallas kernels for 1%

profile of v9, /device:TPU:8, one launch (start us, length us, event | category | flops | bytes accessed | tf_op | source)
XLA Modules:
  0.0 114.2 jit_solution(17196216382212039657)
XLA Ops:
  0.6 2.2 %shard_map.186 = f32[384,128]{1,0:T(8,128)} custom-call(f32[1,32,2048]{2,1,0:T(8,128)} %state_ref.1, f32[32,128]{1,0:T(8,128)} %constant.26.clone.twiddle_hbm.twiddle_ref, bf16[2,192,256]{2,1,0:T(8,128)(2,1)} %constant.27.clone.table_hbm.table_ref), custom_call_target="tpu_custom_call" | custom-call | tf_op jit(solution)/shard_map/pallas_call | solution.py:603
  2.8 0.0 copy-start.13
  2.9 0.0 copy-start.15
  2.9 0.0 copy-start.16
  2.9 0.0 copy-start.17
  2.9 12.5 %all-to-all-start = ((f32[64,1,768]{2,1,0:T(1,128)}), f32[64,1,768]{2,1,0:T(1,128)S(1)}, u32[]{:S(2)}, u32[]{:S(2)}) async-start(f32[64,1,768]{2,1,0:T(1,128)} %bitcast.17), calls=%async_computation | async-start | bytes 393216 | tf_op jit(solution)/shard_map/all_to_all | solution.py:617
  15.5 0.0 copy-start.3
  15.5 0.0 copy-start.6
  15.5 0.0 copy-start.12
  15.5 0.0 copy-start.14
  15.5 1.3 %shard_map.185.weights_ref = f32[8,8,3696]{2,1,0:T(8,128)S(1)} custom-call(f32[8,8]{1,0:T(8,128)S(1)} %copy-done.15, f32[8,8]{1,0:T(8,128)S(1)} %copy-done.16, f32[8]{0:T(128)S(1)} %copy-done.17, f32[8,3696]{1,0:T(8,128)S(1)} %copy-done.13), custom_call_target="tpu_custom_call" | custom-call | flops 8000000 | bytes 2000000 | tf_op jit(solution)/shard_map/pallas_call | solution.py:603
  16.8 9.6 %all-to-all-done = f32[64,1,768]{2,1,0:T(1,128)S(1)} async-done(((f32[64,1,768]{2,1,0:T(1,128)}), f32[64,1,768]{2,1,0:T(1,128)S(1)}, u32[]{:S(2)}, u32[]{:S(2)}) %all-to-all-start) | async-done | bytes 196640 | tf_op jit(solution)/shard_map/all_to_all | solution.py:617
  26.5 0.0 copy-done.12
  26.5 0.0 copy-done.14
  26.5 0.5 shard_map.187
  27.0 0.0 copy-start.1
  27.0 0.0 copy-start.7
  27.0 21.8 %all-gather = f32[64,3696]{1,0:T(8,128)S(1)} all-gather(f32[8,3696]{1,0:T(8,128)S(1)} %get-tuple-element.4), channel_id=2, replica_groups=mesh['layer'=8,'row'=64] {'layer'}, dimensions={0}, use_global_device_ids=true | all-gather | bytes 1064448 | tf_op jit(solution)/shard_map/all_gather | solution.py:648
  48.8 0.0 copy-done.1
  48.8 1.2 %shard_map.188 = f32[1344,128]{1,0:T(8,128)S(1)} custom-call(f32[8,8,3696]{2,1,0:T(8,128)S(1)} %shard_map.185.weights_ref, f32[8,8,3696]{2,1,0:T(8,128)S(1)} %bitcast.9, f32[384,128]{1,0:T(8,128)S(1)} %get-tuple-element.5.spec_ref, bf16[128,256]{1,0:T(8,128)(2,1)S(1)} %copy-done.7, f32[2,64,128]{2,1,0:T(8,128)S(1)} %copy-done.3, ...), custom_call_target="tpu_custom_call" | custom-call | tf_op jit(solution)/shard_map/pallas_call | solution.py:603
  49.9 0.0 copy-start.9
  49.9 0.0 copy-start.10
  50.0 26.8 %all_to_all.20 = f32[64,1,2688]{2,1,0:T(1,128)S(1)} all-to-all(f32[64,1,2688]{2,1,0:T(1,128)S(1)} %bitcast.11), channel_id=1, replica_groups=mesh['layer'=8,'row'=64] {'row'}, dimensions={0} | all-to-all | bytes 1376256 | tf_op jit(solution)/shard_map/all_to_all | solution.py:617
  76.8 0.0 copy-done.10
  76.8 0.0 copy-start.4
  76.8 1.4 %shard_map.189 = f32[384,128]{1,0:T(8,128)S(1)} custom-call(f32[1344,128]{1,0:T(8,128)S(1)} %bitcast.10, f32[32,128]{1,0:T(8,128)S(1)} %copy-done.10, bf16[2,176,256]{2,1,0:T(8,128)(2,1)S(1)} %copy-done.9, bf16[2,192,256]{2,1,0:T(8,128)(2,1)S(1)} %copy-done.2), custom_call_target="tpu_custom_call" | custom-call | tf_op jit(solution)/shard_map/pallas_call | solution.py:603
  78.1 0.0 copy-start.11
  78.1 18.0 %all_to_all.21 = f32[64,1,768]{2,1,0:T(1,128)S(1)} all-to-all(f32[64,1,768]{2,1,0:T(1,128)S(1)} %bitcast.16), channel_id=1, replica_groups=mesh['layer'=8,'row'=64] {'row'}, dimensions={0} | all-to-all | bytes 393216 | tf_op jit(solution)/shard_map/all_to_all | solution.py:617
  96.1 0.8 shard_map.190
  96.9 0.0 copy-start
  96.9 15.9 %all_to_all.22 = f32[64,1,768]{2,1,0:T(1,128)S(1)} all-to-all(f32[64,1,768]{2,1,0:T(1,128)S(1)} %bitcast.14), channel_id=1, replica_groups=mesh['layer'=8,'row'=64] {'row'}, dimensions={0} | all-to-all | bytes 393216 | tf_op jit(solution)/shard_map/all_to_all | solution.py:617
  112.8 1.4 %shard_map.191 = (f32[1,32,2048]{2,1,0:T(8,128)}, f32[1,32,2048]{2,1,0:T(8,128)}) custom-call(f32[384,128]{1,0:T(8,128)S(1)} %bitcast.15, f32[1,32,2048]{2,1,0:T(8,128)S(1)} %copy-done, f32[1,32,2048]{2,1,0:T(8,128)S(1)} %copy-done.5, f32[32,128]{1,0:T(8,128)S(1)} %copy-done.10, bf16[2,192,256]{2,1,0:T(8,128)(2,1)S(1)} %copy-done.8), custom_call_target="tpu_custom_call" | custom-call | tf_op jit(solution)/shard_map/pallas_call | solution.py:603
  (17 shorter events, 0.0 us)
Async XLA Ops:
  2.8 12.6 %copy-start.13 = (f32[8,3696]{1,0:T(8,128)S(1)}, f32[8,3696]{1,0:T(8,128)}, u32[]{:S(2)}) copy-start(f32[8,3696]{1,0:T(8,128)} %constant.38.clone.facts_ref) | copy-start | bytes 354820
  2.9 12.6 %copy-start.15 = (f32[8,8]{1,0:T(8,128)S(1)}, f32[8,8]{1,0:T(8,128)}, u32[]{:S(2)}) copy-start(f32[8,8]{1,0:T(8,128)} %to_ref.1) | copy-start | bytes 772
  2.9 12.6 %copy-start.16 = (f32[8,8]{1,0:T(8,128)S(1)}, f32[8,8]{1,0:T(8,128)}, u32[]{:S(2)}) copy-start(f32[8,8]{1,0:T(8,128)} %from_ref.1) | copy-start | bytes 772
  2.9 12.6 %copy-start.17 = (f32[8]{0:T(128)S(1)}, f32[8]{0:T(128)}, u32[]{:S(2)}) copy-start(f32[8]{0:T(128)} %deform_ref.1) | copy-start | bytes 100
  2.9 23.6 %all-to-all-start = ((f32[64,1,768]{2,1,0:T(1,128)}), f32[64,1,768]{2,1,0:T(1,128)S(1)}, u32[]{:S(2)}, u32[]{:S(2)}) async-start(f32[64,1,768]{2,1,0:T(1,128)} %bitcast.17), calls=%async_computation | async-start | bytes 393216 | tf_op jit(solution)/shard_map/all_to_all | solution.py:617
  15.5 11.0 %copy-start.3 = (f32[2,64,128]{2,1,0:T(8,128)S(1)}, f32[2,64,128]{2,1,0:T(8,128)}, u32[]{:S(2)}) copy-start(f32[2,64,128]{2,1,0:T(8,128)} %constant.32.clone.turn_ref) | copy-start | bytes 196612
  15.5 11.0 %copy-start.6 = (bf16[128,192]{1,0:T(8,128)(2,1)S(1)}, bf16[128,192]{1,0:T(8,128)(2,1)}, u32[]{:S(2)}) copy-start(bf16[128,192]{1,0:T(8,128)(2,1)} %constant.30.clone.radix_ref) | copy-start | bytes 147460
  15.5 11.0 %copy-start.12 = (bf16[256,256]{1,0:T(8,128)(2,1)S(1)}, bf16[256,256]{1,0:T(8,128)(2,1)}, u32[]{:S(2)}) copy-start(bf16[256,256]{1,0:T(8,128)(2,1)} %constant.33.clone.lanes_ref) | copy-start | bytes 393220
  15.5 11.0 %copy-start.14 = (f32[8,128]{1,0:T(8,128)S(1)}, f32[8,128]{1,0:T(8,128)}, u32[]{:S(2)}) copy-start(f32[8,128]{1,0:T(8,128)} %constant.37.clone.facts_ref) | copy-start | bytes 12292
  27.0 21.8 %copy-start.1 = (bf16[384,256]{1,0:T(8,128)(2,1)S(1)}, bf16[384,256]{1,0:T(8,128)(2,1)}, u32[]{:S(2)}) copy-start(bf16[384,256]{1,0:T(8,128)(2,1)} %constant.34.clone.unlanes_ref) | copy-start | bytes 589828
  27.0 21.8 %copy-start.7 = (bf16[128,256]{1,0:T(8,128)(2,1)S(1)}, bf16[128,256]{1,0:T(8,128)(2,1)}, u32[]{:S(2)}) copy-start(bf16[128,256]{1,0:T(8,128)(2,1)} %constant.31.clone.unradix_ref) | copy-start | bytes 196612
  49.9 26.8 %copy-start.2 = (bf16[2,192,256]{2,1,0:T(8,128)(2,1)S(1)}, bf16[2,192,256]{2,1,0:T(8,128)(2,1)}, u32[]{:S(2)}) copy-start(bf16[2,192,256]{2,1,0:T(8,128)(2,1)} %constant.27.clone.table_hbm.table_ref) | copy-start | bytes 589828
  49.9 26.8 %copy-start.9 = (bf16[2,176,256]{2,1,0:T(8,128)(2,1)S(1)}, bf16[2,176,256]{2,1,0:T(8,128)(2,1)}, u32[]{:S(2)}) copy-start(bf16[2,176,256]{2,1,0:T(8,128)(2,1)} %constant.28.clone.untable_ref) | copy-start | bytes 540676
  49.9 26.8 %copy-start.10 = (f32[32,128]{1,0:T(8,128)S(1)}, f32[32,128]{1,0:T(8,128)}, u32[]{:S(2)}) copy-start(f32[32,128]{1,0:T(8,128)} %constant.26.clone.twiddle_hbm.twiddle_ref) | copy-start | bytes 49156
  76.8 19.3 %copy-start.4 = (bf16[2,2,256,256]{3,2,1,0:T(8,128)(2,1)S(1)}, bf16[2,2,256,256]{3,2,1,0:T(8,128)(2,1)}, u32[]{:S(2)}) copy-start(bf16[2,2,256,256]{3,2,1,0:T(8,128)(2,1)} %constant.35.clone.project_ref) | copy-start | bytes 1572868
  78.1 18.0 %copy-start.11 = (bf16[256,256]{1,0:T(8,128)(2,1)S(1)}, bf16[256,256]{1,0:T(8,128)(2,1)}, u32[]{:S(2)}) copy-start(bf16[256,256]{1,0:T(8,128)(2,1)} %constant.36.clone.mean_ref) | copy-start | bytes 393220
  96.1 16.7 %copy-start.5 = (f32[1,32,2048]{2,1,0:T(8,128)S(1)}, f32[1,32,2048]{2,1,0:T(8,128)}, u32[]{:S(2)}) copy-start(f32[1,32,2048]{2,1,0:T(8,128)} %start_ref.1) | copy-start | bytes 786436
  96.1 16.7 %copy-start.8 = (bf16[2,192,256]{2,1,0:T(8,128)(2,1)S(1)}, bf16[2,192,256]{2,1,0:T(8,128)(2,1)}, u32[]{:S(2)}) copy-start(bf16[2,192,256]{2,1,0:T(8,128)(2,1)} %constant.29.clone.untable_ref) | copy-start | bytes 589828
  96.9 15.9 %copy-start = (f32[1,32,2048]{2,1,0:T(8,128)S(1)}, f32[1,32,2048]{2,1,0:T(8,128)}, u32[]{:S(2)}) copy-start(f32[1,32,2048]{2,1,0:T(8,128)} %state_ref.1) | copy-start | bytes 786436

commit v10 on v9

--- a/solution.py
+++ b/solution.py
@@ -311,12 +311,19 @@
 
 
 def y_returned(pairs, radix, twiddle):
+    lane = lax.broadcasted_iota(jnp.int32, (1, 128), 1)
     c, s = twiddle[0], twiddle[1]
     real, imag = [], []
     for pair, turned in pairs:
         re, im = pair[:, :128], pair[:, 128:]
-        real.append(im * c + re * s if turned else re * c - im * s)
-        imag.append(im * s - re * c if turned else re * s + im * c)
+        if turned in (0, 4):
+            real.append(im * c + re * s if turned else re * c - im * s)
+            imag.append(im * s - re * c if turned else re * s + im * c)
+            continue
+        early = lane < 32 * turned
+        re, im = jnp.where(early, im, re), jnp.where(early, -re, im)
+        real.append(re * c - im * s)
+        imag.append(re * s + im * c)
     right = jnp.concatenate([jnp.concatenate(real, axis=1), jnp.concatenate(imag, axis=1)], axis=0)
     return matmul_tall(radix, split(right))
 
@@ -392,14 +399,11 @@
     copies[1].wait()
     copies[2].wait()
     results = x_forward(real, imag, twiddle_ref[...], table_ref)
-    sends = []
     for group in range(2):
         store_x(out_ref, results, group)
         rows = pl.ds(32 * group * CHUNK, 32 * CHUNK)
-        sends.append(pltpu.make_async_copy(out_ref.at[rows], out_hbm.at[rows], sems.at[3 + group]))
-        sends[-1].start()
-    for send in sends:
-        send.wait()
+        pltpu.make_async_copy(out_ref.at[rows], out_hbm.at[rows], sems.at[3]).start()
+    pltpu.make_async_copy(out_ref, out_hbm, sems.at[3]).wait()
 
 
 def weights_kernel(to_ref, from_ref, deform_ref, facts_ref, out_ref):
@@ -445,15 +449,23 @@
         wave_x = x_waves(facts, lax.axis_index("row")) + 64 * jr
         along_y, along_x = wave_y * half_of_zero(wave_x), wave_x * once
         own = spec_ref[KAP * jr : KAP * jr + KAP, :]
-        pieces += [along_y * tile, -along_y * own, along_x * tile, along_x * own]
+        four = [along_y * tile, -along_y * own, along_x * tile, along_x * own]
+        if jr < 5:
+            pieces += four
+            continue
+        alone = lax.broadcasted_iota(jnp.int32, (1, 128), 1) < 2 * JP
+        four = [jnp.where(alone, field, 0.0) for field in four]
+        moved = [four[0]] + [pltpu.roll(four[f], 2 * JP * f, 1) for f in range(1, 4)]
+        pieces.append((moved[0] + moved[1]) + (moved[2] + moved[3]))
     out = matmul_wide(split(jnp.concatenate(pieces, axis=0)), unlanes_ref)
-    pairs = [(out[KAP * i : KAP * i + KAP], i % 4 < 2) for i in range(24)]
+    turned = [4, 4, 0, 0] * 5 + [2]
+    pairs = [(out[KAP * i : KAP * i + KAP], turned[i]) for i in range(21)]
     out = y_returned(pairs, unradix_ref, turn_ref)
-    for jr in range(6):
+    for jr in range(5):
         blocks = [out[:, 128 * (4 * jr + f) : 128 * (4 * jr + f) + 128] for f in range(4)]
-        count = min(MINE - 4 * jr, 4)
-        for jb, block in enumerate(regroup(blocks, range(count))):
+        for jb, block in enumerate(regroup(blocks, range(4))):
             out_ref[pl.ds(4 * jr + jb, 64, stride=MINE), :] = block
+    out_ref[pl.ds(20, 64, stride=MINE), :] = out[:, 128 * 20 :]
 
 
 def jacobian_kernel(in_ref, twiddle_ref, untable_ref, table_ref, out_ref, first_ref, whole_ref, jac):
@@ -531,7 +543,7 @@
         own = jnp.where(first, mean[16 * jr : 16 * jr + 16], 0.0)
         flux = jnp.concatenate([low[:16] - own, low[16:], high], axis=0)
         total = flux - damping[KAP * jr : KAP * jr + KAP]
-        pairs.append((total * jnp.where(zero_wave, 0.5, 1.0) if jr == 0 else total, False))
+        pairs.append((total * jnp.where(zero_wave, 0.5, 1.0) if jr == 0 else total, 0))
     out = y_returned(pairs, unradix_ref, turn_ref)
     for jr in range(6):
         out_ref[pl.ds(jr, 64, stride=CHUNK), :] = out[:, 128 * jr : 128 * jr + 128]
@@ -562,7 +574,6 @@
             own = jnp.where(row % depth < depth // 2, side, 0.0)
             first[...] = matmul(split(own), table, TN)
     twiddle = twiddle_ref[...]
-    sends = []
     for block in range(4):
         rows = slice(8 * block, 8 * block + 8)
 
@@ -582,10 +593,9 @@
             )
         for i, (near, far) in enumerate(((tendency_ref, tendency_hbm), (new_ref, new_hbm))):
             own = (slice(None), pl.ds(8 * block, 8))
-            sends.append(pltpu.make_async_copy(near.at[own], far.at[own], sems.at[2 * block + i]))
-            sends[-1].start()
-    for send in sends:
-        send.wait()
+            pltpu.make_async_copy(near.at[own], far.at[own], sems.at[i]).start()
+    pltpu.make_async_copy(tendency_ref, tendency_hbm, sems.at[0]).wait()
+    pltpu.make_async_copy(new_ref, new_hbm, sems.at[1]).wait()
 
 
 VMEM = pl.BlockSpec(memory_space=pltpu.VMEM)
@@ -633,7 +643,7 @@
     facts = jnp.asarray(lane_facts())
 
     one, four = (64 * CHUNK, 128), (64 * MINE, 128)
-    (columns,) = call(state_kernel, [one], [state, turn_x, forward_x], far_in=True, far_out=True, copies=5)
+    (columns,) = call(state_kernel, [one], [state, turn_x, forward_x], far_in=True, far_out=True, copies=4)
     columns = exchange(columns, devices)
     spectrum, used = call(
         spectrum_kernel, [(6 * KAP, 128), (8, USED)], [columns, radix, turn_y, lanes, facts]
@@ -673,7 +683,7 @@
             [total, state, start_state, turn_x, inverse_chunk],
             scratch=[(128, 256), (256, 256)],
             far_out=True,
-            copies=8,
+            copies=2,
         )
     )
 

time: 115 us -> 114 us (level)
  no operation moved by 1% of the time
where the time goes in v10:
time: 114 us
  blocking collectives  82.4 us (72%)
  starting transfers between devices  12.5 us (11%)
  waiting for transfers between devices  9.61 us (8%)
  Pallas kernels  8.59 us (8%)
    all_to_all x3, blocking collectives, exchange(): lax.all_to_all(sent, 'row', split_axis=0, concat_axis=0, tiled=True)  60.6 us
    all_gather x1, blocking collectives, per_device(): gathered = lax.all_gather(used, 'layer', axis=0, tiled=False)  21.8 us
    all_to_all x1, starting transfers between devices, exchange(): lax.all_to_all(sent, 'row', split_axis=0, concat_axis=0, tiled=True)  12.5 us
    all_to_all x1, waiting for transfers between devices, exchange(): lax.all_to_all(sent, 'row', split_axis=0, concat_axis=0, tiled=True)  9.61 us
    pallas_call x7, Pallas kernels, call(): pl.pallas_call(kernel, out_shape=[jax.ShapeDtypeStruct(shape, F32) for sh...  8.59 us
  transfers between devices with their start and end apart: 1, of which 1 were waited for; matrix products, arithmetic and copies ran while one was open for 0% of the time, Pallas kernels for 1%

profile of v10, /device:TPU:8, one launch (start us, length us, event | category | flops | bytes accessed | tf_op | source)
XLA Modules:
  0.0 114.1 jit_solution(18435003249170063077)
XLA Ops:
  0.6 2.2 %shard_map.186 = f32[384,128]{1,0:T(8,128)} custom-call(f32[1,32,2048]{2,1,0:T(8,128)} %state_ref.1, f32[32,128]{1,0:T(8,128)} %constant.26.clone.twiddle_hbm.twiddle_ref, bf16[2,192,256]{2,1,0:T(8,128)(2,1)} %constant.27.clone.table_hbm.table_ref), custom_call_target="tpu_custom_call" | custom-call | tf_op jit(solution)/shard_map/pallas_call | solution.py:613
  2.8 0.0 copy-start.13
  2.9 0.0 copy-start.15
  2.9 0.0 copy-start.16
  2.9 0.0 copy-start.17
  2.9 12.5 %all-to-all-start = ((f32[64,1,768]{2,1,0:T(1,128)}), f32[64,1,768]{2,1,0:T(1,128)S(1)}, u32[]{:S(2)}, u32[]{:S(2)}) async-start(f32[64,1,768]{2,1,0:T(1,128)} %bitcast.17), calls=%async_computation | async-start | bytes 393216 | tf_op jit(solution)/shard_map/all_to_all | solution.py:627
  15.5 0.0 copy-start.3
  15.5 0.0 copy-start.6
  15.5 0.0 copy-start.12
  15.5 0.0 copy-start.14
  15.5 1.3 %shard_map.185.weights_ref = f32[8,8,3696]{2,1,0:T(8,128)S(1)} custom-call(f32[8,8]{1,0:T(8,128)S(1)} %copy-done.15, f32[8,8]{1,0:T(8,128)S(1)} %copy-done.16, f32[8]{0:T(128)S(1)} %copy-done.17, f32[8,3696]{1,0:T(8,128)S(1)} %copy-done.13), custom_call_target="tpu_custom_call" | custom-call | flops 8000000 | bytes 2000000 | tf_op jit(solution)/shard_map/pallas_call | solution.py:613
  16.8 9.6 %all-to-all-done = f32[64,1,768]{2,1,0:T(1,128)S(1)} async-done(((f32[64,1,768]{2,1,0:T(1,128)}), f32[64,1,768]{2,1,0:T(1,128)S(1)}, u32[]{:S(2)}, u32[]{:S(2)}) %all-to-all-start) | async-done | bytes 196640 | tf_op jit(solution)/shard_map/all_to_all | solution.py:627
  26.4 0.0 copy-done.14
  26.5 0.5 shard_map.187
  27.0 0.0 copy-start.1
  27.0 0.0 copy-start.7
  27.0 21.8 %all-gather = f32[64,3696]{1,0:T(8,128)S(1)} all-gather(f32[8,3696]{1,0:T(8,128)S(1)} %get-tuple-element.4), channel_id=2, replica_groups=mesh['layer'=8,'row'=64] {'layer'}, dimensions={0}, use_global_device_ids=true | all-gather | bytes 1064448 | tf_op jit(solution)/shard_map/all_gather | solution.py:658
  48.8 1.1 shard_map.188
  49.9 0.0 copy-start.2
  49.9 0.0 copy-start.9
  49.9 0.0 copy-start.10
  49.9 26.8 %all_to_all.20 = f32[64,1,2688]{2,1,0:T(1,128)S(1)} all-to-all(f32[64,1,2688]{2,1,0:T(1,128)S(1)} %bitcast.11), channel_id=1, replica_groups=mesh['layer'=8,'row'=64] {'row'}, dimensions={0} | all-to-all | bytes 1376256 | tf_op jit(solution)/shard_map/all_to_all | solution.py:627
  76.7 0.0 copy-done.9
  76.7 0.0 copy-start.4
  76.7 1.4 %shard_map.189 = f32[384,128]{1,0:T(8,128)S(1)} custom-call(f32[1344,128]{1,0:T(8,128)S(1)} %bitcast.10, f32[32,128]{1,0:T(8,128)S(1)} %copy-done.10, bf16[2,176,256]{2,1,0:T(8,128)(2,1)S(1)} %copy-done.9, bf16[2,192,256]{2,1,0:T(8,128)(2,1)S(1)} %copy-done.2), custom_call_target="tpu_custom_call" | custom-call | tf_op jit(solution)/shard_map/pallas_call | solution.py:613
  78.1 0.0 copy-start.11
  78.1 18.0 %all_to_all.21 = f32[64,1,768]{2,1,0:T(1,128)S(1)} all-to-all(f32[64,1,768]{2,1,0:T(1,128)S(1)} %bitcast.16), channel_id=1, replica_groups=mesh['layer'=8,'row'=64] {'row'}, dimensions={0} | all-to-all | bytes 393216 | tf_op jit(solution)/shard_map/all_to_all | solution.py:627
  96.1 0.8 shard_map.190
  96.8 0.0 copy-start
  96.8 15.9 %all_to_all.22 = f32[64,1,768]{2,1,0:T(1,128)S(1)} all-to-all(f32[64,1,768]{2,1,0:T(1,128)S(1)} %bitcast.14), channel_id=1, replica_groups=mesh['layer'=8,'row'=64] {'row'}, dimensions={0} | all-to-all | bytes 393216 | tf_op jit(solution)/shard_map/all_to_all | solution.py:627
  112.7 0.0 copy-done.5
  112.7 1.3 %shard_map.191 = (f32[1,32,2048]{2,1,0:T(8,128)}, f32[1,32,2048]{2,1,0:T(8,128)}) custom-call(f32[384,128]{1,0:T(8,128)S(1)} %bitcast.15, f32[1,32,2048]{2,1,0:T(8,128)S(1)} %copy-done, f32[1,32,2048]{2,1,0:T(8,128)S(1)} %copy-done.5, f32[32,128]{1,0:T(8,128)S(1)} %copy-done.10, bf16[2,192,256]{2,1,0:T(8,128)(2,1)S(1)} %copy-done.8), custom_call_target="tpu_custom_call" | custom-call | tf_op jit(solution)/shard_map/pallas_call | solution.py:613
  (17 shorter events, 0.0 us)
Async XLA Ops:
  2.8 12.6 %copy-start.13 = (f32[8,3696]{1,0:T(8,128)S(1)}, f32[8,3696]{1,0:T(8,128)}, u32[]{:S(2)}) copy-start(f32[8,3696]{1,0:T(8,128)} %constant.38.clone.facts_ref) | copy-start | bytes 354820
  2.9 12.6 %copy-start.15 = (f32[8,8]{1,0:T(8,128)S(1)}, f32[8,8]{1,0:T(8,128)}, u32[]{:S(2)}) copy-start(f32[8,8]{1,0:T(8,128)} %to_ref.1) | copy-start | bytes 772
  2.9 12.6 %copy-start.16 = (f32[8,8]{1,0:T(8,128)S(1)}, f32[8,8]{1,0:T(8,128)}, u32[]{:S(2)}) copy-start(f32[8,8]{1,0:T(8,128)} %from_ref.1) | copy-start | bytes 772
  2.9 12.6 %copy-start.17 = (f32[8]{0:T(128)S(1)}, f32[8]{0:T(128)}, u32[]{:S(2)}) copy-start(f32[8]{0:T(128)} %deform_ref.1) | copy-start | bytes 100
  2.9 23.6 %all-to-all-start = ((f32[64,1,768]{2,1,0:T(1,128)}), f32[64,1,768]{2,1,0:T(1,128)S(1)}, u32[]{:S(2)}, u32[]{:S(2)}) async-start(f32[64,1,768]{2,1,0:T(1,128)} %bitcast.17), calls=%async_computation | async-start | bytes 393216 | tf_op jit(solution)/shard_map/all_to_all | solution.py:627
  15.5 11.0 %copy-start.3 = (f32[2,64,128]{2,1,0:T(8,128)S(1)}, f32[2,64,128]{2,1,0:T(8,128)}, u32[]{:S(2)}) copy-start(f32[2,64,128]{2,1,0:T(8,128)} %constant.32.clone.turn_ref) | copy-start | bytes 196612
  15.5 11.0 %copy-start.6 = (bf16[128,192]{1,0:T(8,128)(2,1)S(1)}, bf16[128,192]{1,0:T(8,128)(2,1)}, u32[]{:S(2)}) copy-start(bf16[128,192]{1,0:T(8,128)(2,1)} %constant.30.clone.radix_ref) | copy-start | bytes 147460
  15.5 11.0 %copy-start.12 = (bf16[256,256]{1,0:T(8,128)(2,1)S(1)}, bf16[256,256]{1,0:T(8,128)(2,1)}, u32[]{:S(2)}) copy-start(bf16[256,256]{1,0:T(8,128)(2,1)} %constant.33.clone.lanes_ref) | copy-start | bytes 393220
  15.5 11.0 %copy-start.14 = (f32[8,128]{1,0:T(8,128)S(1)}, f32[8,128]{1,0:T(8,128)}, u32[]{:S(2)}) copy-start(f32[8,128]{1,0:T(8,128)} %constant.37.clone.facts_ref) | copy-start | bytes 12292
  27.0 21.8 %copy-start.1 = (bf16[384,256]{1,0:T(8,128)(2,1)S(1)}, bf16[384,256]{1,0:T(8,128)(2,1)}, u32[]{:S(2)}) copy-start(bf16[384,256]{1,0:T(8,128)(2,1)} %constant.34.clone.unlanes_ref) | copy-start | bytes 589828
  27.0 21.8 %copy-start.7 = (bf16[128,256]{1,0:T(8,128)(2,1)S(1)}, bf16[128,256]{1,0:T(8,128)(2,1)}, u32[]{:S(2)}) copy-start(bf16[128,256]{1,0:T(8,128)(2,1)} %constant.31.clone.unradix_ref) | copy-start | bytes 196612
  49.9 26.8 %copy-start.2 = (bf16[2,192,256]{2,1,0:T(8,128)(2,1)S(1)}, bf16[2,192,256]{2,1,0:T(8,128)(2,1)}, u32[]{:S(2)}) copy-start(bf16[2,192,256]{2,1,0:T(8,128)(2,1)} %constant.27.clone.table_hbm.table_ref) | copy-start | bytes 589828
  49.9 26.8 %copy-start.9 = (bf16[2,176,256]{2,1,0:T(8,128)(2,1)S(1)}, bf16[2,176,256]{2,1,0:T(8,128)(2,1)}, u32[]{:S(2)}) copy-start(bf16[2,176,256]{2,1,0:T(8,128)(2,1)} %constant.28.clone.untable_ref) | copy-start | bytes 540676
  49.9 26.8 %copy-start.10 = (f32[32,128]{1,0:T(8,128)S(1)}, f32[32,128]{1,0:T(8,128)}, u32[]{:S(2)}) copy-start(f32[32,128]{1,0:T(8,128)} %constant.26.clone.twiddle_hbm.twiddle_ref) | copy-start | bytes 49156
  76.7 19.3 %copy-start.4 = (bf16[2,2,256,256]{3,2,1,0:T(8,128)(2,1)S(1)}, bf16[2,2,256,256]{3,2,1,0:T(8,128)(2,1)}, u32[]{:S(2)}) copy-start(bf16[2,2,256,256]{3,2,1,0:T(8,128)(2,1)} %constant.35.clone.project_ref) | copy-start | bytes 1572868
  78.1 18.0 %copy-start.11 = (bf16[256,256]{1,0:T(8,128)(2,1)S(1)}, bf16[256,256]{1,0:T(8,128)(2,1)}, u32[]{:S(2)}) copy-start(bf16[256,256]{1,0:T(8,128)(2,1)} %constant.36.clone.mean_ref) | copy-start | bytes 393220
  96.0 16.7 %copy-start.5 = (f32[1,32,2048]{2,1,0:T(8,128)S(1)}, f32[1,32,2048]{2,1,0:T(8,128)}, u32[]{:S(2)}) copy-start(f32[1,32,2048]{2,1,0:T(8,128)} %start_ref.1) | copy-start | bytes 786436
  96.0 16.7 %copy-start.8 = (bf16[2,192,256]{2,1,0:T(8,128)(2,1)S(1)}, bf16[2,192,256]{2,1,0:T(8,128)(2,1)}, u32[]{:S(2)}) copy-start(bf16[2,192,256]{2,1,0:T(8,128)(2,1)} %constant.29.clone.untable_ref) | copy-start | bytes 589828
  96.8 15.9 %copy-start = (f32[1,32,2048]{2,1,0:T(8,128)S(1)}, f32[1,32,2048]{2,1,0:T(8,128)}, u32[]{:S(2)}) copy-start(f32[1,32,2048]{2,1,0:T(8,128)} %state_ref.1) | copy-start | bytes 786436

commit v11 on v10

--- a/solution.py
+++ b/solution.py
@@ -513,9 +513,7 @@
         store_x(out_ref, results, group)
 
 
-def projection_kernel(
-    in_ref, spec_ref, radix_ref, unradix_ref, turn_ref, project_ref, mean_ref, unlanes_ref, facts_ref, out_ref
-):
+def damping_kernel(spec_ref, unlanes_ref, facts_ref, out_ref):
     facts = facts_ref[...]
     wave_y = y_waves(facts)
     once = half_of_zero(wave_y)
@@ -525,7 +523,12 @@
         ratio = (wave_x * wave_x + wave_y * wave_y) * (1.0 / (KCUT * KCUT))
         ratio = ratio * ratio
         damped.append(((HYPER_RATE * (ratio * ratio)) * once) * spec_ref[KAP * jr : KAP * jr + KAP, :])
-    damping = matmul_wide(split(jnp.concatenate(damped, axis=0)), unlanes_ref)
+    out_ref[...] = matmul_wide(split(jnp.concatenate(damped, axis=0)), unlanes_ref)
+
+
+def projection_kernel(
+    in_ref, damping_ref, radix_ref, unradix_ref, turn_ref, project_ref, mean_ref, out_ref
+):
     left = [split(pair) for pair in y_turned(in_ref, radix_ref, turn_ref)]
     sides = []
     for side in range(2):
@@ -542,7 +545,7 @@
         low, high = [side[32 * jr : 32 * jr + 32] for side in sides]
         own = jnp.where(first, mean[16 * jr : 16 * jr + 16], 0.0)
         flux = jnp.concatenate([low[:16] - own, low[16:], high], axis=0)
-        total = flux - damping[KAP * jr : KAP * jr + KAP]
+        total = flux - damping_ref[KAP * jr : KAP * jr + KAP, :]
         pairs.append((total * jnp.where(zero_wave, 0.5, 1.0) if jr == 0 else total, 0))
     out = y_returned(pairs, unradix_ref, turn_ref)
     for jr in range(6):
@@ -670,10 +673,16 @@
         scratch=[(128, 256), (1024, 256), (2, 9, ROWS, 128)],
     )
     flux = exchange(flux, devices)
+    (damping,) = call(
+        damping_kernel,
+        [(6 * KAP, 256)],
+        [spectrum, unlanes, facts],
+        cost=pl.CostEstimate(flops=150_000_000, bytes_accessed=1_000_000, transcendentals=0),
+    )
     (total,) = call(
         projection_kernel,
         [one],
-        [flux, spectrum, radix, unradix, turn_y, project, mean, unlanes, facts],
+        [flux, damping, radix, unradix, turn_y, project, mean],
     )
     total = exchange(total, devices)
     return tuple(

time: 114 us -> 115 us (level)
  blocking collectives: 82.4 us -> 64.4 us
  waiting for transfers between devices: 9.61 us -> 20.2 us
  starting transfers between devices: 12.5 us -> 19.8 us
    all_to_all x3 -> x2, blocking collectives: 60.6 us -> 42.6 us  [exchange(): lax.all_to_all(sent, 'row', split_axis=0, concat_axis=0, tiled=True)]
    all_to_all x1 -> x2, waiting for transfers between devices: 9.61 us -> 20.2 us  [exchange(): lax.all_to_all(sent, 'row', split_axis=0, concat_axis=0, tiled=True)]
    all_to_all x1 -> x2, starting transfers between devices: 12.5 us -> 19.8 us  [exchange(): lax.all_to_all(sent, 'row', split_axis=0, concat_axis=0, tiled=True)]
    pallas_call x7 -> x8, Pallas kernels: 8.59 us -> 9.56 us  [call(): pl.pallas_call(kernel, out_shape=[jax.ShapeDtypeStruct(shape, F32) for sh...]
  transfers between devices with their start and end apart: 1 -> 2, of which waited for: 1 -> 2; matrix products, arithmetic and copies ran while one was open for 0% -> 0% of each run, Pallas kernels for 1% -> 1%
where the time goes in v11:
time: 115 us
  blocking collectives  64.4 us (56%)
  waiting for transfers between devices  20.2 us (18%)
  starting transfers between devices  19.8 us (17%)
  Pallas kernels  9.56 us (8%)
    all_to_all x2, blocking collectives, exchange(): lax.all_to_all(sent, 'row', split_axis=0, concat_axis=0, tiled=True)  42.6 us
    all_gather x1, blocking collectives, per_device(): gathered = lax.all_gather(used, 'layer', axis=0, tiled=False)  21.8 us
    all_to_all x2, waiting for transfers between devices, exchange(): lax.all_to_all(sent, 'row', split_axis=0, concat_axis=0, tiled=True)  20.2 us
    all_to_all x2, starting transfers between devices, exchange(): lax.all_to_all(sent, 'row', split_axis=0, concat_axis=0, tiled=True)  19.8 us
    pallas_call x8, Pallas kernels, call(): pl.pallas_call(kernel, out_shape=[jax.ShapeDtypeStruct(shape, F32) for sh...  9.56 us
  transfers between devices with their start and end apart: 2, of which 2 were waited for; matrix products, arithmetic and copies ran while one was open for 0% of the time, Pallas kernels for 1%

profile of v11, /device:TPU:8, one launch (start us, length us, event | category | flops | bytes accessed | tf_op | source)
XLA Modules:
  0.0 114.9 jit_solution(8956609940078418064)
XLA Ops:
  0.6 2.2 %shard_map.186 = f32[384,128]{1,0:T(8,128)} custom-call(f32[1,32,2048]{2,1,0:T(8,128)} %state_ref.1, f32[32,128]{1,0:T(8,128)} %constant.26.clone.twiddle_hbm.twiddle_ref, bf16[2,192,256]{2,1,0:T(8,128)(2,1)} %constant.27.clone.table_hbm.table_ref), custom_call_target="tpu_custom_call" | custom-call | tf_op jit(solution)/shard_map/pallas_call | solution.py:616
  2.8 0.0 copy-start.13
  2.9 0.0 copy-start.15
  2.9 0.0 copy-start.16
  2.9 0.0 copy-start.17
  2.9 12.5 %all-to-all-start = ((f32[64,1,768]{2,1,0:T(1,128)}), f32[64,1,768]{2,1,0:T(1,128)S(1)}, u32[]{:S(2)}, u32[]{:S(2)}) async-start(f32[64,1,768]{2,1,0:T(1,128)} %bitcast.16), calls=%async_computation | async-start | bytes 393216 | tf_op jit(solution)/shard_map/all_to_all | solution.py:630
  15.4 0.0 copy-done.13
  15.4 0.0 copy-done.15
  15.5 0.0 copy-start.3
  15.5 0.0 copy-start.6
  15.5 0.0 copy-start.12
  15.5 0.0 copy-start.14
  15.5 1.3 %shard_map.185.weights_ref = f32[8,8,3696]{2,1,0:T(8,128)S(1)} custom-call(f32[8,8]{1,0:T(8,128)S(1)} %copy-done.15, f32[8,8]{1,0:T(8,128)S(1)} %copy-done.16, f32[8]{0:T(128)S(1)} %copy-done.17, f32[8,3696]{1,0:T(8,128)S(1)} %copy-done.13), custom_call_target="tpu_custom_call" | custom-call | flops 8000000 | bytes 2000000 | tf_op jit(solution)/shard_map/pallas_call | solution.py:616
  16.8 9.6 %all-to-all-done = f32[64,1,768]{2,1,0:T(1,128)S(1)} async-done(((f32[64,1,768]{2,1,0:T(1,128)}), f32[64,1,768]{2,1,0:T(1,128)S(1)}, u32[]{:S(2)}, u32[]{:S(2)}) %all-to-all-start) | async-done | bytes 196640 | tf_op jit(solution)/shard_map/all_to_all | solution.py:630
  26.5 0.5 shard_map.187
  27.0 0.0 copy-start.1
  27.0 0.0 copy-start.7
  27.0 21.8 %all-gather = f32[64,3696]{1,0:T(8,128)S(1)} all-gather(f32[8,3696]{1,0:T(8,128)S(1)} %get-tuple-element.4), channel_id=2, replica_groups=mesh['layer'=8,'row'=64] {'layer'}, dimensions={0}, use_global_device_ids=true | all-gather | bytes 1064448 | tf_op jit(solution)/shard_map/all_gather | solution.py:661
  48.8 1.1 shard_map.188
  49.9 0.0 copy-start.2
  49.9 0.0 copy-start.9
  49.9 0.0 copy-start.10
  49.9 26.8 %all_to_all.20 = f32[64,1,2688]{2,1,0:T(1,128)S(1)} all-to-all(f32[64,1,2688]{2,1,0:T(1,128)S(1)} %bitcast.11), channel_id=1, replica_groups=mesh['layer'=8,'row'=64] {'row'}, dimensions={0} | all-to-all | bytes 1376256 | tf_op jit(solution)/shard_map/all_to_all | solution.py:630
  76.7 2.0 %shard_map.189 = f32[384,128]{1,0:T(8,128)} custom-call(f32[1344,128]{1,0:T(8,128)S(1)} %bitcast.10, f32[32,128]{1,0:T(8,128)S(1)} %copy-done.10, bf16[2,176,256]{2,1,0:T(8,128)(2,1)S(1)} %copy-done.9, bf16[2,192,256]{2,1,0:T(8,128)(2,1)S(1)} %copy-done.2), custom_call_target="tpu_custom_call" | custom-call | tf_op jit(solution)/shard_map/pallas_call | solution.py:616
  78.8 7.3 %all-to-all-start.2 = ((f32[64,1,768]{2,1,0:T(1,128)}), f32[64,1,768]{2,1,0:T(1,128)S(1)}, u32[]{:S(2)}, u32[]{:S(2)}) async-start(f32[64,1,768]{2,1,0:T(1,128)} %bitcast.5), calls=%async_computation.2 | async-start | bytes 393216 | tf_op jit(solution)/shard_map/all_to_all | solution.py:630
  86.1 0.0 copy-start.11
  86.1 0.3 shard_map.190.damping_ref
  86.4 10.5 %all-to-all-done.2 = f32[64,1,768]{2,1,0:T(1,128)S(1)} async-done(((f32[64,1,768]{2,1,0:T(1,128)}), f32[64,1,768]{2,1,0:T(1,128)S(1)}, u32[]{:S(2)}, u32[]{:S(2)}) %all-to-all-start.2) | async-done | bytes 196640 | tf_op jit(solution)/shard_map/all_to_all | solution.py:630
  96.9 0.8 shard_map.191
  97.7 0.0 copy-start
  97.7 15.9 %all_to_all.21 = f32[64,1,768]{2,1,0:T(1,128)S(1)} all-to-all(f32[64,1,768]{2,1,0:T(1,128)S(1)} %bitcast.14), channel_id=1, replica_groups=mesh['layer'=8,'row'=64] {'row'}, dimensions={0} | all-to-all | bytes 393216 | tf_op jit(solution)/shard_map/all_to_all | solution.py:630
  113.6 1.3 %shard_map.192 = (f32[1,32,2048]{2,1,0:T(8,128)}, f32[1,32,2048]{2,1,0:T(8,128)}) custom-call(f32[384,128]{1,0:T(8,128)S(1)} %bitcast.15, f32[1,32,2048]{2,1,0:T(8,128)S(1)} %copy-done, f32[1,32,2048]{2,1,0:T(8,128)S(1)} %copy-done.5, f32[32,128]{1,0:T(8,128)S(1)} %copy-done.10, bf16[2,192,256]{2,1,0:T(8,128)(2,1)S(1)} %copy-done.8), custom_call_target="tpu_custom_call" | custom-call | tf_op jit(solution)/shard_map/pallas_call | solution.py:616
  (19 shorter events, 0.0 us)
Async XLA Ops:
  2.8 12.6 %copy-start.13 = (f32[8,3696]{1,0:T(8,128)S(1)}, f32[8,3696]{1,0:T(8,128)}, u32[]{:S(2)}) copy-start(f32[8,3696]{1,0:T(8,128)} %constant.38.clone.facts_ref) | copy-start | bytes 354820
  2.9 12.6 %copy-start.15 = (f32[8,8]{1,0:T(8,128)S(1)}, f32[8,8]{1,0:T(8,128)}, u32[]{:S(2)}) copy-start(f32[8,8]{1,0:T(8,128)} %to_ref.1) | copy-start | bytes 772
  2.9 12.6 %copy-start.16 = (f32[8,8]{1,0:T(8,128)S(1)}, f32[8,8]{1,0:T(8,128)}, u32[]{:S(2)}) copy-start(f32[8,8]{1,0:T(8,128)} %from_ref.1) | copy-start | bytes 772
  2.9 12.6 %copy-start.17 = (f32[8]{0:T(128)S(1)}, f32[8]{0:T(128)}, u32[]{:S(2)}) copy-start(f32[8]{0:T(128)} %deform_ref.1) | copy-start | bytes 100
  2.9 23.6 %all-to-all-start = ((f32[64,1,768]{2,1,0:T(1,128)}), f32[64,1,768]{2,1,0:T(1,128)S(1)}, u32[]{:S(2)}, u32[]{:S(2)}) async-start(f32[64,1,768]{2,1,0:T(1,128)} %bitcast.16), calls=%async_computation | async-start | bytes 393216 | tf_op jit(solution)/shard_map/all_to_all | solution.py:630
  15.5 11.0 %copy-start.3 = (f32[2,64,128]{2,1,0:T(8,128)S(1)}, f32[2,64,128]{2,1,0:T(8,128)}, u32[]{:S(2)}) copy-start(f32[2,64,128]{2,1,0:T(8,128)} %constant.32.clone.turn_ref) | copy-start | bytes 196612
  15.5 11.0 %copy-start.6 = (bf16[128,192]{1,0:T(8,128)(2,1)S(1)}, bf16[128,192]{1,0:T(8,128)(2,1)}, u32[]{:S(2)}) copy-start(bf16[128,192]{1,0:T(8,128)(2,1)} %constant.30.clone.radix_ref) | copy-start | bytes 147460
  15.5 11.0 %copy-start.12 = (bf16[256,256]{1,0:T(8,128)(2,1)S(1)}, bf16[256,256]{1,0:T(8,128)(2,1)}, u32[]{:S(2)}) copy-start(bf16[256,256]{1,0:T(8,128)(2,1)} %constant.33.clone.lanes_ref) | copy-start | bytes 393220
  15.5 11.0 %copy-start.14 = (f32[8,128]{1,0:T(8,128)S(1)}, f32[8,128]{1,0:T(8,128)}, u32[]{:S(2)}) copy-start(f32[8,128]{1,0:T(8,128)} %constant.37.clone.facts_ref) | copy-start | bytes 12292
  27.0 21.8 %copy-start.1 = (bf16[384,256]{1,0:T(8,128)(2,1)S(1)}, bf16[384,256]{1,0:T(8,128)(2,1)}, u32[]{:S(2)}) copy-start(bf16[384,256]{1,0:T(8,128)(2,1)} %constant.34.clone.unlanes_ref) | copy-start | bytes 589828
  27.0 21.8 %copy-start.7 = (bf16[128,256]{1,0:T(8,128)(2,1)S(1)}, bf16[128,256]{1,0:T(8,128)(2,1)}, u32[]{:S(2)}) copy-start(bf16[128,256]{1,0:T(8,128)(2,1)} %constant.31.clone.unradix_ref) | copy-start | bytes 196612
  49.9 26.8 %copy-start.2 = (bf16[2,192,256]{2,1,0:T(8,128)(2,1)S(1)}, bf16[2,192,256]{2,1,0:T(8,128)(2,1)}, u32[]{:S(2)}) copy-start(bf16[2,192,256]{2,1,0:T(8,128)(2,1)} %constant.27.clone.table_hbm.table_ref) | copy-start | bytes 589828
  49.9 26.8 %copy-start.9 = (bf16[2,176,256]{2,1,0:T(8,128)(2,1)S(1)}, bf16[2,176,256]{2,1,0:T(8,128)(2,1)}, u32[]{:S(2)}) copy-start(bf16[2,176,256]{2,1,0:T(8,128)(2,1)} %constant.28.clone.untable_ref) | copy-start | bytes 540676
  49.9 26.8 %copy-start.10 = (f32[32,128]{1,0:T(8,128)S(1)}, f32[32,128]{1,0:T(8,128)}, u32[]{:S(2)}) copy-start(f32[32,128]{1,0:T(8,128)} %constant.26.clone.twiddle_hbm.twiddle_ref) | copy-start | bytes 49156
  78.8 18.2 %copy-start.4 = (bf16[2,2,256,256]{3,2,1,0:T(8,128)(2,1)S(1)}, bf16[2,2,256,256]{3,2,1,0:T(8,128)(2,1)}, u32[]{:S(2)}) copy-start(bf16[2,2,256,256]{3,2,1,0:T(8,128)(2,1)} %constant.35.clone.project_ref) | copy-start | bytes 1572868
  78.8 18.2 %all-to-all-start.2 = ((f32[64,1,768]{2,1,0:T(1,128)}), f32[64,1,768]{2,1,0:T(1,128)S(1)}, u32[]{:S(2)}, u32[]{:S(2)}) async-start(f32[64,1,768]{2,1,0:T(1,128)} %bitcast.5), calls=%async_computation.2 | async-start | bytes 393216 | tf_op jit(solution)/shard_map/all_to_all | solution.py:630
  86.1 10.9 %copy-start.11 = (bf16[256,256]{1,0:T(8,128)(2,1)S(1)}, bf16[256,256]{1,0:T(8,128)(2,1)}, u32[]{:S(2)}) copy-start(bf16[256,256]{1,0:T(8,128)(2,1)} %constant.36.clone.mean_ref) | copy-start | bytes 393220
  96.9 16.7 %copy-start.5 = (f32[1,32,2048]{2,1,0:T(8,128)S(1)}, f32[1,32,2048]{2,1,0:T(8,128)}, u32[]{:S(2)}) copy-start(f32[1,32,2048]{2,1,0:T(8,128)} %start_ref.1) | copy-start | bytes 786436
  96.9 16.7 %copy-start.8 = (bf16[2,192,256]{2,1,0:T(8,128)(2,1)S(1)}, bf16[2,192,256]{2,1,0:T(8,128)(2,1)}, u32[]{:S(2)}) copy-start(bf16[2,192,256]{2,1,0:T(8,128)(2,1)} %constant.29.clone.untable_ref) | copy-start | bytes 589828
  97.7 15.9 %copy-start = (f32[1,32,2048]{2,1,0:T(8,128)S(1)}, f32[1,32,2048]{2,1,0:T(8,128)}, u32[]{:S(2)}) copy-start(f32[1,32,2048]{2,1,0:T(8,128)} %state_ref.1) | copy-start | bytes 786436

commit v12 on v10

--- a/solution.py
+++ b/solution.py
@@ -406,8 +406,8 @@
     pltpu.make_async_copy(out_ref, out_hbm, sems.at[3]).wait()
 
 
-def weights_kernel(to_ref, from_ref, deform_ref, facts_ref, out_ref):
-    facts = facts_ref[...]
+def weights_kernel(to_ref, from_ref, deform_ref, packed_ref, facts_ref, out_ref, damping_ref):
+    facts = packed_ref[...]
     wave_x = x_waves(facts, lax.axis_index("row"))
     wave_y = y_waves(facts, 8)
     square = wave_x * wave_x + wave_y * wave_y
@@ -419,6 +419,14 @@
             term = modes[m] * to_ref[m, n]
             total = term if total is None else total + term
         out_ref[n] = total
+    facts = facts_ref[...]
+    wave_y = y_waves(facts)
+    once = half_of_zero(wave_y)
+    for jr in range(6):
+        wave_x = x_waves(facts, lax.axis_index("row")) + 64 * jr
+        ratio = (wave_x * wave_x + wave_y * wave_y) * (1.0 / (KCUT * KCUT))
+        ratio = ratio * ratio
+        damping_ref[KAP * jr : KAP * jr + KAP, :] = (HYPER_RATE * (ratio * ratio)) * once
 
 
 def spectrum_kernel(in_ref, radix_ref, turn_ref, lanes_ref, facts_ref, spec_ref, used_ref):
@@ -514,18 +522,9 @@
 
 
 def projection_kernel(
-    in_ref, spec_ref, radix_ref, unradix_ref, turn_ref, project_ref, mean_ref, unlanes_ref, facts_ref, out_ref
+    in_ref, spec_ref, radix_ref, unradix_ref, turn_ref, project_ref, mean_ref, unlanes_ref, damping_ref, out_ref
 ):
-    facts = facts_ref[...]
-    wave_y = y_waves(facts)
-    once = half_of_zero(wave_y)
-    damped = []
-    for jr in range(6):
-        wave_x = x_waves(facts, lax.axis_index("row")) + 64 * jr
-        ratio = (wave_x * wave_x + wave_y * wave_y) * (1.0 / (KCUT * KCUT))
-        ratio = ratio * ratio
-        damped.append(((HYPER_RATE * (ratio * ratio)) * once) * spec_ref[KAP * jr : KAP * jr + KAP, :])
-    damping = matmul_wide(split(jnp.concatenate(damped, axis=0)), unlanes_ref)
+    damping = matmul_wide(split(damping_ref[...] * spec_ref[...]), unlanes_ref)
     left = [split(pair) for pair in y_turned(in_ref, radix_ref, turn_ref)]
     sides = []
     for side in range(2):
@@ -648,10 +647,10 @@
     spectrum, used = call(
         spectrum_kernel, [(6 * KAP, 128), (8, USED)], [columns, radix, turn_y, lanes, facts]
     )
-    (weights,) = call(
+    weights, damping = call(
         weights_kernel,
-        [(8, 8, USED)],
-        [to_modes, from_modes, deform, jnp.asarray(packed_facts())],
+        [(8, 8, USED), (6 * KAP, 128)],
+        [to_modes, from_modes, deform, jnp.asarray(packed_facts()), facts],
         scalars=3,
         cost=pl.CostEstimate(flops=8_000_000, bytes_accessed=2_000_000, transcendentals=0),
     )
@@ -673,7 +672,7 @@
     (total,) = call(
         projection_kernel,
         [one],
-        [flux, spectrum, radix, unradix, turn_y, project, mean, unlanes, facts],
+        [flux, spectrum, radix, unradix, turn_y, project, mean, unlanes, damping],
     )
     total = exchange(total, devices)
     return tuple(

time: 114 us -> 114 us (level)
  no operation moved by 1% of the time
where the time goes in v12:
time: 114 us
  blocking collectives  82.4 us (72%)
  starting transfers between devices  12.5 us (11%)
  waiting for transfers between devices  9.58 us (8%)
  Pallas kernels  8.64 us (8%)
    all_to_all x3, blocking collectives, exchange(): lax.all_to_all(sent, 'row', split_axis=0, concat_axis=0, tiled=True)  60.6 us
    all_gather x1, blocking collectives, per_device(): gathered = lax.all_gather(used, 'layer', axis=0, tiled=False)  21.8 us
    all_to_all x1, starting transfers between devices, exchange(): lax.all_to_all(sent, 'row', split_axis=0, concat_axis=0, tiled=True)  12.5 us
    all_to_all x1, waiting for transfers between devices, exchange(): lax.all_to_all(sent, 'row', split_axis=0, concat_axis=0, tiled=True)  9.58 us
    pallas_call x7, Pallas kernels, call(): pl.pallas_call(kernel, out_shape=[jax.ShapeDtypeStruct(shape, F32) for sh...  8.64 us
  transfers between devices with their start and end apart: 1, of which 1 were waited for; matrix products, arithmetic and copies ran while one was open for 0% of the time, Pallas kernels for 1%

profile of v12, /device:TPU:8, one launch (start us, length us, event | category | flops | bytes accessed | tf_op | source)
XLA Modules:
  0.0 114.1 jit_solution(13737989039082652108)
XLA Ops:
  0.6 2.2 %shard_map.186 = f32[384,128]{1,0:T(8,128)} custom-call(f32[1,32,2048]{2,1,0:T(8,128)} %state_ref.1, f32[32,128]{1,0:T(8,128)} %constant.26.clone.twiddle_hbm.twiddle_ref, bf16[2,192,256]{2,1,0:T(8,128)(2,1)} %constant.27.clone.table_hbm.table_ref), custom_call_target="tpu_custom_call" | custom-call | tf_op jit(solution)/shard_map/pallas_call | solution.py:612
  2.8 0.0 copy-start.13
  2.9 0.0 copy-start.14
  2.9 0.0 copy-start.15
  2.9 0.0 copy-start.16
  2.9 0.0 copy-start.17
  2.9 0.0 copy-start.12
  2.9 12.5 %all-to-all-start = ((f32[64,1,768]{2,1,0:T(1,128)}), f32[64,1,768]{2,1,0:T(1,128)S(1)}, u32[]{:S(2)}, u32[]{:S(2)}) async-start(f32[64,1,768]{2,1,0:T(1,128)} %bitcast.17), calls=%async_computation | async-start | bytes 393216 | tf_op jit(solution)/shard_map/all_to_all | solution.py:626
  15.5 0.0 copy-start.3
  15.5 0.0 copy-start.6
  15.5 1.4 %shard_map.185 = (f32[8,8,3696]{2,1,0:T(8,128)S(1)}, f32[384,128]{1,0:T(8,128)S(1)}) custom-call(f32[8,8]{1,0:T(8,128)S(1)} %copy-done.15, f32[8,8]{1,0:T(8,128)S(1)} %copy-done.16, f32[8]{0:T(128)S(1)} %copy-done.17, f32[8,3696]{1,0:T(8,128)S(1)} %copy-done.13, f32[8,128]{1,0:T(8,128)S(1)} %copy-done.14), custom_call_target="tpu_custom_call" | custom-call | flops 8000000 | bytes 2000000 | tf_op jit(solution)/shard_map/pallas_call | solution.py:612
  16.9 9.6 %all-to-all-done = f32[64,1,768]{2,1,0:T(1,128)S(1)} async-done(((f32[64,1,768]{2,1,0:T(1,128)}), f32[64,1,768]{2,1,0:T(1,128)S(1)}, u32[]{:S(2)}, u32[]{:S(2)}) %all-to-all-start) | async-done | bytes 196640 | tf_op jit(solution)/shard_map/all_to_all | solution.py:626
  26.5 0.0 copy-done.6
  26.5 0.5 shard_map.187
  27.0 0.0 copy-start.1
  27.0 0.0 copy-start.7
  27.0 21.8 %all-gather = f32[64,3696]{1,0:T(8,128)S(1)} all-gather(f32[8,3696]{1,0:T(8,128)S(1)} %get-tuple-element.7), channel_id=2, replica_groups=mesh['layer'=8,'row'=64] {'layer'}, dimensions={0}, use_global_device_ids=true | all-gather | bytes 1064448 | tf_op jit(solution)/shard_map/all_gather | solution.py:657
  48.8 0.0 copy-done.7
  48.8 1.1 shard_map.188
  49.9 0.0 copy-start.2
  49.9 0.0 copy-start.9
  49.9 0.0 copy-start.10
  49.9 26.8 %all_to_all.20 = f32[64,1,2688]{2,1,0:T(1,128)S(1)} all-to-all(f32[64,1,2688]{2,1,0:T(1,128)S(1)} %bitcast.10), channel_id=1, replica_groups=mesh['layer'=8,'row'=64] {'row'}, dimensions={0} | all-to-all | bytes 1376256 | tf_op jit(solution)/shard_map/all_to_all | solution.py:626
  76.7 0.0 copy-done.2
  76.7 0.0 copy-start.4
  76.7 1.4 %shard_map.189 = f32[384,128]{1,0:T(8,128)S(1)} custom-call(f32[1344,128]{1,0:T(8,128)S(1)} %bitcast.11, f32[32,128]{1,0:T(8,128)S(1)} %copy-done.10, bf16[2,176,256]{2,1,0:T(8,128)(2,1)S(1)} %copy-done.9, bf16[2,192,256]{2,1,0:T(8,128)(2,1)S(1)} %copy-done.2), custom_call_target="tpu_custom_call" | custom-call | tf_op jit(solution)/shard_map/pallas_call | solution.py:612
  78.1 0.0 copy-start.11
  78.1 18.0 %all_to_all.21 = f32[64,1,768]{2,1,0:T(1,128)S(1)} all-to-all(f32[64,1,768]{2,1,0:T(1,128)S(1)} %bitcast.16), channel_id=1, replica_groups=mesh['layer'=8,'row'=64] {'row'}, dimensions={0} | all-to-all | bytes 393216 | tf_op jit(solution)/shard_map/all_to_all | solution.py:626
  96.1 0.8 shard_map.190
  96.9 0.0 copy-start
  96.9 15.9 %all_to_all.22 = f32[64,1,768]{2,1,0:T(1,128)S(1)} all-to-all(f32[64,1,768]{2,1,0:T(1,128)S(1)} %bitcast.14), channel_id=1, replica_groups=mesh['layer'=8,'row'=64] {'row'}, dimensions={0} | all-to-all | bytes 393216 | tf_op jit(solution)/shard_map/all_to_all | solution.py:626
  112.8 1.3 %shard_map.191 = (f32[1,32,2048]{2,1,0:T(8,128)}, f32[1,32,2048]{2,1,0:T(8,128)}) custom-call(f32[384,128]{1,0:T(8,128)S(1)} %bitcast.15, f32[1,32,2048]{2,1,0:T(8,128)S(1)} %copy-done, f32[1,32,2048]{2,1,0:T(8,128)S(1)} %copy-done.5, f32[32,128]{1,0:T(8,128)S(1)} %copy-done.10, bf16[2,192,256]{2,1,0:T(8,128)(2,1)S(1)} %copy-done.8), custom_call_target="tpu_custom_call" | custom-call | tf_op jit(solution)/shard_map/pallas_call | solution.py:612
  (17 shorter events, 0.0 us)
Async XLA Ops:
  2.8 12.6 %copy-start.13 = (f32[8,3696]{1,0:T(8,128)S(1)}, f32[8,3696]{1,0:T(8,128)}, u32[]{:S(2)}) copy-start(f32[8,3696]{1,0:T(8,128)} %constant.38.clone.packed_ref) | copy-start | bytes 354820
  2.9 12.6 %copy-start.14 = (f32[8,128]{1,0:T(8,128)S(1)}, f32[8,128]{1,0:T(8,128)}, u32[]{:S(2)}) copy-start(f32[8,128]{1,0:T(8,128)} %constant.37.clone.facts_ref) | copy-start | bytes 12292
  2.9 12.6 %copy-start.15 = (f32[8,8]{1,0:T(8,128)S(1)}, f32[8,8]{1,0:T(8,128)}, u32[]{:S(2)}) copy-start(f32[8,8]{1,0:T(8,128)} %to_ref.1) | copy-start | bytes 772
  2.9 12.6 %copy-start.16 = (f32[8,8]{1,0:T(8,128)S(1)}, f32[8,8]{1,0:T(8,128)}, u32[]{:S(2)}) copy-start(f32[8,8]{1,0:T(8,128)} %from_ref.1) | copy-start | bytes 772
  2.9 12.6 %copy-start.17 = (f32[8]{0:T(128)S(1)}, f32[8]{0:T(128)}, u32[]{:S(2)}) copy-start(f32[8]{0:T(128)} %deform_ref.1) | copy-start | bytes 100
  2.9 23.6 %copy-start.12 = (bf16[256,256]{1,0:T(8,128)(2,1)S(1)}, bf16[256,256]{1,0:T(8,128)(2,1)}, u32[]{:S(2)}) copy-start(bf16[256,256]{1,0:T(8,128)(2,1)} %constant.33.clone.lanes_ref) | copy-start | bytes 393220
  2.9 23.6 %all-to-all-start = ((f32[64,1,768]{2,1,0:T(1,128)}), f32[64,1,768]{2,1,0:T(1,128)S(1)}, u32[]{:S(2)}, u32[]{:S(2)}) async-start(f32[64,1,768]{2,1,0:T(1,128)} %bitcast.17), calls=%async_computation | async-start | bytes 393216 | tf_op jit(solution)/shard_map/all_to_all | solution.py:626
  15.5 11.0 %copy-start.3 = (f32[2,64,128]{2,1,0:T(8,128)S(1)}, f32[2,64,128]{2,1,0:T(8,128)}, u32[]{:S(2)}) copy-start(f32[2,64,128]{2,1,0:T(8,128)} %constant.32.clone.turn_ref) | copy-start | bytes 196612
  15.5 11.0 %copy-start.6 = (bf16[128,192]{1,0:T(8,128)(2,1)S(1)}, bf16[128,192]{1,0:T(8,128)(2,1)}, u32[]{:S(2)}) copy-start(bf16[128,192]{1,0:T(8,128)(2,1)} %constant.30.clone.radix_ref) | copy-start | bytes 147460
  27.0 21.8 %copy-start.1 = (bf16[384,256]{1,0:T(8,128)(2,1)S(1)}, bf16[384,256]{1,0:T(8,128)(2,1)}, u32[]{:S(2)}) copy-start(bf16[384,256]{1,0:T(8,128)(2,1)} %constant.34.clone.unlanes_ref) | copy-start | bytes 589828
  27.0 21.8 %copy-start.7 = (bf16[128,256]{1,0:T(8,128)(2,1)S(1)}, bf16[128,256]{1,0:T(8,128)(2,1)}, u32[]{:S(2)}) copy-start(bf16[128,256]{1,0:T(8,128)(2,1)} %constant.31.clone.unradix_ref) | copy-start | bytes 196612
  49.9 26.8 %copy-start.2 = (bf16[2,192,256]{2,1,0:T(8,128)(2,1)S(1)}, bf16[2,192,256]{2,1,0:T(8,128)(2,1)}, u32[]{:S(2)}) copy-start(bf16[2,192,256]{2,1,0:T(8,128)(2,1)} %constant.27.clone.table_hbm.table_ref) | copy-start | bytes 589828
  49.9 26.8 %copy-start.9 = (bf16[2,176,256]{2,1,0:T(8,128)(2,1)S(1)}, bf16[2,176,256]{2,1,0:T(8,128)(2,1)}, u32[]{:S(2)}) copy-start(bf16[2,176,256]{2,1,0:T(8,128)(2,1)} %constant.28.clone.untable_ref) | copy-start | bytes 540676
  49.9 26.8 %copy-start.10 = (f32[32,128]{1,0:T(8,128)S(1)}, f32[32,128]{1,0:T(8,128)}, u32[]{:S(2)}) copy-start(f32[32,128]{1,0:T(8,128)} %constant.26.clone.twiddle_hbm.twiddle_ref) | copy-start | bytes 49156
  76.7 19.3 %copy-start.4 = (bf16[2,2,256,256]{3,2,1,0:T(8,128)(2,1)S(1)}, bf16[2,2,256,256]{3,2,1,0:T(8,128)(2,1)}, u32[]{:S(2)}) copy-start(bf16[2,2,256,256]{3,2,1,0:T(8,128)(2,1)} %constant.35.clone.project_ref) | copy-start | bytes 1572868
  78.1 18.0 %copy-start.11 = (bf16[256,256]{1,0:T(8,128)(2,1)S(1)}, bf16[256,256]{1,0:T(8,128)(2,1)}, u32[]{:S(2)}) copy-start(bf16[256,256]{1,0:T(8,128)(2,1)} %constant.36.clone.mean_ref) | copy-start | bytes 393220
  96.1 16.7 %copy-start.5 = (f32[1,32,2048]{2,1,0:T(8,128)S(1)}, f32[1,32,2048]{2,1,0:T(8,128)}, u32[]{:S(2)}) copy-start(f32[1,32,2048]{2,1,0:T(8,128)} %start_ref.1) | copy-start | bytes 786436
  96.1 16.7 %copy-start.8 = (bf16[2,192,256]{2,1,0:T(8,128)(2,1)S(1)}, bf16[2,192,256]{2,1,0:T(8,128)(2,1)}, u32[]{:S(2)}) copy-start(bf16[2,192,256]{2,1,0:T(8,128)(2,1)} %constant.29.clone.untable_ref) | copy-start | bytes 589828
  96.9 15.9 %copy-start = (f32[1,32,2048]{2,1,0:T(8,128)S(1)}, f32[1,32,2048]{2,1,0:T(8,128)}, u32[]{:S(2)}) copy-start(f32[1,32,2048]{2,1,0:T(8,128)} %state_ref.1) | copy-start | bytes 786436
